TPU v7x, 32 devices: a whole 2x2x4 slice. The times are simulated.
32 devices in a mesh: chain: 2 (over y), tm: 4 (over z), src: 2 (over x), col: 2 (over core).
Axes of the slice: x: 2, y: 2, z: 4, core: 2. Of those that a mesh axis runs over, the one named last changes fastest.
Arguments:
- cluster_maps: bfloat16 [4, 2048, 1024], P('tm', 'chain'), parts along dimension 1, may hold values from -2 to 2
- inverse_maps: bfloat16 [4, 2048, 1024], P('tm', 'chain'), parts along dimension 1, may hold values from -2 to 2
- seed_columns: float32 [4, 64, 2048], P('tm', ('src', 'col'), 'chain'), parts along dimension 2, may hold values from -1 to 1, as said below
- seed_rows: float32 [4, 64, 2048], P('tm', ('src', 'col'), 'chain'), parts along dimension 2, may hold values from -1 to 1
- ising_field: int32 [4, 4, 1024], P('tm', 'chain'), parts along dimension 1, may hold values 0 or 1
- hop_bonds: int32 [2, 1024], replicated, may hold values 0 or 1
Outputs:
- correlator: float32 [4, 64, 2048], P('tm', ('src', 'col'), 'chain'), parts along dimension 2
There are 2 independent parts, one for each index of `chain`. A program takes and returns all parts, laid end to end along the dimension named above; an argument that names none is the same for every part. Nothing has to cross between parts.
Inputs may be any that keep to these rules, and one draw needn't show every extreme that they name: Rows of seed_columns and seed_rows come from one equal-time Green block per cluster.
All inputs are finite; a program needn't handle non-finite values. No bound on the sum of `ising_field` on one device may be relied on, other than what follows from the above.
Results may differ from a plain program's by a relative error of at most 0.012.
The roundings to bfloat16 on the way count: a program that leaves them out, or rounds other values in their place, can miss the bound.
Values may be sent and summed in bfloat16 or wider, within the bound.
No kernel may reach another device: no remote copies, remote signals or barrier semaphores. Data moves between devices by JAX's collectives and lax.ppermute only.
A program may use at most 64 MiB of HBM per device.

v0:
```python
import math

import jax
import jax.numpy as jnp
from jax import lax
from jax.sharding import PartitionSpec as P

SIDE = 32
SITES = 1024


time_step = 0.25
field_coupling = math.log(math.exp(0.5) + math.sqrt(math.exp(1.0) - 1.0))


def passed_along(block, axis, distance):
    devices = range(lax.axis_size(axis))
    route = [((i - distance) % len(devices), i) for i in devices]
    return lax.ppermute(block, axis, route)


def shifted(values, last_column, first_column):
    ahead_rows = jnp.roll(values, -SIDE, axis=-1)
    behind_rows = jnp.roll(values, SIDE, axis=-1)
    ahead_columns = jnp.where(
        last_column, jnp.roll(values, SIDE - 1, axis=-1), jnp.roll(values, -1, axis=-1)
    )
    behind_columns = jnp.where(
        first_column, jnp.roll(values, 1 - SIDE, axis=-1), jnp.roll(values, 1, axis=-1)
    )
    return (ahead_rows, behind_rows, ahead_columns, behind_columns)


def couplings(hop_bonds):
    bonds_float = hop_bonds.astype(jnp.float32)
    positions = jnp.arange(hop_bonds.shape[-1]) % SIDE
    last_column = positions == SIDE - 1
    first_column = positions == 0
    row_bonds = bonds_float[0]
    column_bonds = bonds_float[1]
    row_back = jnp.roll(row_bonds, SIDE)
    column_back = jnp.where(
        first_column, jnp.roll(column_bonds, 1 - SIDE), jnp.roll(column_bonds, 1)
    )
    return (row_bonds, row_back, column_bonds, column_back, last_column, first_column)


def hopping(values, lattice):
    row_bonds, row_back, column_bonds, column_back, last_column, first_column = lattice
    ahead_rows, behind_rows, ahead_columns, behind_columns = shifted(
        values, last_column, first_column
    )
    return -(
        row_bonds * ahead_rows
        + row_back * behind_rows
        + column_bonds * ahead_columns
        + column_back * behind_columns
    )


def series(values, lattice, orientation):
    single_hop = hopping(values, lattice)
    double_hop = hopping(single_hop, lattice)
    return values + orientation * time_step * single_hop + 0.5 * time_step * time_step * double_hop


def wrapped_product(forward, partner, spin_values, lattice):
    for wrap_index in range(spin_values.shape[0]):
        scale_up = jnp.exp(field_coupling * spin_values[wrap_index])
        scale_down = jnp.exp(-field_coupling * spin_values[wrap_index])
        forward = series(forward * scale_up, lattice, -1.0)
        partner = series(partner * scale_down, lattice, 1.0)
    return forward * partner


def per_device(cluster_maps, inverse_maps, seed_columns, seed_rows, ising_field, hop_bonds):
    clusters = lax.axis_size("tm")
    ref_rows = seed_columns.shape[1]
    lattice = couplings(hop_bonds)
    spin_values = (2 * ising_field[0] - 1).astype(jnp.float32)
    site_ids = jnp.arange(seed_columns.shape[2])
    ref_ids = lax.axis_index(("src", "col")) * ref_rows + jnp.arange(ref_rows)
    same_site = site_ids[None, :] == ref_ids[:, None]
    unequal = jnp.where(same_site, 0.0, 1.0).astype(jnp.float32)
    forward_map = cluster_maps[0]
    inverse_map = inverse_maps[0]
    forward = seed_columns[0]
    partner = seed_rows[0] - same_site.astype(jnp.float32)

    def measure(forward_block, partner_block):
        return wrapped_product(forward_block, partner_block, spin_values, lattice) * unequal

    first_term = measure(forward, partner)
    stored = jnp.zeros((clusters,) + first_term.shape, jnp.float32).at[0].set(first_term)

    def advance(hop_index, state_tuple):
        forward_low, partner_low, stored_terms = state_tuple
        forward_low, partner_low = passed_along((forward_low, partner_low), "tm", 1)
        forward_next = lax.dot_general(
            forward_low, forward_map, (((1,), (1,)), ((), ())), preferred_element_type=jnp.float32
        )
        partner_next = jnp.dot(partner_low, inverse_map, preferred_element_type=jnp.float32)
        term_now = measure(forward_next, partner_next)
        stored_terms = lax.dynamic_update_slice_in_dim(stored_terms, term_now[None], hop_index, 0)
        return (forward_next.astype(jnp.bfloat16), partner_next.astype(jnp.bfloat16), stored_terms)

    state_tuple = lax.fori_loop(
        1, clusters, advance, (forward.astype(jnp.bfloat16), partner.astype(jnp.bfloat16), stored)
    )
    stored = state_tuple[2]
    summed = lax.psum_scatter(stored, "tm", scatter_dimension=0, tiled=True)
    return summed * (SITES / clusters)


def solution(mesh):
    in_specs = (
        P("tm", "chain", None),
        P("tm", "chain", None),
        P("tm", ("src", "col"), "chain"),
        P("tm", ("src", "col"), "chain"),
        P("tm", "chain", None),
        P(),
    )
    out_specs = P("tm", ("src", "col"), "chain")
    return jax.shard_map(
        per_device, mesh=mesh, in_specs=in_specs, out_specs=out_specs, check_vma=False
    )
```

profile of v0, /device:TPU:0, one launch (start us, length us, event | category | flops | bytes accessed | tf_op | source)
XLA Modules:
  0.0 113.5 jit_solution(2083475158672647743)
XLA Ops:
  6.5 0.7 convert_element_type.49
  8.0 0.7 fusion.190
  8.8 0.8 bitcast_multiply_fusion
  9.6 1.5 %fusion.183 = (f32[16,1024]{1,0:T(8,128)S(1)}, bf16[16,1024]{1,0:T(8,128)(2,1)}) fusion(f32[1,16,1024]{2,1,0:T(8,128)} %param.13, f32[1024]{0:T(1024)S(1)} %bitcast.296, s32[16]{0:T(128)S(1)} %iota_add_fusion), kind=kLoop, calls=%fused_computation.294 | loop fusion | flops 81920 | bytes 168000 | tf_op jit(solution)/shard_map/mul | solution.py:72
  11.5 0.7 fusion.254
  12.2 0.7 fusion.255
  12.9 0.7 pad_maximum_fusion
  14.7 0.7 fusion.248
  16.8 0.7 fusion.241
  17.5 0.7 fusion.244
  18.2 0.7 fusion.239
  19.6 0.7 fusion.243
  20.4 0.7 slice_bitcast_fusion
  21.1 0.7 slice_bitcast_fusion.1
  21.8 0.7 slice_bitcast_fusion.4
  22.5 0.7 slice_bitcast_fusion.12
  24.6 0.7 fusion.264
  25.3 0.7 fusion.265
  26.1 0.7 fusion.268
  28.9 0.7 fusion.258
  29.6 0.7 fusion.259
  30.4 0.7 fusion.262
  31.1 0.7 fusion.257
  31.7 0.7 fusion.260
  32.4 0.7 fusion.261
  33.2 0.7 slice_bitcast_fusion.6
  33.9 0.7 slice_bitcast_fusion.7
  34.6 0.7 slice_bitcast_fusion.10
  35.3 0.7 slice_bitcast_fusion.18
  36.0 0.7 slice_bitcast_fusion.19
  36.7 0.7 slice_bitcast_fusion.22
  38.0 2.5 %fusion.84 = f32[1,16,1024]{2,1,0:T(8,128)S(1)} fusion(f32[1,16,32]{2,1,0:T(8,128)} %get-tuple-element.798, f32[1,16,992]{2,1,0:T(8,128)S(1)} %get-tuple-element.802, f32[1,16,992]{2,1,0:T(8,128)S(1)} %get-tuple-element.801, f32[1,16,32]{2,1,0:T(8,128)} %get-tuple-element.797, f32[1,16,993]{2,1,0:T(8,128)S(1)} %get-tuple-element.790, ...), kind=kLoop, calls=%fused_computation.135 | loop fusion | flops 2523136 | bytes 3377216 | tf_op jit(solution)/shard_map/mul | solution.py:91
  40.5 45.5 %while.22 = (s32[]{:T(128)}, bf16[16,1024]{1,0:T(8,128)(2,1)}, bf16[16,1024]{1,0:T(8,128)(2,1)}, f32[4,16,1024]{2,1,0:T(8,128)S(1)}, bf16[1024,1024]{1,0:T(8,128...) while((s32[]{:T(128)}, bf16[16,1024]{1,0:T(8,128)(2,1)}, ...), condition=%wide.region_1.2_spmd.clone.clone, body=%wide.region_0.1_spmd.clone.clone.sunk | while | flops 69644288 | bytes 15410215 | solution.py:107
  40.5 3.1 %collective-permute-start.1 = (bf16[16,1024]{1,0:T(8,128)(2,1)}, bf16[16,1024]{1,0:T(8,128)(2,1)S(1)}, u32[]{:S(2)}, u32[]{:S(2)}) collective-permute-start(bf16[16,1024]{1,0:T(8,128)(2,1)} %get-tuple-element.1106), channel_id=1, source_target_pairs={{12,0},{0,4},{4,8},{8,12},{13,1},{1,5},{5,9},{9,13},{14,2},{2,6},{... | collective-permute-start | bytes 98312 | tf_op jit(solution)/shard_map/while/body/eval_jaxpr/ppermute | solution.py:19
  43.6 1.6 %collective-permute-start = (bf16[16,1024]{1,0:T(8,128)(2,1)}, bf16[16,1024]{1,0:T(8,128)(2,1)S(1)}, u32[]{:S(2)}, u32[]{:S(2)}) collective-permute-start(bf16[16,1024]{1,0:T(8,128)(2,1)} %get-tuple-element.1105), channel_id=1, source_target_pairs={{12,0},{0,4},{4,8},{8,12},{13,1},{1,5},{5,9},{9,13},{14,2},{2,6},{... | collective-permute-start | bytes 98312 | tf_op jit(solution)/shard_map/while/body/eval_jaxpr/ppermute | solution.py:19
  45.2 2.5 %collective-permute-done.1 = bf16[16,1024]{1,0:T(8,128)(2,1)S(1)} collective-permute-done((bf16[16,1024]{1,0:T(8,128)(2,1)}, bf16[16,1024]{1,0:T(8,128)(2,1)S(1)}, u32[]{:S(2)}, u32[]{:S(2)}) %collective-permute-start.1) | collective-permute-done | bytes 32800 | tf_op jit(solution)/shard_map/while/body/eval_jaxpr/ppermute | solution.py:19
  47.7 2.6 %broadcast_multiply_fusion.6 = (f32[16,1024]{1,0:T(8,128)S(1)}, bf16[16,1024]{1,0:T(8,128)(2,1)}) fusion(f32[1024]{0:T(1024)S(1)} %bitcast.290, bf16[16,1024]{1,0:T(8,128)(2,1)S(1)} %collective-permute-done.1, bf16[1024,1024]{1,0:T(8,128)(2,1)} %get-tuple-element.1124), kind=kOutput, calls=%fused_computation.98.clone.1 | convolution fusion | flops 33587200 | bytes 2232320 | tf_op jit(solution)/shard_map/while/body/eval_jaxpr/dot_general | solution.py:102
  52.6 1.3 %broadcast_multiply_fusion.5 = (f32[16,1024]{1,0:T(8,128)S(1)}, bf16[16,1024]{1,0:T(8,128)(2,1)}) fusion(f32[1024]{0:T(1024)S(1)} %bitcast.288, bf16[16,1024]{1,0:T(8,128)(2,1)S(1)} %collective-permute-done, bf16[1024,1024]{1,0:T(8,128)(2,1)S(1)} %get-tuple-element.1123), kind=kOutput, calls=%fused_computation.99.clone.1 | convolution fusion | flops 33587200 | bytes 2232320 | tf_op jit(solution)/shard_map/while/body/eval_jaxpr/dot_general | solution.py:99
  56.7 1.6 %collective-permute-start = (bf16[16,1024]{1,0:T(8,128)(2,1)}, bf16[16,1024]{1,0:T(8,128)(2,1)S(1)}, u32[]{:S(2)}, u32[]{:S(2)}) collective-permute-start(bf16[16,1024]{1,0:T(8,128)(2,1)} %get-tuple-element.1105), channel_id=1, source_target_pairs={{12,0},{0,4},{4,8},{8,12},{13,1},{1,5},{5,9},{9,13},{14,2},{2,6},{... | collective-permute-start | bytes 98312 | tf_op jit(solution)/shard_map/while/body/eval_jaxpr/ppermute | solution.py:19
  58.3 4.1 %collective-permute-done.1 = bf16[16,1024]{1,0:T(8,128)(2,1)S(1)} collective-permute-done((bf16[16,1024]{1,0:T(8,128)(2,1)}, bf16[16,1024]{1,0:T(8,128)(2,1)S(1)}, u32[]{:S(2)}, u32[]{:S(2)}) %collective-permute-start.1) | collective-permute-done | bytes 32800 | tf_op jit(solution)/shard_map/while/body/eval_jaxpr/ppermute | solution.py:19
  62.5 2.6 %broadcast_multiply_fusion.6 = (f32[16,1024]{1,0:T(8,128)S(1)}, bf16[16,1024]{1,0:T(8,128)(2,1)}) fusion(f32[1024]{0:T(1024)S(1)} %bitcast.290, bf16[16,1024]{1,0:T(8,128)(2,1)S(1)} %collective-permute-done.1, bf16[1024,1024]{1,0:T(8,128)(2,1)} %get-tuple-element.1124), kind=kOutput, calls=%fused_computation.98.clone.1 | convolution fusion | flops 33587200 | bytes 2232320 | tf_op jit(solution)/shard_map/while/body/eval_jaxpr/dot_general | solution.py:102
  67.4 1.3 %broadcast_multiply_fusion.5 = (f32[16,1024]{1,0:T(8,128)S(1)}, bf16[16,1024]{1,0:T(8,128)(2,1)}) fusion(f32[1024]{0:T(1024)S(1)} %bitcast.288, bf16[16,1024]{1,0:T(8,128)(2,1)S(1)} %collective-permute-done, bf16[1024,1024]{1,0:T(8,128)(2,1)S(1)} %get-tuple-element.1123), kind=kOutput, calls=%fused_computation.99.clone.1 | convolution fusion | flops 33587200 | bytes 2232320 | tf_op jit(solution)/shard_map/while/body/eval_jaxpr/dot_general | solution.py:99
  71.4 5.8 %collective-permute-done.1 = bf16[16,1024]{1,0:T(8,128)(2,1)S(1)} collective-permute-done((bf16[16,1024]{1,0:T(8,128)(2,1)}, bf16[16,1024]{1,0:T(8,128)(2,1)S(1)}, u32[]{:S(2)}, u32[]{:S(2)}) %collective-permute-start.1) | collective-permute-done | bytes 32800 | tf_op jit(solution)/shard_map/while/body/eval_jaxpr/ppermute | solution.py:19
  77.2 2.6 %broadcast_multiply_fusion.6 = (f32[16,1024]{1,0:T(8,128)S(1)}, bf16[16,1024]{1,0:T(8,128)(2,1)}) fusion(f32[1024]{0:T(1024)S(1)} %bitcast.290, bf16[16,1024]{1,0:T(8,128)(2,1)S(1)} %collective-permute-done.1, bf16[1024,1024]{1,0:T(8,128)(2,1)} %get-tuple-element.1124), kind=kOutput, calls=%fused_computation.98.clone.1 | convolution fusion | flops 33587200 | bytes 2232320 | tf_op jit(solution)/shard_map/while/body/eval_jaxpr/dot_general | solution.py:102
  82.2 1.3 %broadcast_multiply_fusion.5 = (f32[16,1024]{1,0:T(8,128)S(1)}, bf16[16,1024]{1,0:T(8,128)(2,1)}) fusion(f32[1024]{0:T(1024)S(1)} %bitcast.288, bf16[16,1024]{1,0:T(8,128)(2,1)S(1)} %collective-permute-done, bf16[1024,1024]{1,0:T(8,128)(2,1)S(1)} %get-tuple-element.1123), kind=kOutput, calls=%fused_computation.99.clone.1 | convolution fusion | flops 33587200 | bytes 2232320 | tf_op jit(solution)/shard_map/while/body/eval_jaxpr/dot_general | solution.py:99
  86.0 0.7 copy-done.2
  86.7 18.4 %reduce-scatter.2.cloned.1.call-done = f32[1,16,1024]{2,1,0:T(8,128)} async-done(((f32[4,16,1024]{2,1,0:T(8,128)}), f32[1,16,1024]{2,1,0:T(8,128)}) %reduce-scatter.2.cloned.1.call-update) | async-done | bytes 65552 | tf_op jit(solution)/shard_map/reduce_scatter | solution.py:111
  105.2 1.5 %broadcast_multiply_fusion.2 = f32[1,16,1024]{2,1,0:T(8,128)} fusion(f32[1,16,1024]{2,1,0:T(8,128)} %reduce-scatter.2.cloned.1.call-done), kind=kLoop, calls=%fused_computation.296 | loop fusion | flops 16384 | bytes 131072 | tf_op jit(solution)/shard_map/mul | solution.py:112
  (228 shorter events, 23.8 us)
Async XLA Ops:
  6.5 98.6 %reduce-scatter.2.cloned.1.call-start = ((), (), s32[]{:S(2)}) async-start(), calls=%async_computation.1 | async-start | bytes 327680 | tf_op jit(solution)/shard_map/reduce_scatter | solution.py:111
  8.8 3.5 %copy-start.4 = (s32[16]{0:T(128)}, s32[16]{0:T(128)S(1)}, u32[]{:S(2)}) copy-start(s32[16]{0:T(128)S(1)} %iota_add_fusion) | copy-start | bytes 196
  16.8 11.9 %copy-start.1 = (f32[1,16,1024]{2,1,0:T(8,128)S(1)}, f32[1,16,1024]{2,1,0:T(8,128)}, u32[]{:S(2)}) copy-start(f32[1,16,1024]{2,1,0:T(8,128)} %param.12) | copy-start | bytes 196612
  26.1 11.9 %copy-start.3 = (f32[1,16,1024]{2,1,0:T(8,128)S(1)}, f32[1,16,1024]{2,1,0:T(8,128)}, u32[]{:S(2)}) copy-start(f32[1,16,1024]{2,1,0:T(8,128)} %param.13) | copy-start | bytes 196612
  38.0 2.5 %copy-start = (bf16[1,1024,1024]{2,1,0:T(8,128)(2,1)S(1)}, bf16[1,1024,1024]{2,1,0:T(8,128)(2,1)}, u32[]{:S(2)}) copy-start(bf16[1,1024,1024]{2,1,0:T(8,128)(2,1)} %param.10) | copy-start | bytes 6291460
  40.5 7.2 %collective-permute-start.1 = (bf16[16,1024]{1,0:T(8,128)(2,1)}, bf16[16,1024]{1,0:T(8,128)(2,1)S(1)}, u32[]{:S(2)}, u32[]{:S(2)}) collective-permute-start(bf16[16,1024]{1,0:T(8,128)(2,1)} %get-tuple-element.1106), channel_id=1, source_target_pairs={{12,0},{0,4},{4,8},{8,12},{13,1},{1,5},{5,9},{9,13},{14,2},{2,6},{... | collective-permute-start | bytes 98312 | tf_op jit(solution)/shard_map/while/body/eval_jaxpr/ppermute | solution.py:19
  43.6 9.1 %collective-permute-start = (bf16[16,1024]{1,0:T(8,128)(2,1)}, bf16[16,1024]{1,0:T(8,128)(2,1)S(1)}, u32[]{:S(2)}, u32[]{:S(2)}) collective-permute-start(bf16[16,1024]{1,0:T(8,128)(2,1)} %get-tuple-element.1105), channel_id=1, source_target_pairs={{12,0},{0,4},{4,8},{8,12},{13,1},{1,5},{5,9},{9,13},{14,2},{2,6},{... | collective-permute-start | bytes 98312 | tf_op jit(solution)/shard_map/while/body/eval_jaxpr/ppermute | solution.py:19
  54.5 1.7 %copy-start.5 = (s32[16]{0:T(128)S(1)}, s32[16]{0:T(128)}, u32[]{:S(2)}) copy-start(s32[16]{0:T(128)} %get-tuple-element.1130) | copy-start | bytes 196 | tf_op jit(solution)/shard_map/while
  56.5 6.0 %collective-permute-start.1 = (bf16[16,1024]{1,0:T(8,128)(2,1)}, bf16[16,1024]{1,0:T(8,128)(2,1)S(1)}, u32[]{:S(2)}, u32[]{:S(2)}) collective-permute-start(bf16[16,1024]{1,0:T(8,128)(2,1)} %get-tuple-element.1106), channel_id=1, source_target_pairs={{12,0},{0,4},{4,8},{8,12},{13,1},{1,5},{5,9},{9,13},{14,2},{2,6},{... | collective-permute-start | bytes 98312 | tf_op jit(solution)/shard_map/while/body/eval_jaxpr/ppermute | solution.py:19
  56.7 10.7 %collective-permute-start = (bf16[16,1024]{1,0:T(8,128)(2,1)}, bf16[16,1024]{1,0:T(8,128)(2,1)S(1)}, u32[]{:S(2)}, u32[]{:S(2)}) collective-permute-start(bf16[16,1024]{1,0:T(8,128)(2,1)} %get-tuple-element.1105), channel_id=1, source_target_pairs={{12,0},{0,4},{4,8},{8,12},{13,1},{1,5},{5,9},{9,13},{14,2},{2,6},{... | collective-permute-start | bytes 98312 | tf_op jit(solution)/shard_map/while/body/eval_jaxpr/ppermute | solution.py:19
  69.3 1.7 %copy-start.5 = (s32[16]{0:T(128)S(1)}, s32[16]{0:T(128)}, u32[]{:S(2)}) copy-start(s32[16]{0:T(128)} %get-tuple-element.1130) | copy-start | bytes 196 | tf_op jit(solution)/shard_map/while
  71.2 6.0 %collective-permute-start.1 = (bf16[16,1024]{1,0:T(8,128)(2,1)}, bf16[16,1024]{1,0:T(8,128)(2,1)S(1)}, u32[]{:S(2)}, u32[]{:S(2)}) collective-permute-start(bf16[16,1024]{1,0:T(8,128)(2,1)} %get-tuple-element.1106), channel_id=1, source_target_pairs={{12,0},{0,4},{4,8},{8,12},{13,1},{1,5},{5,9},{9,13},{14,2},{2,6},{... | collective-permute-start | bytes 98312 | tf_op jit(solution)/shard_map/while/body/eval_jaxpr/ppermute | solution.py:19
  71.3 10.8 %collective-permute-start = (bf16[16,1024]{1,0:T(8,128)(2,1)}, bf16[16,1024]{1,0:T(8,128)(2,1)S(1)}, u32[]{:S(2)}, u32[]{:S(2)}) collective-permute-start(bf16[16,1024]{1,0:T(8,128)(2,1)} %get-tuple-element.1105), channel_id=1, source_target_pairs={{12,0},{0,4},{4,8},{8,12},{13,1},{1,5},{5,9},{9,13},{14,2},{2,6},{... | collective-permute-start | bytes 98312 | tf_op jit(solution)/shard_map/while/body/eval_jaxpr/ppermute | solution.py:19
  84.0 1.7 %copy-start.5 = (s32[16]{0:T(128)S(1)}, s32[16]{0:T(128)}, u32[]{:S(2)}) copy-start(s32[16]{0:T(128)} %get-tuple-element.1130) | copy-start | bytes 196 | tf_op jit(solution)/shard_map/while
  86.0 0.7 copy-start.2
Sparse Core Ops, SparseCore 0:
  86.9 18.2 reduce-scatter.1
where the time goes:
time: 114 us; the launch traced here: 113 us
  local copies, waits for them, and re-layouts  37.3 us (33%)
  waiting for transfers between devices  30.9 us (27%)
  between operations  13.6 us (12%)
  other arithmetic  13.2 us (12%)
  matrix products  11.6 us (10%)
  starting transfers between devices  6.58 us (6%)
    reduce_scatter x1, waiting for transfers between devices, per_device(): summed = lax.psum_scatter(stored, 'tm', scatter_dimension=0, tiled=True)  18.4 us
    ppermute x6, waiting for transfers between devices, passed_along(): return lax.ppermute(block, axis, route)  12.4 us
    slice x58, local copies, waits for them, and re-layouts, shifted(): behind_rows = jnp.roll(values, SIDE, axis=-1)  9.41 us
    slice x58, local copies, waits for them, and re-layouts, shifted(): jnp.roll(values, 1 - SIDE, axis=-1)  9.38 us
    slice x58, local copies, waits for them, and re-layouts, shifted(): jnp.roll(values, 1, axis=-1)  8.79 us
    dot_general x3, matrix products, advance(): jnp.dot(partner_low, inverse_map, preferred_element_type=jnp.float32)  7.75 us
    ppermute x6, starting transfers between devices, passed_along(): return lax.ppermute(block, axis, route)  6.58 us
    dot_general x3, matrix products, advance(): lax.dot_general(forward_low, forward_map, (((1,), (1,)), ((), ())), prefe...  3.81 us
  transfers between devices with their start and end apart: 7, of which 4 were waited for; matrix products, arithmetic and copies ran while one was open for 13% of the time, Pallas kernels for 0%

commit v1 on v0

v1 whole, which is shorter than its diff:
```python
import functools
import math

import jax
import jax.numpy as jnp
from jax import lax
from jax.experimental import pallas as pl
from jax.experimental.pallas import tpu as pltpu
from jax.sharding import PartitionSpec as P

time_step = 0.25
field_coupling = math.log(math.exp(0.5) + math.sqrt(math.exp(1.0) - 1.0))

LANES = 128


def rolled(blocks, shift):
    return [pltpu.roll(block, shift % LANES, 1) for block in blocks]


def hops(blocks, side, coefs):
    count = len(blocks)
    lane = lax.broadcasted_iota(jnp.int32, blocks[0].shape, 1)
    column = lane % side
    ahead = rolled(blocks, -side)
    behind = rolled(blocks, side)
    right, right_wrap = rolled(blocks, -1), rolled(blocks, side - 1)
    left, left_wrap = rolled(blocks, 1), rolled(blocks, 1 - side)
    out = []
    for j in range(count):
        row_ahead = jnp.where(lane < LANES - side, ahead[j], ahead[(j + 1) % count])
        row_behind = jnp.where(lane >= side, behind[j], behind[j - 1])
        column_ahead = jnp.where(column == side - 1, right_wrap[j], right[j])
        column_behind = jnp.where(column == 0, left_wrap[j], left[j])
        up, down, forth, back = [c[j] for c in coefs]
        out.append(up * row_ahead + down * row_behind + (forth * column_ahead + back * column_behind))
    return out


def series(blocks, side, coefs, sign):
    inner = [u + (0.5 * sign) * h for u, h in zip(blocks, hops(blocks, side, coefs))]
    return [u + sign * h for u, h in zip(blocks, hops(inner, side, coefs))]


def split(values):
    return [values[:, j : j + LANES] for j in range(0, values.shape[1], LANES)]


def coupling_blocks(bonds, side):
    weights = bonds.astype(jnp.float32) * time_step
    rows, columns = split(weights[0:1]), split(weights[1:2])
    count = len(rows)
    lane = lax.broadcasted_iota(jnp.int32, rows[0].shape, 1)
    moved = rolled(rows, side)
    rows_back = [jnp.where(lane >= side, moved[j], moved[j - 1]) for j in range(count)]
    columns_back = [
        jnp.where(lane % side == 0, wrap, left)
        for wrap, left in zip(rolled(columns, 1 - side), rolled(columns, 1))
    ]
    return rows, rows_back, columns, columns_back


def measure_kernel(side, base_ref, forward_ref, partner_ref, field_ref, bonds_ref, out_ref):
    coefs = coupling_blocks(bonds_ref[...], side)
    spins = (2 * field_ref[...] - 1).astype(jnp.float32)
    up, down = jnp.exp(field_coupling * spins), jnp.exp(-field_coupling * spins)
    forward, partner = split(forward_ref[...]), split(partner_ref[...])
    for wrap in range(spins.shape[0]):
        scale_up, scale_down = split(up[wrap : wrap + 1]), split(down[wrap : wrap + 1])
        forward = series([u * s for u, s in zip(forward, scale_up)], side, coefs, 1.0)
        partner = series([u * s for u, s in zip(partner, scale_down)], side, coefs, -1.0)
    row = lax.broadcasted_iota(jnp.int32, forward[0].shape, 0) + base_ref[0]
    lane = lax.broadcasted_iota(jnp.int32, forward[0].shape, 1)
    for j, (f, p) in enumerate(zip(forward, partner)):
        term = jnp.where(lane + j * LANES == row, 0.0, f * p)
        out_ref[:, j * LANES : (j + 1) * LANES] = term.astype(out_ref.dtype)


def measured(base, forward, partner, field, bonds):
    vmem = pl.BlockSpec(memory_space=pltpu.VMEM)
    side = math.isqrt(bonds.shape[1])
    return pl.pallas_call(
        functools.partial(measure_kernel, side),
        out_shape=jax.ShapeDtypeStruct(forward.shape, jnp.bfloat16),
        in_specs=[pl.BlockSpec(memory_space=pltpu.SMEM), vmem, vmem, vmem, vmem],
        out_specs=vmem,
        cost_estimate=pl.CostEstimate(flops=200 * forward.size, bytes_accessed=8 * forward.size, transcendentals=0),
    )(base, forward, partner, field, bonds)


def per_device(cluster_maps, inverse_maps, seed_columns, seed_rows, ising_field, hop_bonds):
    clusters = lax.axis_size("tm")
    anchor = lax.axis_index("tm")
    ref_rows, sites = seed_columns.shape[1:]
    base = lax.axis_index(("src", "col")) * ref_rows
    same_site = jnp.arange(sites)[None, :] == (base + jnp.arange(ref_rows))[:, None]
    forward_map, inverse_map = cluster_maps[0], inverse_maps[0]
    forward = seed_columns[0]
    partner = seed_rows[0] - same_site.astype(jnp.float32)
    around = [(i, (i + 1) % clusters) for i in range(clusters)]

    def measure(forward_block, partner_block):
        return measured(base[None].astype(jnp.int32), forward_block, partner_block, ising_field[0], hop_bonds)

    terms = []
    for displacement in range(clusters):
        if displacement:
            forward_low = lax.ppermute(forward.astype(jnp.bfloat16), "tm", around)
            partner_low = lax.ppermute(partner.astype(jnp.bfloat16), "tm", around)
            forward = lax.dot_general(
                forward_low, forward_map, (((1,), (1,)), ((), ())), preferred_element_type=jnp.float32
            )
            partner = jnp.dot(partner_low, inverse_map, preferred_element_type=jnp.float32)
        terms.append(measure(forward, partner))
    terms = jnp.stack(terms)
    total = None
    for step in range(clusters):
        term = lax.dynamic_index_in_dim(terms, (anchor + step) % clusters, 0, keepdims=False)
        if step:
            term = lax.ppermute(term, "tm", [(i, (i + step) % clusters) for i in range(clusters)])
        total = term.astype(jnp.float32) if total is None else total + term.astype(jnp.float32)
    return (total * (sites / clusters))[None]


def solution(mesh):
    in_specs = (
        P("tm", "chain", None),
        P("tm", "chain", None),
        P("tm", ("src", "col"), "chain"),
        P("tm", ("src", "col"), "chain"),
        P("tm", "chain", None),
        P(),
    )
    out_specs = P("tm", ("src", "col"), "chain")
    return jax.shard_map(
        per_device, mesh=mesh, in_specs=in_specs, out_specs=out_specs, check_vma=False
    )
```

time: 114 us -> 40.5 us (0.36)
  local copies, waits for them, and re-layouts: 37.3 us -> 0.12 us
  waiting for transfers between devices: 30.9 us -> 5.22 us
  between operations: 13.6 us -> 0.05 us
  Pallas kernels: 0 us -> 10.5 us
  other arithmetic: 13.2 us -> 3.97 us
  starting transfers between devices: 6.58 us -> 13.2 us
  matrix products: 11.6 us -> 6.91 us
    slice x180 -> x0, local copies, waits for them, and re-layouts: 28.3 us -> none  [the longest x58 9.41 us: shifted(): behind_rows = jnp.roll(values, SIDE, axis=-1)]
    reduce_scatter x1 -> x0, waiting for transfers between devices: 18.4 us -> none  [per_device(): summed = lax.psum_scatter(stored, 'tm', scatter_dimension=0, tiled=True)]
    pallas_call x0 -> x4, Pallas kernels: none -> 10.5 us  [measured(): pl.pallas_call(functools.partial(measure_kernel, side), out_shape=jax.Sha...]
    concatenate x13 -> x0, local copies, waits for them, and re-layouts: 8.25 us -> none  [the longest x4 2.76 us: shifted(): behind_rows = jnp.roll(values, SIDE, axis=-1)]
    mul x12 -> x0, other arithmetic: 7.45 us -> none  [the longest x1 2.46 us: measure(): wrapped_product(forward_block, partner_block, spin_values, lattice)]
    ppermute x6 -> x9, waiting for transfers between devices: 12.4 us -> 5.22 us  [the longest x3 4.81 us: per_device(): lax.ppermute(term, 'tm', [(i, (i + step) % clusters) for i in range(clust...]
    ppermute x6 -> x9, starting transfers between devices: 6.58 us -> 13.2 us  [the longest x3 5.92 us: per_device(): forward_low = lax.ppermute(forward.astype(jnp.bfloat16), 'tm', around)]
    dot_general x6, matrix products: 11.6 us -> 6.91 us  [the longest x3 3.87 us: per_device(): lax.dot_general(forward_low, forward_map, (((1,), (1,)), ((), ())), prefe...]
  transfers between devices with their start and end apart: 7 -> 9, of which waited for: 4 -> 5; matrix products, arithmetic and copies ran while one was open for 13% -> 19% of each run, Pallas kernels for 0% -> 20%
where the time goes in v1:
time: 40.5 us; the launch traced here: 40 us
  starting transfers between devices  13.2 us (33%)
  Pallas kernels  10.5 us (26%)
  matrix products  6.91 us (17%)
  waiting for transfers between devices  5.22 us (13%)
  other arithmetic  3.97 us (10%)
    pallas_call x4, Pallas kernels, measured(): pl.pallas_call(functools.partial(measure_kernel, side), out_shape=jax.Sha...  10.5 us
    ppermute x3, starting transfers between devices, per_device(): forward_low = lax.ppermute(forward.astype(jnp.bfloat16), 'tm', around)  5.92 us
    ppermute x3, waiting for transfers between devices, per_device(): lax.ppermute(term, 'tm', [(i, (i + step) % clusters) for i in range(clust...  4.81 us
    ppermute x3, starting transfers between devices, per_device(): lax.ppermute(term, 'tm', [(i, (i + step) % clusters) for i in range(clust...  3.88 us
    dot_general x3, matrix products, per_device(): lax.dot_general(forward_low, forward_map, (((1,), (1,)), ((), ())), prefe...  3.87 us
    ppermute x3, starting transfers between devices, per_device(): partner_low = lax.ppermute(partner.astype(jnp.bfloat16), 'tm', around)  3.44 us
    dot_general x3, matrix products, per_device(): jnp.dot(partner_low, inverse_map, preferred_element_type=jnp.float32)  3.04 us
    convert_element_type x1, other arithmetic, per_device(): partner_low = lax.ppermute(partner.astype(jnp.bfloat16), 'tm', around)  1.54 us
  transfers between devices with their start and end apart: 9, of which 5 were waited for; matrix products, arithmetic and copies ran while one was open for 19% of the time, Pallas kernels for 20%

profile of v1, /device:TPU:0, one launch (start us, length us, event | category | flops | bytes accessed | tf_op | source)
XLA Modules:
  0.0 40.0 jit_solution(18319437820218199389)
XLA Ops:
  0.0 0.0 copy-start
  0.0 1.0 %bitcast_convert_fusion = bf16[16,1024]{1,0:T(8,128)(2,1)S(1)} fusion(f32[1,16,1024]{2,1,0:T(8,128)} %param.8), kind=kLoop, calls=%fused_computation.24 | loop fusion | flops 16384 | bytes 98304 | tf_op jit(solution)/shard_map/convert_element_type | solution.py:108
  1.0 3.0 %collective-permute-start = (bf16[16,1024]{1,0:T(8,128)(2,1)S(1)}, bf16[16,1024]{1,0:T(8,128)(2,1)S(1)}, u32[]{:S(2)}, u32[]{:S(2)}) collective-permute-start(bf16[16,1024]{1,0:T(8,128)(2,1)S(1)} %bitcast_convert_fusion), channel_id=1, source_target_pairs={{0,4},{4,8},{8,12},{12,0},{1,5},{5,9},{9,13},{13,1},{2,6},{6,10},{... | collective-permute-start | bytes 98312 | tf_op jit(solution)/shard_map/ppermute | solution.py:108
  4.0 1.5 %fusion.16 = (bf16[16,1024]{1,0:T(8,128)(2,1)S(1)}, f32[16,1024]{1,0:T(8,128)}) fusion(s32[16]{0:T(128)S(1)} %iota_add_fusion, f32[1,16,1024]{2,1,0:T(8,128)} %param.9), kind=kLoop, calls=%fused_computation.25 | loop fusion | flops 65536 | bytes 163904 | tf_op jit(solution)/shard_map/convert_element_type | solution.py:109
  5.6 1.6 %collective-permute-start.1 = (bf16[16,1024]{1,0:T(8,128)(2,1)S(1)}, bf16[16,1024]{1,0:T(8,128)(2,1)S(1)}, u32[]{:S(2)}, u32[]{:S(2)}) collective-permute-start(bf16[16,1024]{1,0:T(8,128)(2,1)S(1)} %get-tuple-element.5), channel_id=1, source_target_pairs={{0,4},{4,8},{8,12},{12,0},{1,5},{5,9},{9,13},{13,1},{2,6},{6,10},{... | collective-permute-start | bytes 98312 | tf_op jit(solution)/shard_map/ppermute | solution.py:109
  7.1 2.6 %shard_map.64 = bf16[16,1024]{1,0:T(8,128)(2,1)} custom-call(s32[1]{0:T(128)} %bitcast.base_ref, f32[16,1024]{1,0:T(8,128)} %bitcast.50, f32[16,1024]{1,0:T(8,128)} %get-tuple-element.6.partner_ref, s32[2,1024]{1,0:T(2,128)} %bitcast.51, s32[2,1024]{1,0:T(2,128)} %bonds_ref.7), custom_call_target="tpu_custom_call" | custom-call | flops 3276800 | bytes 131072 | tf_op jit(solution)/shard_map/pallas_call | solution.py:82
  9.8 0.0 copy-start.1
  9.8 0.0 collective-permute-done
  9.8 0.0 copy-done
  9.8 1.3 %fusion.17 = (bf16[16,1024]{1,0:T(8,128)(2,1)S(1)}, f32[16,1024]{1,0:T(8,128)}) fusion(bf16[16,1024]{1,0:T(8,128)(2,1)S(1)} %collective-permute-done, bf16[1,1024,1024]{2,1,0:T(8,128)(2,1)S(1)} %copy-done), kind=kOutput, calls=%fused_computation.26 | convolution fusion | flops 33570816 | bytes 2228224 | tf_op jit(solution)/shard_map/dot_general | solution.py:110
  11.1 1.6 %collective-permute-start.2 = (bf16[16,1024]{1,0:T(8,128)(2,1)S(1)}, bf16[16,1024]{1,0:T(8,128)(2,1)S(1)}, u32[]{:S(2)}, u32[]{:S(2)}) collective-permute-start(bf16[16,1024]{1,0:T(8,128)(2,1)S(1)} %get-tuple-element.10), channel_id=1, source_target_pairs={{0,4},{4,8},{8,12},{12,0},{1,5},{5,9},{9,13},{13,1},{2,6},{6,10},{... | collective-permute-start | bytes 98312 | tf_op jit(solution)/shard_map/ppermute | solution.py:108
  12.6 0.0 collective-permute-done.1
  12.7 0.0 copy-done.1
  12.7 1.0 %fusion.19 = (bf16[16,1024]{1,0:T(8,128)(2,1)S(1)}, f32[16,1024]{1,0:T(8,128)}) fusion(bf16[16,1024]{1,0:T(8,128)(2,1)S(1)} %collective-permute-done.1, bf16[1,1024,1024]{2,1,0:T(8,128)(2,1)S(1)} %copy-done.1), kind=kOutput, calls=%fused_computation.28 | convolution fusion | flops 33570816 | bytes 2228224 | tf_op jit(solution)/shard_map/dot_general | solution.py:113
  13.7 0.3 collective-permute-start.3
  14.0 2.6 %shard_map.65 = bf16[16,1024]{1,0:T(8,128)(2,1)} custom-call(s32[1]{0:T(128)} %bitcast.base_ref, f32[16,1024]{1,0:T(8,128)} %get-tuple-element.11.forward_ref, f32[16,1024]{1,0:T(8,128)} %get-tuple-element.15.partner_ref, s32[2,1024]{1,0:T(2,128)} %bitcast.52, s32[2,1024]{1,0:T(2,128)} %bonds_ref.7), custom_call_target="tpu_custom_call" | custom-call | flops 3276800 | bytes 131072 | tf_op jit(solution)/shard_map/pallas_call | solution.py:82
  16.6 0.0 copy-start.2
  16.6 0.2 collective-permute-done.2
  16.8 1.3 %fusion.18 = (bf16[16,1024]{1,0:T(8,128)(2,1)S(1)}, f32[16,1024]{1,0:T(8,128)}) fusion(bf16[16,1024]{1,0:T(8,128)(2,1)S(1)} %collective-permute-done.2, bf16[1,1024,1024]{2,1,0:T(8,128)(2,1)S(1)} %copy-done), kind=kOutput, calls=%fused_computation.27 | convolution fusion | flops 33570816 | bytes 2228224 | tf_op jit(solution)/shard_map/dot_general | solution.py:110
  18.1 1.3 %collective-permute-start.4 = (bf16[16,1024]{1,0:T(8,128)(2,1)S(1)}, bf16[16,1024]{1,0:T(8,128)(2,1)S(1)}, u32[]{:S(2)}, u32[]{:S(2)}) collective-permute-start(bf16[16,1024]{1,0:T(8,128)(2,1)S(1)} %get-tuple-element.12), channel_id=1, source_target_pairs={{0,4},{4,8},{8,12},{12,0},{1,5},{5,9},{9,13},{13,1},{2,6},{6,10},{... | collective-permute-start | bytes 98312 | tf_op jit(solution)/shard_map/ppermute | solution.py:108
  19.4 0.0 collective-permute-done.3
  19.4 0.0 copy-done.2
  19.4 1.0 %fusion.20 = (bf16[16,1024]{1,0:T(8,128)(2,1)S(1)}, f32[16,1024]{1,0:T(8,128)}) fusion(bf16[16,1024]{1,0:T(8,128)(2,1)S(1)} %collective-permute-done.3, bf16[1,1024,1024]{2,1,0:T(8,128)(2,1)S(1)} %copy-done.2), kind=kOutput, calls=%fused_computation.29 | convolution fusion | flops 33570816 | bytes 2228224 | tf_op jit(solution)/shard_map/dot_general | solution.py:113
  20.4 1.6 %collective-permute-start.5 = (bf16[16,1024]{1,0:T(8,128)(2,1)S(1)}, bf16[16,1024]{1,0:T(8,128)(2,1)S(1)}, u32[]{:S(2)}, u32[]{:S(2)}) collective-permute-start(bf16[16,1024]{1,0:T(8,128)(2,1)S(1)} %get-tuple-element.16), channel_id=1, source_target_pairs={{0,4},{4,8},{8,12},{12,0},{1,5},{5,9},{9,13},{13,1},{2,6},{6,10},{... | collective-permute-start | bytes 98312 | tf_op jit(solution)/shard_map/ppermute | solution.py:109
  22.0 2.6 %shard_map.66 = bf16[16,1024]{1,0:T(8,128)(2,1)} custom-call(s32[1]{0:T(128)} %bitcast.base_ref, f32[16,1024]{1,0:T(8,128)} %get-tuple-element.13.forward_ref, f32[16,1024]{1,0:T(8,128)} %get-tuple-element.17.partner_ref, s32[2,1024]{1,0:T(2,128)} %bitcast.53, s32[2,1024]{1,0:T(2,128)} %bonds_ref.7), custom_call_target="tpu_custom_call" | custom-call | flops 3276800 | bytes 131072 | tf_op jit(solution)/shard_map/pallas_call | solution.py:82
  24.6 0.0 copy-start.3
  24.6 0.0 copy-start.4
  24.6 0.0 copy-start.5
  24.6 0.0 copy-start.6
  24.6 0.0 collective-permute-done.4
  24.6 1.3 %fusion.6.forward_ref = f32[16,1024]{1,0:T(8,128)} fusion(bf16[16,1024]{1,0:T(8,128)(2,1)S(1)} %collective-permute-done.4, bf16[1,1024,1024]{2,1,0:T(8,128)(2,1)S(1)} %copy-done), kind=kOutput, calls=%fused_computation.6 | convolution fusion | flops 33554432 | bytes 2195456 | tf_op jit(solution)/shard_map/dot_general | solution.py:110
  25.9 0.2 collective-permute-done.5
  26.1 0.1 copy-done.3
  26.2 1.0 %fusion.partner_ref = f32[16,1024]{1,0:T(8,128)} fusion(bf16[16,1024]{1,0:T(8,128)(2,1)S(1)} %collective-permute-done.5, bf16[1,1024,1024]{2,1,0:T(8,128)(2,1)S(1)} %copy-done.3), kind=kOutput, calls=%fused_computation | convolution fusion | flops 33554432 | bytes 2195456 | tf_op jit(solution)/shard_map/dot_general | solution.py:113
  27.2 2.6 %shard_map.67 = bf16[16,1024]{1,0:T(8,128)(2,1)} custom-call(s32[1]{0:T(128)} %bitcast.base_ref, f32[16,1024]{1,0:T(8,128)} %fusion.6.forward_ref, f32[16,1024]{1,0:T(8,128)} %fusion.partner_ref, s32[2,1024]{1,0:T(2,128)} %bitcast.54, s32[2,1024]{1,0:T(2,128)} %bonds_ref.7), custom_call_target="tpu_custom_call" | custom-call | flops 3276800 | bytes 131072 | tf_op jit(solution)/shard_map/pallas_call | solution.py:82
  29.8 0.0 copy-done.4
  29.8 0.0 copy-done.5
  29.8 0.0 copy-done.6
  29.9 0.8 %pad_maximum_fusion = bf16[4,16,1024]{2,1,0:T(8,128)(2,1)S(1)} fusion(bf16[1,16,1024]{2,1,0:T(8,128)(2,1)} %bitcast.58, bf16[1,16,1024]{2,1,0:T(8,128)(2,1)S(1)} %bitcast.57, bf16[1,16,1024]{2,1,0:T(8,128)(2,1)S(1)} %bitcast.56, bf16[1,16,1024]{2,1,0:T(8,128)(2,1)S(1)} %bitcast.55), kind=kLoop, calls=%fused_computation.12 | loop fusion | flops 196608 | bytes 262144 | tf_op jit(solution)/shard_map/stack | solution.py:115
  30.7 1.6 %collective-permute-start.6 = (bf16[16,1024]{1,0:T(8,128)(2,1)S(1)}, bf16[16,1024]{1,0:T(8,128)(2,1)S(1)}, u32[]{:S(2)}, u32[]{:S(2)}) collective-permute-start(bf16[16,1024]{1,0:T(8,128)(2,1)S(1)} %get-tuple-element.7), channel_id=1, source_target_pairs={{0,4},{4,8},{8,12},{12,0},{1,5},{5,9},{9,13},{13,1},{2,6},{6,10},{... | collective-permute-start | bytes 98312 | tf_op jit(solution)/shard_map/ppermute | solution.py:120
  32.3 2.2 %collective-permute-start.8 = (bf16[16,1024]{1,0:T(8,128)(2,1)S(1)}, bf16[16,1024]{1,0:T(8,128)(2,1)S(1)}, u32[]{:S(2)}, u32[]{:S(2)}) collective-permute-start(bf16[16,1024]{1,0:T(8,128)(2,1)S(1)} %get-tuple-element.8), channel_id=1, source_target_pairs={{0,12},{4,0},{8,4},{12,8},{1,13},{5,1},{9,5},{13,9},{2,14},{6,2},{... | collective-permute-start | bytes 98312 | tf_op jit(solution)/shard_map/ppermute | solution.py:120
  34.5 0.0 collective-permute-start.7
  34.5 2.0 %collective-permute-done.6 = bf16[16,1024]{1,0:T(8,128)(2,1)S(1)} collective-permute-done((bf16[16,1024]{1,0:T(8,128)(2,1)S(1)}, bf16[16,1024]{1,0:T(8,128)(2,1)S(1)}, u32[]{:S(2)}, u32[]{:S(2)}) %collective-permute-start.6) | collective-permute-done | bytes 32800 | tf_op jit(solution)/shard_map/ppermute | solution.py:120
  36.6 0.1 collective-permute-done.8
  36.7 2.6 %collective-permute-done.7 = bf16[16,1024]{1,0:T(8,128)(2,1)S(1)} collective-permute-done((bf16[16,1024]{1,0:T(8,128)(2,1)S(1)}, bf16[16,1024]{1,0:T(8,128)(2,1)S(1)}, u32[]{:S(2)}, u32[]{:S(2)}) %collective-permute-start.7) | collective-permute-done | bytes 32800 | tf_op jit(solution)/shard_map/ppermute | solution.py:120
  39.4 0.7 %fusion.15 = f32[1,16,1024]{2,1,0:T(8,128)} fusion(bf16[16,1024]{1,0:T(8,128)(2,1)S(1)} %collective-permute-done.8, bf16[16,1024]{1,0:T(8,128)(2,1)S(1)} %collective-permute-done.7, bf16[16,1024]{1,0:T(8,128)(2,1)S(1)} %collective-permute-done.6, bf16[4,16,1024]{2,1,0:T(8,128)(2,1)S(1)} %pad_maximum_fusion, s32[]{:T(128)S(6)} %select_n.33), kind=kLoop, calls=%fused_computation.17 | loop fusion | flops 131072 | bytes 196612 | tf_op jit(solution)/shard_map/broadcast_in_dim | solution.py:122
  (2 shorter events, 0.0 us)
Async XLA Ops:
  0.0 9.8 %copy-start = (bf16[1,1024,1024]{2,1,0:T(8,128)(2,1)S(1)}, bf16[1,1024,1024]{2,1,0:T(8,128)(2,1)}, u32[]{:S(2)}) copy-start(bf16[1,1024,1024]{2,1,0:T(8,128)(2,1)} %param.6) | copy-start | bytes 6291460
  1.0 8.8 %collective-permute-start = (bf16[16,1024]{1,0:T(8,128)(2,1)S(1)}, bf16[16,1024]{1,0:T(8,128)(2,1)S(1)}, u32[]{:S(2)}, u32[]{:S(2)}) collective-permute-start(bf16[16,1024]{1,0:T(8,128)(2,1)S(1)} %bitcast_convert_fusion), channel_id=1, source_target_pairs={{0,4},{4,8},{8,12},{12,0},{1,5},{5,9},{9,13},{13,1},{2,6},{6,10},{... | collective-permute-start | bytes 98312 | tf_op jit(solution)/shard_map/ppermute | solution.py:108
  5.6 7.1 %collective-permute-start.1 = (bf16[16,1024]{1,0:T(8,128)(2,1)S(1)}, bf16[16,1024]{1,0:T(8,128)(2,1)S(1)}, u32[]{:S(2)}, u32[]{:S(2)}) collective-permute-start(bf16[16,1024]{1,0:T(8,128)(2,1)S(1)} %get-tuple-element.5), channel_id=1, source_target_pairs={{0,4},{4,8},{8,12},{12,0},{1,5},{5,9},{9,13},{13,1},{2,6},{6,10},{... | collective-permute-start | bytes 98312 | tf_op jit(solution)/shard_map/ppermute | solution.py:109
  9.8 2.9 %copy-start.1 = (bf16[1,1024,1024]{2,1,0:T(8,128)(2,1)S(1)}, bf16[1,1024,1024]{2,1,0:T(8,128)(2,1)}, u32[]{:S(2)}) copy-start(bf16[1,1024,1024]{2,1,0:T(8,128)(2,1)} %param.7) | copy-start | bytes 6291460
  11.1 5.7 %collective-permute-start.2 = (bf16[16,1024]{1,0:T(8,128)(2,1)S(1)}, bf16[16,1024]{1,0:T(8,128)(2,1)S(1)}, u32[]{:S(2)}, u32[]{:S(2)}) collective-permute-start(bf16[16,1024]{1,0:T(8,128)(2,1)S(1)} %get-tuple-element.10), channel_id=1, source_target_pairs={{0,4},{4,8},{8,12},{12,0},{1,5},{5,9},{9,13},{13,1},{2,6},{6,10},{... | collective-permute-start | bytes 98312 | tf_op jit(solution)/shard_map/ppermute | solution.py:108
  13.7 5.7 %collective-permute-start.3 = (bf16[16,1024]{1,0:T(8,128)(2,1)S(1)}, bf16[16,1024]{1,0:T(8,128)(2,1)S(1)}, u32[]{:S(2)}, u32[]{:S(2)}) collective-permute-start(bf16[16,1024]{1,0:T(8,128)(2,1)S(1)} %get-tuple-element.14), channel_id=1, source_target_pairs={{0,4},{4,8},{8,12},{12,0},{1,5},{5,9},{9,13},{13,1},{2,6},{6,10},{... | collective-permute-start | bytes 98312 | tf_op jit(solution)/shard_map/ppermute | solution.py:109
  16.6 2.8 %copy-start.2 = (bf16[1,1024,1024]{2,1,0:T(8,128)(2,1)S(1)}, bf16[1,1024,1024]{2,1,0:T(8,128)(2,1)}, u32[]{:S(2)}) copy-start(bf16[1,1024,1024]{2,1,0:T(8,128)(2,1)} %param.7) | copy-start | bytes 6291460
  18.1 6.6 %collective-permute-start.4 = (bf16[16,1024]{1,0:T(8,128)(2,1)S(1)}, bf16[16,1024]{1,0:T(8,128)(2,1)S(1)}, u32[]{:S(2)}, u32[]{:S(2)}) collective-permute-start(bf16[16,1024]{1,0:T(8,128)(2,1)S(1)} %get-tuple-element.12), channel_id=1, source_target_pairs={{0,4},{4,8},{8,12},{12,0},{1,5},{5,9},{9,13},{13,1},{2,6},{6,10},{... | collective-permute-start | bytes 98312 | tf_op jit(solution)/shard_map/ppermute | solution.py:108
  20.4 5.7 %collective-permute-start.5 = (bf16[16,1024]{1,0:T(8,128)(2,1)S(1)}, bf16[16,1024]{1,0:T(8,128)(2,1)S(1)}, u32[]{:S(2)}, u32[]{:S(2)}) collective-permute-start(bf16[16,1024]{1,0:T(8,128)(2,1)S(1)} %get-tuple-element.16), channel_id=1, source_target_pairs={{0,4},{4,8},{8,12},{12,0},{1,5},{5,9},{9,13},{13,1},{2,6},{6,10},{... | collective-permute-start | bytes 98312 | tf_op jit(solution)/shard_map/ppermute | solution.py:109
  24.6 1.6 %copy-start.3 = (bf16[1,1024,1024]{2,1,0:T(8,128)(2,1)S(1)}, bf16[1,1024,1024]{2,1,0:T(8,128)(2,1)}, u32[]{:S(2)}) copy-start(bf16[1,1024,1024]{2,1,0:T(8,128)(2,1)} %param.7) | copy-start | bytes 6291460
  24.6 5.2 %copy-start.4 = (bf16[16,1024]{1,0:T(8,128)(2,1)S(1)}, bf16[16,1024]{1,0:T(8,128)(2,1)}, u32[]{:S(2)}) copy-start(bf16[16,1024]{1,0:T(8,128)(2,1)} %shard_map.64) | copy-start | bytes 98308
  24.6 5.2 %copy-start.5 = (bf16[16,1024]{1,0:T(8,128)(2,1)S(1)}, bf16[16,1024]{1,0:T(8,128)(2,1)}, u32[]{:S(2)}) copy-start(bf16[16,1024]{1,0:T(8,128)(2,1)} %shard_map.65) | copy-start | bytes 98308
  24.6 5.2 %copy-start.6 = (bf16[16,1024]{1,0:T(8,128)(2,1)S(1)}, bf16[16,1024]{1,0:T(8,128)(2,1)}, u32[]{:S(2)}) copy-start(bf16[16,1024]{1,0:T(8,128)(2,1)} %shard_map.66) | copy-start | bytes 98308
  30.7 5.9 %collective-permute-start.6 = (bf16[16,1024]{1,0:T(8,128)(2,1)S(1)}, bf16[16,1024]{1,0:T(8,128)(2,1)S(1)}, u32[]{:S(2)}, u32[]{:S(2)}) collective-permute-start(bf16[16,1024]{1,0:T(8,128)(2,1)S(1)} %get-tuple-element.7), channel_id=1, source_target_pairs={{0,4},{4,8},{8,12},{12,0},{1,5},{5,9},{9,13},{13,1},{2,6},{6,10},{... | collective-permute-start | bytes 98312 | tf_op jit(solution)/shard_map/ppermute | solution.py:120
  32.3 4.4 %collective-permute-start.8 = (bf16[16,1024]{1,0:T(8,128)(2,1)S(1)}, bf16[16,1024]{1,0:T(8,128)(2,1)S(1)}, u32[]{:S(2)}, u32[]{:S(2)}) collective-permute-start(bf16[16,1024]{1,0:T(8,128)(2,1)S(1)} %get-tuple-element.8), channel_id=1, source_target_pairs={{0,12},{4,0},{8,4},{12,8},{1,13},{5,1},{9,5},{13,9},{2,14},{6,2},{... | collective-permute-start | bytes 98312 | tf_op jit(solution)/shard_map/ppermute | solution.py:120
  34.5 4.8 %collective-permute-start.7 = (bf16[16,1024]{1,0:T(8,128)(2,1)S(1)}, bf16[16,1024]{1,0:T(8,128)(2,1)S(1)}, u32[]{:S(2)}, u32[]{:S(2)}) collective-permute-start(bf16[16,1024]{1,0:T(8,128)(2,1)S(1)} %get-tuple-element.9), channel_id=1, source_target_pairs={{0,8},{4,12},{8,0},{12,4},{1,9},{5,13},{9,1},{13,5},{2,10},{6,14},... | collective-permute-start | bytes 98312 | tf_op jit(solution)/shard_map/ppermute | solution.py:120

commit v2 on v1

--- a/solution.py
+++ b/solution.py
@@ -84,6 +84,7 @@
         out_shape=jax.ShapeDtypeStruct(forward.shape, jnp.bfloat16),
         in_specs=[pl.BlockSpec(memory_space=pltpu.SMEM), vmem, vmem, vmem, vmem],
         out_specs=vmem,
+        compiler_params=pltpu.CompilerParams(vmem_limit_bytes=4 << 20),
         cost_estimate=pl.CostEstimate(flops=200 * forward.size, bytes_accessed=8 * forward.size, transcendentals=0),
     )(base, forward, partner, field, bonds)
 
@@ -105,19 +106,20 @@
     terms = []
     for displacement in range(clusters):
         if displacement:
-            forward_low = lax.ppermute(forward.astype(jnp.bfloat16), "tm", around)
-            partner_low = lax.ppermute(partner.astype(jnp.bfloat16), "tm", around)
+            low = jnp.concatenate([forward.astype(jnp.bfloat16), partner.astype(jnp.bfloat16)])
+            low = lax.ppermute(low, "tm", around)
             forward = lax.dot_general(
-                forward_low, forward_map, (((1,), (1,)), ((), ())), preferred_element_type=jnp.float32
+                low[:ref_rows], forward_map, (((1,), (1,)), ((), ())), preferred_element_type=jnp.float32
             )
-            partner = jnp.dot(partner_low, inverse_map, preferred_element_type=jnp.float32)
+            partner = jnp.dot(low[ref_rows:], inverse_map, preferred_element_type=jnp.float32)
         terms.append(measure(forward, partner))
     terms = jnp.stack(terms)
     total = None
-    for step in range(clusters):
-        term = lax.dynamic_index_in_dim(terms, (anchor + step) % clusters, 0, keepdims=False)
+    for step in (0,1,2,3):
+        place = anchor ^ step
+        term = lax.dynamic_index_in_dim(terms, place, 0, keepdims=False)
         if step:
-            term = lax.ppermute(term, "tm", [(i, (i + step) % clusters) for i in range(clusters)])
+            term = lax.ppermute(term, "tm", [(i, i ^ step) for i in range(clusters)])
         total = term.astype(jnp.float32) if total is None else total + term.astype(jnp.float32)
     return (total * (sites / clusters))[None]
 

time: 40.5 us -> 33.2 us (0.82)
  waiting for transfers between devices: 5.22 us -> 15.5 us
  starting transfers between devices: 13.2 us -> 6.74 us
  Pallas kernels: 10.5 us -> 4.61 us
  matrix products: 6.91 us -> 3.11 us
  other arithmetic: 3.97 us -> 2.91 us
    ppermute x9 -> x6, waiting for transfers between devices: 5.22 us -> 15.5 us  [the longest x3 12.8 us: per_device(): low = lax.ppermute(low, 'tm', around)]
    ppermute x9 -> x6, starting transfers between devices: 13.2 us -> 6.74 us  [the longest x3 3.55 us: per_device(): term = lax.ppermute(term, 'tm', [(i, i ^ step) for i in range(clusters)])]
    pallas_call x4, Pallas kernels: 10.5 us -> 4.61 us  [measured(): pl.pallas_call(functools.partial(measure_kernel, side), out_shape=jax.Sha...]
    dot_general x6, matrix products: 6.91 us -> 3.11 us  [the longest x3 1.95 us: per_device(): lax.dot_general(low[:ref_rows], forward_map, (((1,), (1,)), ((), ())), pr...]
    another operation x1, other arithmetic: 0.78 us -> 0.02 us  [per_device(): terms = jnp.stack(terms)]
  transfers between devices with their start and end apart: 9 -> 6, of which waited for: 5 -> 6; matrix products, arithmetic and copies ran while one was open for 19% -> 0% of each run, Pallas kernels for 20% -> 10%
where the time goes in v2:
time: 33.2 us; the launch traced here: 33.1 us
  waiting for transfers between devices  15.5 us (47%)
  starting transfers between devices  6.74 us (20%)
  Pallas kernels  4.61 us (14%)
  matrix products  3.11 us (9%)
  other arithmetic  2.91 us (9%)
    ppermute x3, waiting for transfers between devices, per_device(): low = lax.ppermute(low, 'tm', around)  12.8 us
    pallas_call x4, Pallas kernels, measured(): pl.pallas_call(functools.partial(measure_kernel, side), out_shape=jax.Sha...  4.61 us
    ppermute x3, starting transfers between devices, per_device(): term = lax.ppermute(term, 'tm', [(i, i ^ step) for i in range(clusters)])  3.55 us
    ppermute x3, starting transfers between devices, per_device(): low = lax.ppermute(low, 'tm', around)  3.19 us
    ppermute x3, waiting for transfers between devices, per_device(): term = lax.ppermute(term, 'tm', [(i, i ^ step) for i in range(clusters)])  2.65 us
    dot_general x3, matrix products, per_device(): lax.dot_general(low[:ref_rows], forward_map, (((1,), (1,)), ((), ())), pr...  1.95 us
    convert_element_type x1, other arithmetic, per_device(): partner.astype(jnp.bfloat16)  1.21 us
    dot_general x3, matrix products, per_device(): jnp.dot(low[ref_rows:], inverse_map, preferred_element_type=jnp.float32)  1.15 us
  transfers between devices with their start and end apart: 6, of which 6 were waited for; matrix products, arithmetic and copies ran while one was open for 0% of the time, Pallas kernels for 10%

profile of v2, /device:TPU:0, one launch (start us, length us, event | category | flops | bytes accessed | tf_op | source)
XLA Modules:
  0.0 33.1 jit_solution(833913530681829198)
XLA Ops:
  0.0 0.0 copy-start
  0.0 0.0 copy-start.4
  0.0 1.0 %bitcast_convert_fusion = bf16[16,1024]{1,0:T(8,128)(2,1)S(1)} fusion(f32[1,16,1024]{2,1,0:T(8,128)} %param.8), kind=kLoop, calls=%fused_computation.33 | loop fusion | flops 16384 | bytes 98304 | tf_op jit(solution)/shard_map/convert_element_type | solution.py:109
  1.0 1.2 %fusion.22 = (bf16[16,1024]{1,0:T(8,128)(2,1)S(1)}, f32[16,1024]{1,0:T(8,128)S(1)}) fusion(s32[16]{0:T(128)S(1)} %iota_add_fusion, f32[1,16,1024]{2,1,0:T(8,128)} %param.9), kind=kLoop, calls=%fused_computation.34 | loop fusion | flops 65536 | bytes 163904 | tf_op jit(solution)/shard_map/convert_element_type | solution.py:109
  2.2 3.1 %collective-permute-start = (bf16[32,1024]{1,0:T(8,128)(2,1)S(1)}, bf16[32,1024]{1,0:T(8,128)(2,1)S(1)}, u32[]{:S(2)}, u32[]{:S(2)}) collective-permute-start(bf16[32,1024]{1,0:T(8,128)(2,1)S(1)} %pad_maximum_fusion.1), channel_id=1, source_target_pairs={{0,4},{4,8},{8,12},{12,0},{1,5},{5,9},{9,13},{13,1},{2,6},{6,10},{... | collective-permute-start | bytes 196616 | tf_op jit(solution)/shard_map/ppermute | solution.py:110
  5.3 4.3 %collective-permute-done = bf16[32,1024]{1,0:T(8,128)(2,1)S(1)} collective-permute-done((bf16[32,1024]{1,0:T(8,128)(2,1)S(1)}, bf16[32,1024]{1,0:T(8,128)(2,1)S(1)}, u32[]{:S(2)}, u32[]{:S(2)}) %collective-permute-start) | collective-permute-done | bytes 65568 | tf_op jit(solution)/shard_map/ppermute | solution.py:110
  9.6 0.0 copy-done
  9.6 0.4 %fusion.23 = (bf16[16,1024]{1,0:T(8,128)(2,1)S(1)}, f32[16,1024]{1,0:T(8,128)S(1)}) fusion(bf16[1,1024,1024]{2,1,0:T(8,128)(2,1)S(1)} %copy-done, bf16[32,1024]{1,0:T(8,128)(2,1)S(1)} %collective-permute-done), kind=kOutput, calls=%fused_computation.35 | convolution fusion | flops 33570816 | bytes 2228224 | tf_op jit(solution)/shard_map/dot_general | solution.py:114
  10.0 0.0 copy-done.4
  10.0 0.7 %fusion.24 = (bf16[16,1024]{1,0:T(8,128)(2,1)S(1)}, f32[16,1024]{1,0:T(8,128)S(1)}) fusion(bf16[1,1024,1024]{2,1,0:T(8,128)(2,1)S(1)} %copy-done.4, bf16[32,1024]{1,0:T(8,128)(2,1)S(1)} %collective-permute-done), kind=kOutput, calls=%fused_computation.36 | convolution fusion | flops 33570816 | bytes 2228224 | tf_op jit(solution)/shard_map/dot_general | solution.py:111
  10.6 0.0 copy-start.1
  10.7 0.0 copy-start.2
  10.7 0.0 copy-start.3
  10.7 0.1 collective-permute-start.1
  10.7 6.0 %collective-permute-done.1 = bf16[32,1024]{1,0:T(8,128)(2,1)S(1)} collective-permute-done((bf16[32,1024]{1,0:T(8,128)(2,1)S(1)}, bf16[32,1024]{1,0:T(8,128)(2,1)S(1)}, u32[]{:S(2)}, u32[]{:S(2)}) %collective-permute-start.1) | collective-permute-done | bytes 65568 | tf_op jit(solution)/shard_map/ppermute | solution.py:110
  16.8 0.4 %fusion.25 = (bf16[16,1024]{1,0:T(8,128)(2,1)S(1)}, f32[16,1024]{1,0:T(8,128)S(1)}) fusion(bf16[1,1024,1024]{2,1,0:T(8,128)(2,1)S(1)} %copy-done, bf16[32,1024]{1,0:T(8,128)(2,1)S(1)} %collective-permute-done.1), kind=kOutput, calls=%fused_computation.37 | convolution fusion | flops 33570816 | bytes 2228224 | tf_op jit(solution)/shard_map/dot_general | solution.py:114
  17.2 0.7 %fusion.26 = (bf16[16,1024]{1,0:T(8,128)(2,1)S(1)}, f32[16,1024]{1,0:T(8,128)S(1)}) fusion(bf16[1,1024,1024]{2,1,0:T(8,128)(2,1)S(1)} %copy-done.4, bf16[32,1024]{1,0:T(8,128)(2,1)S(1)} %collective-permute-done.1), kind=kOutput, calls=%fused_computation.38 | convolution fusion | flops 33570816 | bytes 2228224 | tf_op jit(solution)/shard_map/dot_general | solution.py:111
  17.9 0.1 collective-permute-start.2
  17.9 0.0 copy-start.5
  18.0 0.0 copy-done.1
  18.0 0.0 copy-done.2
  18.0 0.0 copy-done.3
  18.0 1.1 %shard_map.64 = bf16[16,1024]{1,0:T(8,128)(2,1)S(1)} custom-call(s32[1]{0:T(128)} %bitcast.base_ref, f32[16,1024]{1,0:T(8,128)S(1)} %bitcast.44, f32[16,1024]{1,0:T(8,128)S(1)} %get-tuple-element.6.partner_ref, s32[2,1024]{1,0:T(2,128)S(1)} %bitcast.45, s32[2,1024]{1,0:T(2,128)S(1)} %copy-done.3), custom_call_target="tpu_custom_call" | custom-call | flops 3276800 | bytes 131072 | tf_op jit(solution)/shard_map/pallas_call | solution.py:82
  19.1 1.1 %shard_map.65 = bf16[16,1024]{1,0:T(8,128)(2,1)S(1)} custom-call(s32[1]{0:T(128)} %bitcast.base_ref, f32[16,1024]{1,0:T(8,128)S(1)} %get-tuple-element.13.forward_ref, f32[16,1024]{1,0:T(8,128)S(1)} %get-tuple-element.11.partner_ref, s32[2,1024]{1,0:T(2,128)S(1)} %bitcast.46, s32[2,1024]{1,0:T(2,128)S(1)} %copy-done.3), custom_call_target="tpu_custom_call" | custom-call | flops 3276800 | bytes 131072 | tf_op jit(solution)/shard_map/pallas_call | solution.py:82
  20.3 1.1 %shard_map.66 = bf16[16,1024]{1,0:T(8,128)(2,1)S(1)} custom-call(s32[1]{0:T(128)} %bitcast.base_ref, f32[16,1024]{1,0:T(8,128)S(1)} %get-tuple-element.17.forward_ref, f32[16,1024]{1,0:T(8,128)S(1)} %get-tuple-element.15.partner_ref, s32[2,1024]{1,0:T(2,128)S(1)} %bitcast.47, s32[2,1024]{1,0:T(2,128)S(1)} %copy-done.3), custom_call_target="tpu_custom_call" | custom-call | flops 3276800 | bytes 131072 | tf_op jit(solution)/shard_map/pallas_call | solution.py:82
  21.5 2.5 %collective-permute-done.2 = bf16[32,1024]{1,0:T(8,128)(2,1)S(1)} collective-permute-done((bf16[32,1024]{1,0:T(8,128)(2,1)S(1)}, bf16[32,1024]{1,0:T(8,128)(2,1)S(1)}, u32[]{:S(2)}, u32[]{:S(2)}) %collective-permute-start.2) | collective-permute-done | bytes 65568 | tf_op jit(solution)/shard_map/ppermute | solution.py:110
  24.0 0.4 %fusion.partner_ref = f32[16,1024]{1,0:T(8,128)S(1)} fusion(bf16[1,1024,1024]{2,1,0:T(8,128)(2,1)S(1)} %copy-done, bf16[32,1024]{1,0:T(8,128)(2,1)S(1)} %collective-permute-done.2), kind=kOutput, calls=%fused_computation | convolution fusion | flops 33554432 | bytes 2195456 | tf_op jit(solution)/shard_map/dot_general | solution.py:114
  24.4 0.0 copy-done.5
  24.4 0.7 %fusion.6.forward_ref = f32[16,1024]{1,0:T(8,128)S(1)} fusion(bf16[1,1024,1024]{2,1,0:T(8,128)(2,1)S(1)} %copy-done.5, bf16[32,1024]{1,0:T(8,128)(2,1)S(1)} %collective-permute-done.2), kind=kOutput, calls=%fused_computation.6 | convolution fusion | flops 33554432 | bytes 2195456 | tf_op jit(solution)/shard_map/dot_general | solution.py:111
  25.0 1.2 %shard_map.67 = bf16[16,1024]{1,0:T(8,128)(2,1)S(1)} custom-call(s32[1]{0:T(128)} %bitcast.base_ref, f32[16,1024]{1,0:T(8,128)S(1)} %fusion.6.forward_ref, f32[16,1024]{1,0:T(8,128)S(1)} %fusion.partner_ref, s32[2,1024]{1,0:T(2,128)S(1)} %bitcast.48, s32[2,1024]{1,0:T(2,128)S(1)} %copy-done.3), custom_call_target="tpu_custom_call" | custom-call | flops 3276800 | bytes 131072 | tf_op jit(solution)/shard_map/pallas_call | solution.py:82
  26.2 0.1 collective-permute-start.3
  26.3 1.3 %collective-permute-start.5 = (bf16[16,1024]{1,0:T(8,128)(2,1)S(1)}, bf16[16,1024]{1,0:T(8,128)(2,1)S(1)}, u32[]{:S(2)}, u32[]{:S(2)}) collective-permute-start(bf16[16,1024]{1,0:T(8,128)(2,1)S(1)} %get-tuple-element.8), channel_id=1, source_target_pairs={{0,12},{4,8},{8,4},{12,0},{1,13},{5,9},{9,5},{13,1},{2,14},{6,10},... | collective-permute-start | bytes 98312 | tf_op jit(solution)/shard_map/ppermute | solution.py:122
  27.6 2.2 %collective-permute-start.4 = (bf16[16,1024]{1,0:T(8,128)(2,1)S(1)}, bf16[16,1024]{1,0:T(8,128)(2,1)S(1)}, u32[]{:S(2)}, u32[]{:S(2)}) collective-permute-start(bf16[16,1024]{1,0:T(8,128)(2,1)S(1)} %get-tuple-element.9), channel_id=1, source_target_pairs={{0,8},{4,12},{8,0},{12,4},{1,9},{5,13},{9,1},{13,5},{2,10},{6,14},... | collective-permute-start | bytes 98312 | tf_op jit(solution)/shard_map/ppermute | solution.py:122
  29.8 0.4 %collective-permute-done.3 = bf16[16,1024]{1,0:T(8,128)(2,1)S(1)} collective-permute-done((bf16[16,1024]{1,0:T(8,128)(2,1)S(1)}, bf16[16,1024]{1,0:T(8,128)(2,1)S(1)}, u32[]{:S(2)}, u32[]{:S(2)}) %collective-permute-start.3) | collective-permute-done | bytes 32800 | tf_op jit(solution)/shard_map/ppermute | solution.py:122
  30.2 1.9 %collective-permute-done.5 = bf16[16,1024]{1,0:T(8,128)(2,1)S(1)} collective-permute-done((bf16[16,1024]{1,0:T(8,128)(2,1)S(1)}, bf16[16,1024]{1,0:T(8,128)(2,1)S(1)}, u32[]{:S(2)}, u32[]{:S(2)}) %collective-permute-start.5) | collective-permute-done | bytes 32800 | tf_op jit(solution)/shard_map/ppermute | solution.py:122
  32.1 0.4 %collective-permute-done.4 = bf16[16,1024]{1,0:T(8,128)(2,1)S(1)} collective-permute-done((bf16[16,1024]{1,0:T(8,128)(2,1)S(1)}, bf16[16,1024]{1,0:T(8,128)(2,1)S(1)}, u32[]{:S(2)}, u32[]{:S(2)}) %collective-permute-start.4) | collective-permute-done | bytes 32800 | tf_op jit(solution)/shard_map/ppermute | solution.py:122
  32.4 0.7 %fusion.15 = f32[1,16,1024]{2,1,0:T(8,128)} fusion(bf16[16,1024]{1,0:T(8,128)(2,1)S(1)} %collective-permute-done.5, bf16[16,1024]{1,0:T(8,128)(2,1)S(1)} %collective-permute-done.4, bf16[16,1024]{1,0:T(8,128)(2,1)S(1)} %collective-permute-done.3, bf16[4,16,1024]{2,1,0:T(8,128)(2,1)S(1)} %pad_maximum_fusion, s32[]{:T(128)S(6)} %select_n.13), kind=kLoop, calls=%fused_computation.20 | loop fusion | flops 131072 | bytes 196612 | tf_op jit(solution)/shard_map/broadcast_in_dim | solution.py:124
  (6 shorter events, 0.1 us)
Async XLA Ops:
  0.0 9.6 %copy-start = (bf16[1,1024,1024]{2,1,0:T(8,128)(2,1)S(1)}, bf16[1,1024,1024]{2,1,0:T(8,128)(2,1)}, u32[]{:S(2)}) copy-start(bf16[1,1024,1024]{2,1,0:T(8,128)(2,1)} %param.7) | copy-start | bytes 6291460
  0.0 10.0 %copy-start.4 = (bf16[1,1024,1024]{2,1,0:T(8,128)(2,1)S(1)}, bf16[1,1024,1024]{2,1,0:T(8,128)(2,1)}, u32[]{:S(2)}) copy-start(bf16[1,1024,1024]{2,1,0:T(8,128)(2,1)} %param.6) | copy-start | bytes 6291460
  2.2 7.3 %collective-permute-start = (bf16[32,1024]{1,0:T(8,128)(2,1)S(1)}, bf16[32,1024]{1,0:T(8,128)(2,1)S(1)}, u32[]{:S(2)}, u32[]{:S(2)}) collective-permute-start(bf16[32,1024]{1,0:T(8,128)(2,1)S(1)} %pad_maximum_fusion.1), channel_id=1, source_target_pairs={{0,4},{4,8},{8,12},{12,0},{1,5},{5,9},{9,13},{13,1},{2,6},{6,10},{... | collective-permute-start | bytes 196616 | tf_op jit(solution)/shard_map/ppermute | solution.py:110
  10.6 7.3 %copy-start.1 = (f32[1,16,1024]{2,1,0:T(8,128)S(1)}, f32[1,16,1024]{2,1,0:T(8,128)}, u32[]{:S(2)}) copy-start(f32[1,16,1024]{2,1,0:T(8,128)} %param.8) | copy-start | bytes 196612
  10.7 7.3 %copy-start.2 = (s32[1,2,1024]{2,1,0:T(2,128)S(1)}, s32[1,2,1024]{2,1,0:T(2,128)}, u32[]{:S(2)}) copy-start(s32[1,2,1024]{2,1,0:T(2,128)} %param.10) | copy-start | bytes 24580
  10.7 7.3 %copy-start.3 = (s32[2,1024]{1,0:T(2,128)S(1)}, s32[2,1024]{1,0:T(2,128)}, u32[]{:S(2)}) copy-start(s32[2,1024]{1,0:T(2,128)} %bonds_ref.7) | copy-start | bytes 24580
  10.7 6.1 %collective-permute-start.1 = (bf16[32,1024]{1,0:T(8,128)(2,1)S(1)}, bf16[32,1024]{1,0:T(8,128)(2,1)S(1)}, u32[]{:S(2)}, u32[]{:S(2)}) collective-permute-start(bf16[32,1024]{1,0:T(8,128)(2,1)S(1)} %pad_maximum_fusion.2), channel_id=1, source_target_pairs={{0,4},{4,8},{8,12},{12,0},{1,5},{5,9},{9,13},{13,1},{2,6},{6,10},{... | collective-permute-start | bytes 196616 | tf_op jit(solution)/shard_map/ppermute | solution.py:110
  17.9 6.1 %collective-permute-start.2 = (bf16[32,1024]{1,0:T(8,128)(2,1)S(1)}, bf16[32,1024]{1,0:T(8,128)(2,1)S(1)}, u32[]{:S(2)}, u32[]{:S(2)}) collective-permute-start(bf16[32,1024]{1,0:T(8,128)(2,1)S(1)} %pad_maximum_fusion.3), channel_id=1, source_target_pairs={{0,4},{4,8},{8,12},{12,0},{1,5},{5,9},{9,13},{13,1},{2,6},{6,10},{... | collective-permute-start | bytes 196616 | tf_op jit(solution)/shard_map/ppermute | solution.py:110
  17.9 6.4 %copy-start.5 = (bf16[1,1024,1024]{2,1,0:T(8,128)(2,1)S(1)}, bf16[1,1024,1024]{2,1,0:T(8,128)(2,1)}, u32[]{:S(2)}) copy-start(bf16[1,1024,1024]{2,1,0:T(8,128)(2,1)} %param.6) | copy-start | bytes 6291460
  26.2 4.0 %collective-permute-start.3 = (bf16[16,1024]{1,0:T(8,128)(2,1)S(1)}, bf16[16,1024]{1,0:T(8,128)(2,1)S(1)}, u32[]{:S(2)}, u32[]{:S(2)}) collective-permute-start(bf16[16,1024]{1,0:T(8,128)(2,1)S(1)} %get-tuple-element.7), channel_id=1, source_target_pairs={{0,4},{4,0},{8,12},{12,8},{1,5},{5,1},{9,13},{13,9},{2,6},{6,2},{1... | collective-permute-start | bytes 98312 | tf_op jit(solution)/shard_map/ppermute | solution.py:122
  26.3 5.8 %collective-permute-start.5 = (bf16[16,1024]{1,0:T(8,128)(2,1)S(1)}, bf16[16,1024]{1,0:T(8,128)(2,1)S(1)}, u32[]{:S(2)}, u32[]{:S(2)}) collective-permute-start(bf16[16,1024]{1,0:T(8,128)(2,1)S(1)} %get-tuple-element.8), channel_id=1, source_target_pairs={{0,12},{4,8},{8,4},{12,0},{1,13},{5,9},{9,5},{13,1},{2,14},{6,10},... | collective-permute-start | bytes 98312 | tf_op jit(solution)/shard_map/ppermute | solution.py:122
  27.6 4.8 %collective-permute-start.4 = (bf16[16,1024]{1,0:T(8,128)(2,1)S(1)}, bf16[16,1024]{1,0:T(8,128)(2,1)S(1)}, u32[]{:S(2)}, u32[]{:S(2)}) collective-permute-start(bf16[16,1024]{1,0:T(8,128)(2,1)S(1)} %get-tuple-element.9), channel_id=1, source_target_pairs={{0,8},{4,12},{8,0},{12,4},{1,9},{5,13},{9,1},{13,5},{2,10},{6,14},... | collective-permute-start | bytes 98312 | tf_op jit(solution)/shard_map/ppermute | solution.py:122

commit v3 on v2

v3 whole, which is shorter than its diff:
```python
import functools
import math

import jax
import jax.numpy as jnp
from jax import lax
from jax.experimental import pallas as pl
from jax.experimental.pallas import tpu as pltpu
from jax.sharding import PartitionSpec as P

time_step = 0.25
field_coupling = math.log(math.exp(0.5) + math.sqrt(math.exp(1.0) - 1.0))

LANES = 128
VMEM = pl.BlockSpec(memory_space=pltpu.VMEM)
SMEM = pl.BlockSpec(memory_space=pltpu.SMEM)
ANY = pl.BlockSpec(memory_space=pl.ANY)


def params(mebibytes=4):
    return pltpu.CompilerParams(vmem_limit_bytes=mebibytes << 20)


def cost(flops, bytes_accessed):
    return pl.CostEstimate(flops=flops, bytes_accessed=bytes_accessed, transcendentals=0)


def rolled(blocks, shift):
    return [pltpu.roll(block, shift % LANES, 1) for block in blocks]


def split(values):
    return [values[:, j : j + LANES] for j in range(0, values.shape[1], LANES)]


def hops(blocks, side, coefs):
    count = len(blocks)
    lane = lax.broadcasted_iota(jnp.int32, blocks[0].shape, 1)
    column = lane % side
    ahead = rolled(blocks, -side)
    behind = rolled(blocks, side)
    right, right_wrap = rolled(blocks, -1), rolled(blocks, side - 1)
    left, left_wrap = rolled(blocks, 1), rolled(blocks, 1 - side)
    out = []
    for j in range(count):
        row_ahead = jnp.where(lane < LANES - side, ahead[j], ahead[(j + 1) % count])
        row_behind = jnp.where(lane >= side, behind[j], behind[j - 1])
        column_ahead = jnp.where(column == side - 1, right_wrap[j], right[j])
        column_behind = jnp.where(column == 0, left_wrap[j], left[j])
        up, down, forth, back = [c[j] for c in coefs]
        out.append((up * row_ahead + down * row_behind) + (forth * column_ahead + back * column_behind))
    return out


def factors_kernel(side, field_ref, bonds_ref, out_ref):
    weights = bonds_ref[...].astype(jnp.float32) * time_step
    rows, columns = split(weights[0:1]), split(weights[1:2])
    lane = lax.broadcasted_iota(jnp.int32, rows[0].shape, 1)
    moved = rolled(rows, side)
    wrapped, left = rolled(columns, 1 - side), rolled(columns, 1)
    for j in range(len(rows)):
        place = slice(j * LANES, (j + 1) * LANES)
        out_ref[0:1, place] = rows[j]
        out_ref[1:2, place] = jnp.where(lane >= side, moved[j], moved[j - 1])
        out_ref[2:3, place] = columns[j]
        out_ref[3:4, place] = jnp.where(lane % side == 0, wrapped[j], left[j])
    spins = (2 * field_ref[...] - 1).astype(jnp.float32)
    wraps = spins.shape[0]
    out_ref[4 : 4 + wraps, :] = jnp.exp(field_coupling * spins)
    out_ref[4 + wraps : 4 + 2 * wraps, :] = jnp.exp(-field_coupling * spins)


def factors(field, bonds):
    wraps, sites = field.shape
    return pl.pallas_call(
        functools.partial(factors_kernel, math.isqrt(sites)),
        out_shape=jax.ShapeDtypeStruct((4 + 2 * wraps, sites), jnp.float32),
        in_specs=[VMEM, VMEM],
        out_specs=VMEM,
        compiler_params=params(),
        cost_estimate=cost(64 * sites, 64 * sites),
    )(field, bonds)


def measure_kernel(side, base_ref, forward_ref, partner_ref, factors_ref, out_ref):
    coefs = [split(factors_ref[k : k + 1, :]) for k in range(4)]
    wraps = (factors_ref.shape[0] - 4) // 2
    forward, partner = split(forward_ref[...]), split(partner_ref[...])
    for wrap in range(wraps):
        scale_up = split(factors_ref[4 + wrap : 5 + wrap, :])
        scale_down = split(factors_ref[4 + wraps + wrap : 5 + wraps + wrap, :])
        forward = [u * s for u, s in zip(forward, scale_up)]
        partner = [u * s for u, s in zip(partner, scale_down)]
        hop_forward, hop_partner = hops(forward, side, coefs), hops(partner, side, coefs)
        half_forward = [u + 0.5 * h for u, h in zip(forward, hop_forward)]
        half_partner = [u - 0.5 * h for u, h in zip(partner, hop_partner)]
        hop_forward, hop_partner = hops(half_forward, side, coefs), hops(half_partner, side, coefs)
        forward = [u + h for u, h in zip(forward, hop_forward)]
        partner = [u - h for u, h in zip(partner, hop_partner)]
    row = lax.broadcasted_iota(jnp.int32, forward[0].shape, 0) + base_ref[0]
    lane = lax.broadcasted_iota(jnp.int32, forward[0].shape, 1)
    for j, (f, p) in enumerate(zip(forward, partner)):
        term = jnp.where(lane + j * LANES == row, 0.0, f * p)
        out_ref[:, j * LANES : (j + 1) * LANES] = term.astype(out_ref.dtype)


def measured(base, forward, partner, rates):
    return pl.pallas_call(
        functools.partial(measure_kernel, math.isqrt(forward.shape[1])),
        out_shape=jax.ShapeDtypeStruct(forward.shape, jnp.bfloat16),
        in_specs=[SMEM, VMEM, VMEM, VMEM],
        out_specs=VMEM,
        compiler_params=params(),
        cost_estimate=cost(200 * forward.size, 12 * forward.size),
    )(base, forward, partner, rates)


def packed_kernel(base_ref, columns_ref, rows_ref, out_ref, columns, rows, arrived):
    copies = [
        pltpu.make_async_copy(columns_ref, columns, arrived.at[0]),
        pltpu.make_async_copy(rows_ref, rows, arrived.at[1]),
    ]
    for copy in copies:
        copy.start()
    for copy in copies:
        copy.wait()
    count = columns.shape[0]
    row = lax.broadcasted_iota(jnp.int32, rows.shape, 0) + base_ref[0]
    lane = lax.broadcasted_iota(jnp.int32, rows.shape, 1)
    out_ref[0:count, :] = columns[...].astype(out_ref.dtype)
    out_ref[count:, :] = jnp.where(lane == row, rows[...] - 1.0, rows[...]).astype(out_ref.dtype)


def packed(base, columns, rows):
    count, sites = columns.shape
    return pl.pallas_call(
        packed_kernel,
        out_shape=jax.ShapeDtypeStruct((2 * count, sites), jnp.bfloat16),
        in_specs=[SMEM, ANY, ANY],
        out_specs=VMEM,
        scratch_shapes=[
            pltpu.VMEM(columns.shape, columns.dtype),
            pltpu.VMEM(rows.shape, rows.dtype),
            pltpu.SemaphoreType.DMA((2,)),
        ],
        compiler_params=params(),
        cost_estimate=cost(4 * rows.size, 12 * rows.size),
    )(
        base,
        pltpu.with_memory_space_constraint(columns, pltpu.HBM),
        pltpu.with_memory_space_constraint(rows, pltpu.HBM),
    )


def turned_kernel(map_ref, out_ref):
    out_ref[...] = map_ref[...].T


def turned(dense):
    return pl.pallas_call(
        turned_kernel,
        out_shape=jax.ShapeDtypeStruct(dense.shape[::-1], dense.dtype),
        in_specs=[VMEM],
        out_specs=VMEM,
        compiler_params=params(8),
        cost_estimate=cost(dense.size, 4 * dense.size),
    )(dense)


def per_device(cluster_maps, inverse_maps, seed_columns, seed_rows, ising_field, hop_bonds):
    clusters = lax.axis_size("tm")
    anchor = lax.axis_index("tm")
    ref_rows, sites = seed_columns.shape[1:]
    first = lax.axis_index(("src", "col")) * ref_rows
    base = first[None].astype(jnp.int32)
    same_site = jnp.arange(sites)[None, :] == (first + jnp.arange(ref_rows))[:, None]
    around = [(i, (i + 1) % clusters) for i in range(clusters)]
    forward_map, inverse_map = cluster_maps[0], inverse_maps[0]
    forward = seed_columns[0]
    partner = seed_rows[0] - same_site.astype(jnp.float32)
    rates = factors(ising_field[0], hop_bonds)

    terms = [measured(base, forward, partner, rates)]
    low = packed(base, seed_columns[0], seed_rows[0])
    for displacement in range(1, clusters):
        if displacement >= 3:
            low, *terms[: displacement - 1] = lax.optimization_barrier((low, *terms[: displacement - 1]))
        low = lax.ppermute(low, "tm", around)
        forward = lax.dot_general(
            low[:ref_rows], forward_map, (((1,), (1,)), ((), ())), preferred_element_type=jnp.float32
        )
        partner = jnp.dot(low[ref_rows:], inverse_map, preferred_element_type=jnp.float32)
        terms.append(measured(base, forward, partner, rates))
        low = jnp.concatenate([forward, partner]).astype(jnp.bfloat16)
    terms = jnp.stack(terms)
    total = None
    for step in (0, 2, 1, 3):
        term = lax.dynamic_index_in_dim(terms, anchor ^ step, 0, keepdims=False)
        if step:
            term = lax.ppermute(term, "tm", [(i, i ^ step) for i in range(clusters)])
        total = term.astype(jnp.float32) if total is None else total + term.astype(jnp.float32)
    return (total * (sites / clusters))[None]


def solution(mesh):
    in_specs = (
        P("tm", "chain", None),
        P("tm", "chain", None),
        P("tm", ("src", "col"), "chain"),
        P("tm", ("src", "col"), "chain"),
        P("tm", "chain", None),
        P(),
    )
    out_specs = P("tm", ("src", "col"), "chain")
    return jax.shard_map(
        per_device, mesh=mesh, in_specs=in_specs, out_specs=out_specs, check_vma=False
    )
```

time: 33.2 us -> 31.4 us (0.946)
  other arithmetic: 2.91 us -> 0.79 us
    convert_element_type x2 -> x0, other arithmetic: 2.2 us -> none  [the longest x1 1.21 us: per_device(): partner.astype(jnp.bfloat16)]
    ppermute x3, waiting for transfers between devices: 12.8 us -> 13.4 us  [per_device(): low = lax.ppermute(low, 'tm', around)]
    ppermute x3, waiting for transfers between devices: 2.65 us -> 2.3 us  [per_device(): term = lax.ppermute(term, 'tm', [(i, i ^ step) for i in range(clusters)])]
    pallas_call x4 -> x6, Pallas kernels: 4.61 us -> 4.76 us  [the longest x4 3.61 us: measured(): pl.pallas_call(functools.partial(measure_kernel, math.isqrt(forward.shape...]
  transfers between devices with their start and end apart: 6 -> 6, of which waited for: 6 -> 5; matrix products, arithmetic and copies ran while one was open for 0% -> 0% of each run, Pallas kernels for 10% -> 9%
where the time goes in v3:
time: 31.4 us; the launch traced here: 31.3 us
  waiting for transfers between devices  15.7 us (50%)
  starting transfers between devices  6.74 us (21%)
  Pallas kernels  4.76 us (15%)
  matrix products  3.11 us (10%)
  other arithmetic  0.79 us (3%)
    ppermute x3, waiting for transfers between devices, per_device(): low = lax.ppermute(low, 'tm', around)  13.4 us
    pallas_call x4, Pallas kernels, measured(): pl.pallas_call(functools.partial(measure_kernel, math.isqrt(forward.shape...  3.61 us
    ppermute x3, starting transfers between devices, per_device(): term = lax.ppermute(term, 'tm', [(i, i ^ step) for i in range(clusters)])  3.55 us
    ppermute x3, starting transfers between devices, per_device(): low = lax.ppermute(low, 'tm', around)  3.19 us
    ppermute x3, waiting for transfers between devices, per_device(): term = lax.ppermute(term, 'tm', [(i, i ^ step) for i in range(clusters)])  2.3 us
    dot_general x3, matrix products, per_device(): lax.dot_general(low[:ref_rows], forward_map, (((1,), (1,)), ((), ())), pr...  1.95 us
    dot_general x3, matrix products, per_device(): jnp.dot(low[ref_rows:], inverse_map, preferred_element_type=jnp.float32)  1.16 us
    pallas_call x1, Pallas kernels, packed(): pl.pallas_call(packed_kernel, out_shape=jax.ShapeDtypeStruct((2 * count,...  1.05 us
  transfers between devices with their start and end apart: 6, of which 5 were waited for; matrix products, arithmetic and copies ran while one was open for 0% of the time, Pallas kernels for 9%

profile of v3, /device:TPU:0, one launch (start us, length us, event | category | flops | bytes accessed | tf_op | source)
XLA Modules:
  0.0 31.3 jit_solution(11944438707244038833)
XLA Ops:
  0.0 0.0 copy-start
  0.0 0.0 copy-start.4
  0.0 1.1 %shard_map.64 = bf16[32,1024]{1,0:T(8,128)(2,1)S(1)} custom-call(s32[1]{0:T(128)} %bitcast.base_ref, f32[16,1024]{1,0:T(8,128)} %bitcast.42, f32[16,1024]{1,0:T(8,128)} %bitcast.49), custom_call_target="tpu_custom_call" | custom-call | flops 65536 | bytes 196608 | tf_op jit(solution)/shard_map/pallas_call | solution.py:136
  1.1 3.1 %collective-permute-start = (bf16[32,1024]{1,0:T(8,128)(2,1)S(1)}, bf16[32,1024]{1,0:T(8,128)(2,1)S(1)}, u32[]{:S(2)}, u32[]{:S(2)}) collective-permute-start(bf16[32,1024]{1,0:T(8,128)(2,1)S(1)} %shard_map.64), channel_id=1, source_target_pairs={{0,4},{4,8},{8,12},{12,0},{1,5},{5,9},{9,13},{13,1},{2,6},{6,10},{... | collective-permute-start | bytes 196616 | tf_op jit(solution)/shard_map/ppermute | solution.py:188
  4.1 0.0 copy-start.6
  4.1 0.0 copy-start.2
  4.1 0.0 copy-start.3
  4.2 0.0 copy-start.1
  4.2 4.2 %collective-permute-done = bf16[32,1024]{1,0:T(8,128)(2,1)S(1)} collective-permute-done((bf16[32,1024]{1,0:T(8,128)(2,1)S(1)}, bf16[32,1024]{1,0:T(8,128)(2,1)S(1)}, u32[]{:S(2)}, u32[]{:S(2)}) %collective-permute-start) | collective-permute-done | bytes 65568 | tf_op jit(solution)/shard_map/ppermute | solution.py:188
  8.4 0.0 copy-done
  8.4 0.4 %fusion.22 = (bf16[16,1024]{1,0:T(8,128)(2,1)S(1)}, f32[16,1024]{1,0:T(8,128)S(1)}) fusion(bf16[1,1024,1024]{2,1,0:T(8,128)(2,1)S(1)} %copy-done, bf16[32,1024]{1,0:T(8,128)(2,1)S(1)} %collective-permute-done), kind=kOutput, calls=%fused_computation.32 | convolution fusion | flops 33570816 | bytes 2228224 | tf_op jit(solution)/shard_map/dot_general | solution.py:192
  8.8 0.0 copy-done.4
  8.8 0.7 %fusion.23 = (bf16[16,1024]{1,0:T(8,128)(2,1)S(1)}, f32[16,1024]{1,0:T(8,128)S(1)}) fusion(bf16[1,1024,1024]{2,1,0:T(8,128)(2,1)S(1)} %copy-done.4, bf16[32,1024]{1,0:T(8,128)(2,1)S(1)} %collective-permute-done), kind=kOutput, calls=%fused_computation.33 | convolution fusion | flops 33570816 | bytes 2228224 | tf_op jit(solution)/shard_map/dot_general | solution.py:189
  9.5 0.1 collective-permute-start.1
  9.5 0.0 copy-done.6
  9.6 0.1 convert_subtract_fusion.partner_ref
  9.6 0.0 copy-done.2
  9.6 0.0 copy-done.3
  9.6 0.1 shard_map.65.factors_ref
  9.7 0.0 copy-done.1
  9.8 0.9 %shard_map.66 = bf16[16,1024]{1,0:T(8,128)(2,1)S(1)} custom-call(s32[1]{0:T(128)} %bitcast.base_ref, f32[16,1024]{1,0:T(8,128)S(1)} %bitcast.43, f32[16,1024]{1,0:T(8,128)S(1)} %convert_subtract_fusion.partner_ref, f32[8,1024]{1,0:T(8,128)S(1)} %shard_map.65.factors_ref), custom_call_target="tpu_custom_call" | custom-call | flops 3276800 | bytes 196608 | tf_op jit(solution)/shard_map/pallas_call | solution.py:108
  10.7 0.9 %shard_map.67 = bf16[16,1024]{1,0:T(8,128)(2,1)S(1)} custom-call(s32[1]{0:T(128)} %bitcast.base_ref, f32[16,1024]{1,0:T(8,128)S(1)} %get-tuple-element.17.forward_ref, f32[16,1024]{1,0:T(8,128)S(1)} %get-tuple-element.15.partner_ref, f32[8,1024]{1,0:T(8,128)S(1)} %shard_map.65.factors_ref), custom_call_target="tpu_custom_call" | custom-call | flops 3276800 | bytes 196608 | tf_op jit(solution)/shard_map/pallas_call | solution.py:108
  11.6 4.0 %collective-permute-done.1 = bf16[32,1024]{1,0:T(8,128)(2,1)S(1)} collective-permute-done((bf16[32,1024]{1,0:T(8,128)(2,1)S(1)}, bf16[32,1024]{1,0:T(8,128)(2,1)S(1)}, u32[]{:S(2)}, u32[]{:S(2)}) %collective-permute-start.1) | collective-permute-done | bytes 65568 | tf_op jit(solution)/shard_map/ppermute | solution.py:188
  15.6 0.4 %fusion.24 = (bf16[16,1024]{1,0:T(8,128)(2,1)S(1)}, f32[16,1024]{1,0:T(8,128)S(1)}) fusion(bf16[1,1024,1024]{2,1,0:T(8,128)(2,1)S(1)} %copy-done, bf16[32,1024]{1,0:T(8,128)(2,1)S(1)} %collective-permute-done.1), kind=kOutput, calls=%fused_computation.34 | convolution fusion | flops 33570816 | bytes 2228224 | tf_op jit(solution)/shard_map/dot_general | solution.py:192
  16.0 0.7 %fusion.25 = (bf16[16,1024]{1,0:T(8,128)(2,1)S(1)}, f32[16,1024]{1,0:T(8,128)S(1)}) fusion(bf16[1,1024,1024]{2,1,0:T(8,128)(2,1)S(1)} %copy-done.4, bf16[32,1024]{1,0:T(8,128)(2,1)S(1)} %collective-permute-done.1), kind=kOutput, calls=%fused_computation.35 | convolution fusion | flops 33570816 | bytes 2228224 | tf_op jit(solution)/shard_map/dot_general | solution.py:189
  16.7 0.1 collective-permute-start.2
  16.7 0.0 copy-start.5
  16.8 0.9 %shard_map.68 = bf16[16,1024]{1,0:T(8,128)(2,1)S(1)} custom-call(s32[1]{0:T(128)} %bitcast.base_ref, f32[16,1024]{1,0:T(8,128)S(1)} %get-tuple-element.21.forward_ref, f32[16,1024]{1,0:T(8,128)S(1)} %get-tuple-element.19.partner_ref, f32[8,1024]{1,0:T(8,128)S(1)} %shard_map.65.factors_ref), custom_call_target="tpu_custom_call" | custom-call | flops 3276800 | bytes 196608 | tf_op jit(solution)/shard_map/pallas_call | solution.py:108
  17.7 5.1 %collective-permute-done.2 = bf16[32,1024]{1,0:T(8,128)(2,1)S(1)} collective-permute-done((bf16[32,1024]{1,0:T(8,128)(2,1)S(1)}, bf16[32,1024]{1,0:T(8,128)(2,1)S(1)}, u32[]{:S(2)}, u32[]{:S(2)}) %collective-permute-start.2) | collective-permute-done | bytes 65568 | tf_op jit(solution)/shard_map/ppermute | solution.py:188
  22.8 0.4 %fusion.partner_ref = f32[16,1024]{1,0:T(8,128)S(1)} fusion(bf16[1,1024,1024]{2,1,0:T(8,128)(2,1)S(1)} %copy-done, bf16[32,1024]{1,0:T(8,128)(2,1)S(1)} %collective-permute-done.2), kind=kOutput, calls=%fused_computation | convolution fusion | flops 33554432 | bytes 2195456 | tf_op jit(solution)/shard_map/dot_general | solution.py:192
  23.2 0.0 copy-done.5
  23.2 0.7 %fusion.6.forward_ref = f32[16,1024]{1,0:T(8,128)S(1)} fusion(bf16[1,1024,1024]{2,1,0:T(8,128)(2,1)S(1)} %copy-done.5, bf16[32,1024]{1,0:T(8,128)(2,1)S(1)} %collective-permute-done.2), kind=kOutput, calls=%fused_computation.6 | convolution fusion | flops 33554432 | bytes 2195456 | tf_op jit(solution)/shard_map/dot_general | solution.py:189
  23.8 0.9 %shard_map.69 = bf16[16,1024]{1,0:T(8,128)(2,1)S(1)} custom-call(s32[1]{0:T(128)} %bitcast.base_ref, f32[16,1024]{1,0:T(8,128)S(1)} %fusion.6.forward_ref, f32[16,1024]{1,0:T(8,128)S(1)} %fusion.partner_ref, f32[8,1024]{1,0:T(8,128)S(1)} %shard_map.65.factors_ref), custom_call_target="tpu_custom_call" | custom-call | flops 3276800 | bytes 196608 | tf_op jit(solution)/shard_map/pallas_call | solution.py:108
  24.8 0.1 collective-permute-start.3
  24.9 0.6 %collective-permute-start.5 = (bf16[16,1024]{1,0:T(8,128)(2,1)S(1)}, bf16[16,1024]{1,0:T(8,128)(2,1)S(1)}, u32[]{:S(2)}, u32[]{:S(2)}) collective-permute-start(bf16[16,1024]{1,0:T(8,128)(2,1)S(1)} %get-tuple-element.12), channel_id=1, source_target_pairs={{0,12},{4,8},{8,4},{12,0},{1,13},{5,9},{9,5},{13,1},{2,14},{6,10},... | collective-permute-start | bytes 98312 | tf_op jit(solution)/shard_map/ppermute | solution.py:200
  25.4 2.9 %collective-permute-start.4 = (bf16[16,1024]{1,0:T(8,128)(2,1)S(1)}, bf16[16,1024]{1,0:T(8,128)(2,1)S(1)}, u32[]{:S(2)}, u32[]{:S(2)}) collective-permute-start(bf16[16,1024]{1,0:T(8,128)(2,1)S(1)} %get-tuple-element.13), channel_id=1, source_target_pairs={{0,4},{4,0},{8,12},{12,8},{1,5},{5,1},{9,13},{13,9},{2,6},{6,2},{1... | collective-permute-start | bytes 98312 | tf_op jit(solution)/shard_map/ppermute | solution.py:200
  28.3 1.3 %collective-permute-done.3 = bf16[16,1024]{1,0:T(8,128)(2,1)S(1)} collective-permute-done((bf16[16,1024]{1,0:T(8,128)(2,1)S(1)}, bf16[16,1024]{1,0:T(8,128)(2,1)S(1)}, u32[]{:S(2)}, u32[]{:S(2)}) %collective-permute-start.3) | collective-permute-done | bytes 32800 | tf_op jit(solution)/shard_map/ppermute | solution.py:200
  29.7 1.0 %collective-permute-done.5 = bf16[16,1024]{1,0:T(8,128)(2,1)S(1)} collective-permute-done((bf16[16,1024]{1,0:T(8,128)(2,1)S(1)}, bf16[16,1024]{1,0:T(8,128)(2,1)S(1)}, u32[]{:S(2)}, u32[]{:S(2)}) %collective-permute-start.5) | collective-permute-done | bytes 32800 | tf_op jit(solution)/shard_map/ppermute | solution.py:200
  30.6 0.0 collective-permute-done.4
  30.6 0.7 %fusion.15 = f32[1,16,1024]{2,1,0:T(8,128)} fusion(bf16[16,1024]{1,0:T(8,128)(2,1)S(1)} %collective-permute-done.5, bf16[16,1024]{1,0:T(8,128)(2,1)S(1)} %collective-permute-done.4, bf16[16,1024]{1,0:T(8,128)(2,1)S(1)} %collective-permute-done.3, bf16[4,16,1024]{2,1,0:T(8,128)(2,1)S(1)} %pad_maximum_fusion, s32[]{:T(128)S(6)} %select_n.13), kind=kLoop, calls=%fused_computation.19 | loop fusion | flops 131072 | bytes 196612 | tf_op jit(solution)/shard_map/broadcast_in_dim | solution.py:202
  (5 shorter events, 0.1 us)
Async XLA Ops:
  0.0 8.4 %copy-start = (bf16[1,1024,1024]{2,1,0:T(8,128)(2,1)S(1)}, bf16[1,1024,1024]{2,1,0:T(8,128)(2,1)}, u32[]{:S(2)}) copy-start(bf16[1,1024,1024]{2,1,0:T(8,128)(2,1)} %param.7) | copy-start | bytes 6291460
  0.0 8.8 %copy-start.4 = (bf16[1,1024,1024]{2,1,0:T(8,128)(2,1)S(1)}, bf16[1,1024,1024]{2,1,0:T(8,128)(2,1)}, u32[]{:S(2)}) copy-start(bf16[1,1024,1024]{2,1,0:T(8,128)(2,1)} %param.6) | copy-start | bytes 6291460
  1.1 7.3 %collective-permute-start = (bf16[32,1024]{1,0:T(8,128)(2,1)S(1)}, bf16[32,1024]{1,0:T(8,128)(2,1)S(1)}, u32[]{:S(2)}, u32[]{:S(2)}) collective-permute-start(bf16[32,1024]{1,0:T(8,128)(2,1)S(1)} %shard_map.64), channel_id=1, source_target_pairs={{0,4},{4,8},{8,12},{12,0},{1,5},{5,9},{9,13},{13,1},{2,6},{6,10},{... | collective-permute-start | bytes 196616 | tf_op jit(solution)/shard_map/ppermute | solution.py:188
  4.1 5.4 %copy-start.6 = (f32[1,16,1024]{2,1,0:T(8,128)S(1)}, f32[1,16,1024]{2,1,0:T(8,128)}, u32[]{:S(2)}) copy-start(f32[1,16,1024]{2,1,0:T(8,128)} %param.9) | copy-start | bytes 196612
  4.1 5.5 %copy-start.2 = (s32[1,2,1024]{2,1,0:T(2,128)S(1)}, s32[1,2,1024]{2,1,0:T(2,128)}, u32[]{:S(2)}) copy-start(s32[1,2,1024]{2,1,0:T(2,128)} %param.10) | copy-start | bytes 24580
  4.1 5.5 %copy-start.3 = (s32[2,1024]{1,0:T(2,128)S(1)}, s32[2,1024]{1,0:T(2,128)}, u32[]{:S(2)}) copy-start(s32[2,1024]{1,0:T(2,128)} %bonds_ref.1) | copy-start | bytes 24580
  4.2 5.6 %copy-start.1 = (f32[1,16,1024]{2,1,0:T(8,128)S(1)}, f32[1,16,1024]{2,1,0:T(8,128)}, u32[]{:S(2)}) copy-start(f32[1,16,1024]{2,1,0:T(8,128)} %param.8) | copy-start | bytes 196612
  9.5 6.1 %collective-permute-start.1 = (bf16[32,1024]{1,0:T(8,128)(2,1)S(1)}, bf16[32,1024]{1,0:T(8,128)(2,1)S(1)}, u32[]{:S(2)}, u32[]{:S(2)}) collective-permute-start(bf16[32,1024]{1,0:T(8,128)(2,1)S(1)} %pad_maximum_fusion.1), channel_id=1, source_target_pairs={{0,4},{4,8},{8,12},{12,0},{1,5},{5,9},{9,13},{13,1},{2,6},{6,10},{... | collective-permute-start | bytes 196616 | tf_op jit(solution)/shard_map/ppermute | solution.py:188
  16.7 6.1 %collective-permute-start.2 = (bf16[32,1024]{1,0:T(8,128)(2,1)S(1)}, bf16[32,1024]{1,0:T(8,128)(2,1)S(1)}, u32[]{:S(2)}, u32[]{:S(2)}) collective-permute-start(bf16[32,1024]{1,0:T(8,128)(2,1)S(1)} %pad_maximum_fusion.2), channel_id=1, source_target_pairs={{0,4},{4,8},{8,12},{12,0},{1,5},{5,9},{9,13},{13,1},{2,6},{6,10},{... | collective-permute-start | bytes 196616 | tf_op jit(solution)/shard_map/ppermute | solution.py:188
  16.7 6.4 %copy-start.5 = (bf16[1,1024,1024]{2,1,0:T(8,128)(2,1)S(1)}, bf16[1,1024,1024]{2,1,0:T(8,128)(2,1)}, u32[]{:S(2)}) copy-start(bf16[1,1024,1024]{2,1,0:T(8,128)(2,1)} %param.6) | copy-start | bytes 6291460
  24.8 4.9 %collective-permute-start.3 = (bf16[16,1024]{1,0:T(8,128)(2,1)S(1)}, bf16[16,1024]{1,0:T(8,128)(2,1)S(1)}, u32[]{:S(2)}, u32[]{:S(2)}) collective-permute-start(bf16[16,1024]{1,0:T(8,128)(2,1)S(1)} %get-tuple-element.11), channel_id=1, source_target_pairs={{0,8},{4,12},{8,0},{12,4},{1,9},{5,13},{9,1},{13,5},{2,10},{6,14},... | collective-permute-start | bytes 98312 | tf_op jit(solution)/shard_map/ppermute | solution.py:200
  24.9 5.8 %collective-permute-start.5 = (bf16[16,1024]{1,0:T(8,128)(2,1)S(1)}, bf16[16,1024]{1,0:T(8,128)(2,1)S(1)}, u32[]{:S(2)}, u32[]{:S(2)}) collective-permute-start(bf16[16,1024]{1,0:T(8,128)(2,1)S(1)} %get-tuple-element.12), channel_id=1, source_target_pairs={{0,12},{4,8},{8,4},{12,0},{1,13},{5,9},{9,5},{13,1},{2,14},{6,10},... | collective-permute-start | bytes 98312 | tf_op jit(solution)/shard_map/ppermute | solution.py:200
  25.4 5.2 %collective-permute-start.4 = (bf16[16,1024]{1,0:T(8,128)(2,1)S(1)}, bf16[16,1024]{1,0:T(8,128)(2,1)S(1)}, u32[]{:S(2)}, u32[]{:S(2)}) collective-permute-start(bf16[16,1024]{1,0:T(8,128)(2,1)S(1)} %get-tuple-element.13), channel_id=1, source_target_pairs={{0,4},{4,0},{8,12},{12,8},{1,5},{5,1},{9,13},{13,9},{2,6},{6,2},{1... | collective-permute-start | bytes 98312 | tf_op jit(solution)/shard_map/ppermute | solution.py:200

commit v4 on v3

--- a/solution.py
+++ b/solution.py
@@ -82,7 +82,8 @@
     )(field, bonds)
 
 
-def measure_kernel(side, base_ref, forward_ref, partner_ref, factors_ref, out_ref):
+def measure_kernel(side, base_ref, forward_ref, partner_ref, factors_ref, *rest):
+    out_ref = rest[-1]
     coefs = [split(factors_ref[k : k + 1, :]) for k in range(4)]
     wraps = (factors_ref.shape[0] - 4) // 2
     forward, partner = split(forward_ref[...]), split(partner_ref[...])
@@ -104,15 +105,15 @@
         out_ref[:, j * LANES : (j + 1) * LANES] = term.astype(out_ref.dtype)
 
 
-def measured(base, forward, partner, rates):
+def measured(base, forward, partner, rates, *kept):
     return pl.pallas_call(
         functools.partial(measure_kernel, math.isqrt(forward.shape[1])),
         out_shape=jax.ShapeDtypeStruct(forward.shape, jnp.bfloat16),
-        in_specs=[SMEM, VMEM, VMEM, VMEM],
+        in_specs=[SMEM, VMEM, VMEM, VMEM] + [ANY] * len(kept),
         out_specs=VMEM,
         compiler_params=params(),
         cost_estimate=cost(200 * forward.size, 12 * forward.size),
-    )(base, forward, partner, rates)
+    )(base, forward, partner, rates, *(pltpu.with_memory_space_constraint(k, pltpu.VMEM) for k in kept))
 
 
 def packed_kernel(base_ref, columns_ref, rows_ref, out_ref, columns, rows, arrived):
@@ -171,33 +172,47 @@
     clusters = lax.axis_size("tm")
     anchor = lax.axis_index("tm")
     ref_rows, sites = seed_columns.shape[1:]
-    first = lax.axis_index(("src", "col")) * ref_rows
-    base = first[None].astype(jnp.int32)
+    cores = lax.axis_size("col")
+    core = lax.axis_index("col")
+
+    def first_ref(displacement):
+        origin = (core - (displacement > anchor).astype(jnp.int32)) % cores
+        return (lax.axis_index("src") * cores + origin) * ref_rows
+
+    def route(targets):
+        return [
+            (k * cores + c, t * cores + (c + shift) % cores)
+            for k, (t, shift) in enumerate(targets)
+            for c in range(cores)
+        ]
+
+    around = route([((k + 1) % clusters, (k + 1) // clusters) for k in range(clusters)])
+    first = first_ref(0)
     same_site = jnp.arange(sites)[None, :] == (first + jnp.arange(ref_rows))[:, None]
-    around = [(i, (i + 1) % clusters) for i in range(clusters)]
-    forward_map, inverse_map = cluster_maps[0], inverse_maps[0]
+    forward_map, inverse_map = turned(cluster_maps[0]), inverse_maps[0]
     forward = seed_columns[0]
     partner = seed_rows[0] - same_site.astype(jnp.float32)
     rates = factors(ising_field[0], hop_bonds)
 
-    terms = [measured(base, forward, partner, rates)]
-    low = packed(base, seed_columns[0], seed_rows[0])
+    terms = [measured(first[None], forward, partner, rates)]
+    low = packed(first[None], seed_columns[0], seed_rows[0])
     for displacement in range(1, clusters):
         if displacement >= 3:
             low, *terms[: displacement - 1] = lax.optimization_barrier((low, *terms[: displacement - 1]))
-        low = lax.ppermute(low, "tm", around)
+        low = lax.ppermute(low, ("tm", "col"), around)
         forward = lax.dot_general(
-            low[:ref_rows], forward_map, (((1,), (1,)), ((), ())), preferred_element_type=jnp.float32
+            low[:ref_rows], forward_map, (((1,), (0,)), ((), ())), preferred_element_type=jnp.float32
         )
         partner = jnp.dot(low[ref_rows:], inverse_map, preferred_element_type=jnp.float32)
-        terms.append(measured(base, forward, partner, rates))
+        terms.append(measured(first_ref(displacement)[None], forward, partner, rates, *((forward_map,) if displacement == clusters - 2 else ())))
         low = jnp.concatenate([forward, partner]).astype(jnp.bfloat16)
     terms = jnp.stack(terms)
     total = None
     for step in (0, 2, 1, 3):
         term = lax.dynamic_index_in_dim(terms, anchor ^ step, 0, keepdims=False)
         if step:
-            term = lax.ppermute(term, "tm", [(i, i ^ step) for i in range(clusters)])
+            back = route([(k ^ step, -(k < k ^ step)) for k in range(clusters)])
+            term = lax.ppermute(term, ("tm", "col"), back)
         total = term.astype(jnp.float32) if total is None else total + term.astype(jnp.float32)
     return (total * (sites / clusters))[None]
 

time: 31.4 us -> 29.7 us (0.946)
  the two profiles are of different devices: /device:TPU:0 before, /device:TPU:3 now
where the time goes in v4:
time: 29.7 us; the launch traced here: 29.5 us
  waiting for transfers between devices  13 us (44%)
  Pallas kernels  5.38 us (18%)
  starting transfers between devices  4.46 us (15%)
  local copies, waits for them, and re-layouts  3.23 us (11%)
  matrix products  2.32 us (8%)
  other arithmetic  0.77 us (3%)
  between operations  0.31 us (1%)
    ppermute x3, waiting for transfers between devices, per_device(): low = lax.ppermute(low, ('tm', 'col'), around)  9.74 us
    pallas_call x4, Pallas kernels, measured(): pl.pallas_call(functools.partial(measure_kernel, math.isqrt(forward.shape...  3.6 us
    ppermute x3, waiting for transfers between devices, per_device(): term = lax.ppermute(term, ('tm', 'col'), back)  3.26 us
    unnamed x20, local copies, waits for them, and re-layouts  3.22 us
    ppermute x3, starting transfers between devices, per_device(): term = lax.ppermute(term, ('tm', 'col'), back)  2.97 us
    ppermute x3, starting transfers between devices, per_device(): low = lax.ppermute(low, ('tm', 'col'), around)  1.48 us
    dot_general x3, matrix products, per_device(): lax.dot_general(low[:ref_rows], forward_map, (((1,), (0,)), ((), ())), pr...  1.17 us
    dot_general x3, matrix products, per_device(): jnp.dot(low[ref_rows:], inverse_map, preferred_element_type=jnp.float32)  1.16 us
  transfers between devices with their start and end apart: 6, of which 6 were waited for; matrix products, arithmetic and copies ran while one was open for 0% of the time, Pallas kernels for 12%

profile of v4, /device:TPU:3, one launch (start us, length us, event | category | flops | bytes accessed | tf_op | source)
XLA Modules:
  0.0 29.5 jit_solution(14845535238048308399)
XLA Ops:
  0.0 0.0 copy-start
  0.0 1.0 %shard_map.64 = bf16[32,1024]{1,0:T(8,128)(2,1)S(1)} custom-call(s32[1]{0:T(128)} %bitcast.base_ref, f32[16,1024]{1,0:T(8,128)} %bitcast.39, f32[16,1024]{1,0:T(8,128)} %bitcast.46), custom_call_target="tpu_custom_call" | custom-call | flops 65536 | bytes 196608 | tf_op jit(solution)/shard_map/pallas_call | solution.py:137
  1.1 1.4 %collective-permute-start = (bf16[32,1024]{1,0:T(8,128)(2,1)S(1)}, bf16[32,1024]{1,0:T(8,128)(2,1)S(1)}, u32[]{:S(2)}, u32[]{:S(2)}) collective-permute-start(bf16[32,1024]{1,0:T(8,128)(2,1)S(1)} %shard_map.64), channel_id=1, source_target_pairs={{0,4},{1,5},{4,8},{5,9},{8,12},{9,13},{12,1},{13,0},{2,6},{3,7},{6... | collective-permute-start | bytes 196616 | tf_op jit(solution)/shard_map/ppermute | solution.py:202
  2.4 0.0 copy-start.5
  2.4 1.6 %copy-done.5 = bf16[1,1024,1024]{2,1,0:T(8,128)(2,1)S(1)} copy-done((bf16[1,1024,1024]{2,1,0:T(8,128)(2,1)S(1)}, bf16[1,1024,1024]{2,1,0:T(8,128)(2,1)}, u32[]{:S(2)}) %copy-start.5) | copy-done | bytes 2097176
  4.0 0.6 %shard_map.65.rest_0_ = bf16[1024,1024]{1,0:T(8,128)(2,1)S(1)} custom-call(bf16[1024,1024]{1,0:T(8,128)(2,1)S(1)} %bitcast.38), custom_call_target="tpu_custom_call" | custom-call | flops 1048576 | bytes 4194304 | tf_op jit(solution)/shard_map/pallas_call | solution.py:161
  4.6 0.0 copy-start.1
  4.7 0.0 copy-start.9
  4.7 0.0 copy-start.7
  4.7 0.0 copy-start.8
  4.7 0.0 copy-start.6
  4.7 2.6 %collective-permute-done = bf16[32,1024]{1,0:T(8,128)(2,1)S(1)} collective-permute-done((bf16[32,1024]{1,0:T(8,128)(2,1)S(1)}, bf16[32,1024]{1,0:T(8,128)(2,1)S(1)}, u32[]{:S(2)}, u32[]{:S(2)}) %collective-permute-start) | collective-permute-done | bytes 65568 | tf_op jit(solution)/shard_map/ppermute | solution.py:202
  7.3 0.0 copy-done
  7.3 0.4 %fusion.19 = (bf16[16,1024]{1,0:T(8,128)(2,1)S(1)}, f32[16,1024]{1,0:T(8,128)S(1)}) fusion(bf16[1,1024,1024]{2,1,0:T(8,128)(2,1)S(1)} %copy-done, bf16[32,1024]{1,0:T(8,128)(2,1)S(1)} %collective-permute-done), kind=kOutput, calls=%fused_computation.29 | convolution fusion | flops 33570816 | bytes 2228224 | tf_op jit(solution)/shard_map/dot_general | solution.py:206
  7.7 0.4 %fusion.20 = (bf16[16,1024]{1,0:T(8,128)(2,1)S(1)}, f32[16,1024]{1,0:T(8,128)S(1)}) fusion(bf16[1024,1024]{1,0:T(8,128)(2,1)S(1)} %shard_map.65.rest_0_, bf16[32,1024]{1,0:T(8,128)(2,1)S(1)} %collective-permute-done), kind=kOutput, calls=%fused_computation.30 | convolution fusion | flops 33570816 | bytes 2228224 | tf_op jit(solution)/shard_map/dot_general | solution.py:203
  8.1 0.0 copy-done.1
  8.1 0.1 collective-permute-start.1
  8.2 0.0 copy-done.9
  8.2 0.1 convert_subtract_fusion.partner_ref
  8.3 0.0 copy-done.7
  8.3 0.0 copy-done.8
  8.3 0.1 shard_map.66.factors_ref
  8.4 0.0 copy-done.6
  8.4 0.0 copy-start.2
  8.4 0.9 %shard_map.67 = bf16[16,1024]{1,0:T(8,128)(2,1)S(1)} custom-call(s32[1]{0:T(128)} %bitcast.base_ref, f32[16,1024]{1,0:T(8,128)S(1)} %bitcast.40, f32[16,1024]{1,0:T(8,128)S(1)} %convert_subtract_fusion.partner_ref, f32[8,1024]{1,0:T(8,128)S(1)} %shard_map.66.factors_ref), custom_call_target="tpu_custom_call" | custom-call | flops 3276800 | bytes 196608 | tf_op jit(solution)/shard_map/pallas_call | solution.py:109
  9.4 0.9 %shard_map.68 = bf16[16,1024]{1,0:T(8,128)(2,1)S(1)} custom-call(s32[1]{0:T(128)} %bitcast.6.base_ref, f32[16,1024]{1,0:T(8,128)S(1)} %get-tuple-element.17.forward_ref, f32[16,1024]{1,0:T(8,128)S(1)} %get-tuple-element.15.partner_ref, f32[8,1024]{1,0:T(8,128)S(1)} %shard_map.66.factors_ref), custom_call_target="tpu_custom_call" | custom-call | flops 3276800 | bytes 196608 | tf_op jit(solution)/shard_map/pallas_call | solution.py:109
  10.3 3.8 %collective-permute-done.1 = bf16[32,1024]{1,0:T(8,128)(2,1)S(1)} collective-permute-done((bf16[32,1024]{1,0:T(8,128)(2,1)S(1)}, bf16[32,1024]{1,0:T(8,128)(2,1)S(1)}, u32[]{:S(2)}, u32[]{:S(2)}) %collective-permute-start.1) | collective-permute-done | bytes 65568 | tf_op jit(solution)/shard_map/ppermute | solution.py:202
  14.1 0.4 %fusion.21 = (bf16[16,1024]{1,0:T(8,128)(2,1)S(1)}, f32[16,1024]{1,0:T(8,128)S(1)}) fusion(bf16[1,1024,1024]{2,1,0:T(8,128)(2,1)S(1)} %copy-done, bf16[32,1024]{1,0:T(8,128)(2,1)S(1)} %collective-permute-done.1), kind=kOutput, calls=%fused_computation.31 | convolution fusion | flops 33570816 | bytes 2228224 | tf_op jit(solution)/shard_map/dot_general | solution.py:206
  14.5 0.0 copy-done.2
  14.5 0.4 %fusion.22 = (bf16[16,1024]{1,0:T(8,128)(2,1)S(1)}, f32[16,1024]{1,0:T(8,128)S(1)}) fusion(bf16[1024,1024]{1,0:T(8,128)(2,1)S(1)} %copy-done.2, bf16[32,1024]{1,0:T(8,128)(2,1)S(1)} %collective-permute-done.1), kind=kOutput, calls=%fused_computation.32 | convolution fusion | flops 33570816 | bytes 2228224 | tf_op jit(solution)/shard_map/dot_general | solution.py:203
  14.9 0.1 collective-permute-start.2
  15.0 0.0 copy-start.3
  15.0 1.6 %copy-done.3 = bf16[1024,1024]{1,0:T(8,128)(2,1)S(1)} copy-done((bf16[1024,1024]{1,0:T(8,128)(2,1)S(1)}, bf16[1024,1024]{1,0:T(8,128)(2,1)}, u32[]{:S(2)}) %copy-start.3) | copy-done | bytes 2097176
  16.6 0.0 copy-start.4
  16.6 0.9 %shard_map.69 = bf16[16,1024]{1,0:T(8,128)(2,1)S(1)} custom-call(s32[1]{0:T(128)} %bitcast.9.base_ref, f32[16,1024]{1,0:T(8,128)S(1)} %get-tuple-element.21.forward_ref, f32[16,1024]{1,0:T(8,128)S(1)} %get-tuple-element.19.partner_ref, f32[8,1024]{1,0:T(8,128)S(1)} %shard_map.66.factors_ref, bf16[1024,1024]{1,0:T(8,128)(2,1)S(1)} %copy-done.3), custom_call_target="tpu_custom_call" | custom-call | flops 3276800 | bytes 196608 | tf_op jit(solution)/shard_map/pallas_call | solution.py:109
  17.5 3.3 %collective-permute-done.2 = bf16[32,1024]{1,0:T(8,128)(2,1)S(1)} collective-permute-done((bf16[32,1024]{1,0:T(8,128)(2,1)S(1)}, bf16[32,1024]{1,0:T(8,128)(2,1)S(1)}, u32[]{:S(2)}, u32[]{:S(2)}) %collective-permute-start.2) | collective-permute-done | bytes 65568 | tf_op jit(solution)/shard_map/ppermute | solution.py:202
  20.8 0.0 copy-done.4
  20.8 0.4 %fusion.11.forward_ref = f32[16,1024]{1,0:T(8,128)S(1)} fusion(bf16[1024,1024]{1,0:T(8,128)(2,1)S(1)} %copy-done.4, bf16[32,1024]{1,0:T(8,128)(2,1)S(1)} %collective-permute-done.2), kind=kOutput, calls=%fused_computation.17 | convolution fusion | flops 33554432 | bytes 2195456 | tf_op jit(solution)/shard_map/dot_general | solution.py:203
  21.2 0.4 %fusion.partner_ref = f32[16,1024]{1,0:T(8,128)S(1)} fusion(bf16[1,1024,1024]{2,1,0:T(8,128)(2,1)S(1)} %copy-done, bf16[32,1024]{1,0:T(8,128)(2,1)S(1)} %collective-permute-done.2), kind=kOutput, calls=%fused_computation | convolution fusion | flops 33554432 | bytes 2195456 | tf_op jit(solution)/shard_map/dot_general | solution.py:206
  21.6 0.9 %shard_map.70 = bf16[16,1024]{1,0:T(8,128)(2,1)S(1)} custom-call(s32[1]{0:T(128)} %bitcast.11.base_ref, f32[16,1024]{1,0:T(8,128)S(1)} %fusion.11.forward_ref, f32[16,1024]{1,0:T(8,128)S(1)} %fusion.partner_ref, f32[8,1024]{1,0:T(8,128)S(1)} %shard_map.66.factors_ref), custom_call_target="tpu_custom_call" | custom-call | flops 3276800 | bytes 196608 | tf_op jit(solution)/shard_map/pallas_call | solution.py:109
  22.6 0.1 collective-permute-start.3
  22.6 0.9 %collective-permute-start.5 = (bf16[16,1024]{1,0:T(8,128)(2,1)S(1)}, bf16[16,1024]{1,0:T(8,128)(2,1)S(1)}, u32[]{:S(2)}, u32[]{:S(2)}) collective-permute-start(bf16[16,1024]{1,0:T(8,128)(2,1)S(1)} %get-tuple-element.12), channel_id=1, source_target_pairs={{0,13},{1,12},{4,9},{5,8},{8,4},{9,5},{12,0},{13,1},{2,15},{3,14},... | collective-permute-start | bytes 98312 | tf_op jit(solution)/shard_map/ppermute | solution.py:215
  23.5 2.0 %collective-permute-start.4 = (bf16[16,1024]{1,0:T(8,128)(2,1)S(1)}, bf16[16,1024]{1,0:T(8,128)(2,1)S(1)}, u32[]{:S(2)}, u32[]{:S(2)}) collective-permute-start(bf16[16,1024]{1,0:T(8,128)(2,1)S(1)} %get-tuple-element.13), channel_id=1, source_target_pairs={{0,5},{1,4},{4,0},{5,1},{8,13},{9,12},{12,8},{13,9},{2,7},{3,6},{6... | collective-permute-start | bytes 98312 | tf_op jit(solution)/shard_map/ppermute | solution.py:215
  25.6 0.7 %collective-permute-done.3 = bf16[16,1024]{1,0:T(8,128)(2,1)S(1)} collective-permute-done((bf16[16,1024]{1,0:T(8,128)(2,1)S(1)}, bf16[16,1024]{1,0:T(8,128)(2,1)S(1)}, u32[]{:S(2)}, u32[]{:S(2)}) %collective-permute-start.3) | collective-permute-done | bytes 32800 | tf_op jit(solution)/shard_map/ppermute | solution.py:215
  26.3 1.2 %collective-permute-done.5 = bf16[16,1024]{1,0:T(8,128)(2,1)S(1)} collective-permute-done((bf16[16,1024]{1,0:T(8,128)(2,1)S(1)}, bf16[16,1024]{1,0:T(8,128)(2,1)S(1)}, u32[]{:S(2)}, u32[]{:S(2)}) %collective-permute-start.5) | collective-permute-done | bytes 32800 | tf_op jit(solution)/shard_map/ppermute | solution.py:215
  27.5 1.4 %collective-permute-done.4 = bf16[16,1024]{1,0:T(8,128)(2,1)S(1)} collective-permute-done((bf16[16,1024]{1,0:T(8,128)(2,1)S(1)}, bf16[16,1024]{1,0:T(8,128)(2,1)S(1)}, u32[]{:S(2)}, u32[]{:S(2)}) %collective-permute-start.4) | collective-permute-done | bytes 32800 | tf_op jit(solution)/shard_map/ppermute | solution.py:215
  28.8 0.7 %fusion.9 = f32[1,16,1024]{2,1,0:T(8,128)} fusion(bf16[16,1024]{1,0:T(8,128)(2,1)S(1)} %collective-permute-done.5, bf16[16,1024]{1,0:T(8,128)(2,1)S(1)} %collective-permute-done.4, bf16[16,1024]{1,0:T(8,128)(2,1)S(1)} %collective-permute-done.3, bf16[4,16,1024]{2,1,0:T(8,128)(2,1)S(1)} %pad_maximum_fusion, s32[]{:T(128)S(6)} %select_n.36), kind=kLoop, calls=%fused_computation.13 | loop fusion | flops 131072 | bytes 196612 | tf_op jit(solution)/shard_map/broadcast_in_dim | solution.py:217
  (5 shorter events, 0.1 us)
Async XLA Ops:
  0.0 7.3 %copy-start = (bf16[1,1024,1024]{2,1,0:T(8,128)(2,1)S(1)}, bf16[1,1024,1024]{2,1,0:T(8,128)(2,1)}, u32[]{:S(2)}) copy-start(bf16[1,1024,1024]{2,1,0:T(8,128)(2,1)} %param.7) | copy-start | bytes 6291460
  1.1 6.3 %collective-permute-start = (bf16[32,1024]{1,0:T(8,128)(2,1)S(1)}, bf16[32,1024]{1,0:T(8,128)(2,1)S(1)}, u32[]{:S(2)}, u32[]{:S(2)}) collective-permute-start(bf16[32,1024]{1,0:T(8,128)(2,1)S(1)} %shard_map.64), channel_id=1, source_target_pairs={{0,4},{1,5},{4,8},{5,9},{8,12},{9,13},{12,1},{13,0},{2,6},{3,7},{6... | collective-permute-start | bytes 196616 | tf_op jit(solution)/shard_map/ppermute | solution.py:202
  2.4 1.6 %copy-start.5 = (bf16[1,1024,1024]{2,1,0:T(8,128)(2,1)S(1)}, bf16[1,1024,1024]{2,1,0:T(8,128)(2,1)}, u32[]{:S(2)}) copy-start(bf16[1,1024,1024]{2,1,0:T(8,128)(2,1)} %param.6) | copy-start | bytes 6291460
  4.6 3.5 %copy-start.1 = (bf16[1024,1024]{1,0:T(8,128)(2,1)}, bf16[1024,1024]{1,0:T(8,128)(2,1)S(1)}, u32[]{:S(2)}) copy-start(bf16[1024,1024]{1,0:T(8,128)(2,1)S(1)} %shard_map.65.rest_0_) | copy-start | bytes 6291460
  4.7 3.5 %copy-start.9 = (f32[1,16,1024]{2,1,0:T(8,128)S(1)}, f32[1,16,1024]{2,1,0:T(8,128)}, u32[]{:S(2)}) copy-start(f32[1,16,1024]{2,1,0:T(8,128)} %param.9) | copy-start | bytes 196612
  4.7 3.6 %copy-start.7 = (s32[1,2,1024]{2,1,0:T(2,128)S(1)}, s32[1,2,1024]{2,1,0:T(2,128)}, u32[]{:S(2)}) copy-start(s32[1,2,1024]{2,1,0:T(2,128)} %param.10) | copy-start | bytes 24580
  4.7 3.6 %copy-start.8 = (s32[2,1024]{1,0:T(2,128)S(1)}, s32[2,1024]{1,0:T(2,128)}, u32[]{:S(2)}) copy-start(s32[2,1024]{1,0:T(2,128)} %bonds_ref.1) | copy-start | bytes 24580
  4.7 3.7 %copy-start.6 = (f32[1,16,1024]{2,1,0:T(8,128)S(1)}, f32[1,16,1024]{2,1,0:T(8,128)}, u32[]{:S(2)}) copy-start(f32[1,16,1024]{2,1,0:T(8,128)} %param.8) | copy-start | bytes 196612
  8.1 6.0 %collective-permute-start.1 = (bf16[32,1024]{1,0:T(8,128)(2,1)S(1)}, bf16[32,1024]{1,0:T(8,128)(2,1)S(1)}, u32[]{:S(2)}, u32[]{:S(2)}) collective-permute-start(bf16[32,1024]{1,0:T(8,128)(2,1)S(1)} %pad_maximum_fusion.1), channel_id=1, source_target_pairs={{0,4},{1,5},{4,8},{5,9},{8,12},{9,13},{12,1},{13,0},{2,6},{3,7},{6... | collective-permute-start | bytes 196616 | tf_op jit(solution)/shard_map/ppermute | solution.py:202
  8.4 6.0 %copy-start.2 = (bf16[1024,1024]{1,0:T(8,128)(2,1)S(1)}, bf16[1024,1024]{1,0:T(8,128)(2,1)}, u32[]{:S(2)}) copy-start(bf16[1024,1024]{1,0:T(8,128)(2,1)} %copy-done.1) | copy-start | bytes 6291460
  14.9 6.0 %collective-permute-start.2 = (bf16[32,1024]{1,0:T(8,128)(2,1)S(1)}, bf16[32,1024]{1,0:T(8,128)(2,1)S(1)}, u32[]{:S(2)}, u32[]{:S(2)}) collective-permute-start(bf16[32,1024]{1,0:T(8,128)(2,1)S(1)} %pad_maximum_fusion.2), channel_id=1, source_target_pairs={{0,4},{1,5},{4,8},{5,9},{8,12},{9,13},{12,1},{13,0},{2,6},{3,7},{6... | collective-permute-start | bytes 196616 | tf_op jit(solution)/shard_map/ppermute | solution.py:202
  15.0 1.6 %copy-start.3 = (bf16[1024,1024]{1,0:T(8,128)(2,1)S(1)}, bf16[1024,1024]{1,0:T(8,128)(2,1)}, u32[]{:S(2)}) copy-start(bf16[1024,1024]{1,0:T(8,128)(2,1)} %copy-done.1) | copy-start | bytes 6291460
  16.6 4.2 %copy-start.4 = (bf16[1024,1024]{1,0:T(8,128)(2,1)S(1)}, bf16[1024,1024]{1,0:T(8,128)(2,1)}, u32[]{:S(2)}) copy-start(bf16[1024,1024]{1,0:T(8,128)(2,1)} %copy-done.1) | copy-start | bytes 6291460
  22.6 3.7 %collective-permute-start.3 = (bf16[16,1024]{1,0:T(8,128)(2,1)S(1)}, bf16[16,1024]{1,0:T(8,128)(2,1)S(1)}, u32[]{:S(2)}, u32[]{:S(2)}) collective-permute-start(bf16[16,1024]{1,0:T(8,128)(2,1)S(1)} %get-tuple-element.11), channel_id=1, source_target_pairs={{0,9},{1,8},{4,13},{5,12},{8,0},{9,1},{12,4},{13,5},{2,11},{3,10},... | collective-permute-start | bytes 98312 | tf_op jit(solution)/shard_map/ppermute | solution.py:215
  22.6 4.8 %collective-permute-start.5 = (bf16[16,1024]{1,0:T(8,128)(2,1)S(1)}, bf16[16,1024]{1,0:T(8,128)(2,1)S(1)}, u32[]{:S(2)}, u32[]{:S(2)}) collective-permute-start(bf16[16,1024]{1,0:T(8,128)(2,1)S(1)} %get-tuple-element.12), channel_id=1, source_target_pairs={{0,13},{1,12},{4,9},{5,8},{8,4},{9,5},{12,0},{13,1},{2,15},{3,14},... | collective-permute-start | bytes 98312 | tf_op jit(solution)/shard_map/ppermute | solution.py:215
  23.5 5.3 %collective-permute-start.4 = (bf16[16,1024]{1,0:T(8,128)(2,1)S(1)}, bf16[16,1024]{1,0:T(8,128)(2,1)S(1)}, u32[]{:S(2)}, u32[]{:S(2)}) collective-permute-start(bf16[16,1024]{1,0:T(8,128)(2,1)S(1)} %get-tuple-element.13), channel_id=1, source_target_pairs={{0,5},{1,4},{4,0},{5,1},{8,13},{9,12},{12,8},{13,9},{2,7},{3,6},{6... | collective-permute-start | bytes 98312 | tf_op jit(solution)/shard_map/ppermute | solution.py:215

commit v5 on v4

--- a/solution.py
+++ b/solution.py
@@ -113,37 +113,35 @@
         out_specs=VMEM,
         compiler_params=params(),
         cost_estimate=cost(200 * forward.size, 12 * forward.size),
-    )(base, forward, partner, rates, *(pltpu.with_memory_space_constraint(k, pltpu.VMEM) for k in kept))
-
-
-def packed_kernel(base_ref, columns_ref, rows_ref, out_ref, columns, rows, arrived):
+    )(base, forward, partner, rates, *kept)
+
+
+def packed_kernel(base_ref, columns_ref, rows_ref, forward_low, partner_low, forward_ref, partner_ref, rows, arrived):
     copies = [
-        pltpu.make_async_copy(columns_ref, columns, arrived.at[0]),
+        pltpu.make_async_copy(columns_ref, forward_ref, arrived.at[0]),
         pltpu.make_async_copy(rows_ref, rows, arrived.at[1]),
     ]
     for copy in copies:
         copy.start()
     for copy in copies:
         copy.wait()
-    count = columns.shape[0]
     row = lax.broadcasted_iota(jnp.int32, rows.shape, 0) + base_ref[0]
     lane = lax.broadcasted_iota(jnp.int32, rows.shape, 1)
-    out_ref[0:count, :] = columns[...].astype(out_ref.dtype)
-    out_ref[count:, :] = jnp.where(lane == row, rows[...] - 1.0, rows[...]).astype(out_ref.dtype)
+    partner = jnp.where(lane == row, rows[...] - 1.0, rows[...])
+    partner_ref[...] = partner
+    partner_low[...] = partner.astype(partner_low.dtype)
+    forward_low[...] = forward_ref[...].astype(forward_low.dtype)
 
 
 def packed(base, columns, rows):
-    count, sites = columns.shape
+    low = jax.ShapeDtypeStruct(rows.shape, jnp.bfloat16)
+    full = jax.ShapeDtypeStruct(rows.shape, jnp.float32)
     return pl.pallas_call(
         packed_kernel,
-        out_shape=jax.ShapeDtypeStruct((2 * count, sites), jnp.bfloat16),
+        out_shape=(low, low, full, full),
         in_specs=[SMEM, ANY, ANY],
-        out_specs=VMEM,
-        scratch_shapes=[
-            pltpu.VMEM(columns.shape, columns.dtype),
-            pltpu.VMEM(rows.shape, rows.dtype),
-            pltpu.SemaphoreType.DMA((2,)),
-        ],
+        out_specs=(VMEM,) * 4,
+        scratch_shapes=[pltpu.VMEM(rows.shape, rows.dtype), pltpu.SemaphoreType.DMA((2,))],
         compiler_params=params(),
         cost_estimate=cost(4 * rows.size, 12 * rows.size),
     )(
@@ -153,19 +151,31 @@
     )
 
 
-def turned_kernel(map_ref, out_ref):
-    out_ref[...] = map_ref[...].T
+def turned_kernel(map_ref, out_ref, held, arrived):
+    rows = held.shape[1]
+    copies = [
+        pltpu.make_async_copy(map_ref.at[pl.ds(part * rows, rows)], held.at[part], arrived.at[part])
+        for part in range(held.shape[0])
+    ]
+    for copy in copies:
+        copy.start()
+    for part, copy in enumerate(copies):
+        copy.wait()
+        out_ref[:, part * rows : (part + 1) * rows] = held[part].T
 
 
 def turned(dense):
+    parts = 4
+    rows, columns = dense.shape[0] // parts, dense.shape[1]
     return pl.pallas_call(
         turned_kernel,
         out_shape=jax.ShapeDtypeStruct(dense.shape[::-1], dense.dtype),
-        in_specs=[VMEM],
+        in_specs=[ANY],
         out_specs=VMEM,
+        scratch_shapes=[pltpu.VMEM((parts, rows, columns), dense.dtype), pltpu.SemaphoreType.DMA((parts,))],
         compiler_params=params(8),
         cost_estimate=cost(dense.size, 4 * dense.size),
-    )(dense)
+    )(pltpu.with_memory_space_constraint(dense, pltpu.HBM))
 
 
 def per_device(cluster_maps, inverse_maps, seed_columns, seed_rows, ising_field, hop_bonds):
@@ -182,38 +192,52 @@
     def route(targets):
         return [
             (k * cores + c, t * cores + (c + shift) % cores)
-            for k, (t, shift) in enumerate(targets)
+            for k, (t, shift) in targets.items()
             for c in range(cores)
         ]
 
-    around = route([((k + 1) % clusters, (k + 1) // clusters) for k in range(clusters)])
-    first = first_ref(0)
-    same_site = jnp.arange(sites)[None, :] == (first + jnp.arange(ref_rows))[:, None]
+    around = route({k: ((k + 1) % clusters, (k + 1) // clusters) for k in range(clusters)})
     forward_map, inverse_map = turned(cluster_maps[0]), inverse_maps[0]
-    forward = seed_columns[0]
-    partner = seed_rows[0] - same_site.astype(jnp.float32)
     rates = factors(ising_field[0], hop_bonds)
-
-    terms = [measured(first[None], forward, partner, rates)]
-    low = packed(first[None], seed_columns[0], seed_rows[0])
+    first = first_ref(0)[None]
+    forward_low, partner_low, forward, partner = packed(first, seed_columns[0], seed_rows[0])
+    start = (forward, partner)
+
+    terms = []
     for displacement in range(1, clusters):
+        low = jnp.concatenate([forward_low, partner_low])
         if displacement >= 3:
             low, *terms[: displacement - 1] = lax.optimization_barrier((low, *terms[: displacement - 1]))
         low = lax.ppermute(low, ("tm", "col"), around)
-        forward = lax.dot_general(
-            low[:ref_rows], forward_map, (((1,), (0,)), ((), ())), preferred_element_type=jnp.float32
-        )
+        forward = jnp.dot(low[:ref_rows], forward_map, preferred_element_type=jnp.float32)
         partner = jnp.dot(low[ref_rows:], inverse_map, preferred_element_type=jnp.float32)
-        terms.append(measured(first_ref(displacement)[None], forward, partner, rates, *((forward_map,) if displacement == clusters - 2 else ())))
-        low = jnp.concatenate([forward, partner]).astype(jnp.bfloat16)
-    terms = jnp.stack(terms)
-    total = None
-    for step in (0, 2, 1, 3):
-        term = lax.dynamic_index_in_dim(terms, anchor ^ step, 0, keepdims=False)
-        if step:
-            back = route([(k ^ step, -(k < k ^ step)) for k in range(clusters)])
-            term = lax.ppermute(term, ("tm", "col"), back)
-        total = term.astype(jnp.float32) if total is None else total + term.astype(jnp.float32)
+        forward_low, partner_low = forward.astype(jnp.bfloat16), partner.astype(jnp.bfloat16)
+        if displacement == 1:
+            rates, *start = lax.optimization_barrier((rates, *start, forward_low))[:3]
+            terms.append(measured(first, *start, rates))
+        kept = (forward_map,) if displacement == clusters - 1 else ()
+        terms.append(measured(first_ref(displacement)[None], forward, partner, rates, *kept))
+    last = clusters - 1
+    *early, late = terms
+    early = jnp.stack(early)
+
+    def early_term(target):
+        return lax.dynamic_index_in_dim(early, jnp.minimum(target, last - 1), 0, keepdims=False)
+
+    def sent(term, targets):
+        return lax.ppermute(term, ("tm", "col"), route(targets))
+
+    def shifted(step):
+        return {k: ((k + step) % clusters, -(k < (k + step) % clusters)) for k in range(clusters)}
+
+    arrived = [sent(early_term((anchor + step) % clusters), shifted(step)) for step in range(clusters - 2, 0, -1)]
+    soon = sum(term.astype(jnp.float32) for term in arrived)
+
+    total = jnp.where(anchor == last, late, early_term(anchor)).astype(jnp.float32)
+    total = total + jnp.where(anchor == last, 0.0, soon)
+    total = total + sent(jnp.where(anchor == 0, late, early_term(anchor - 1)), shifted(-1)).astype(jnp.float32)
+    for k in range(last - 1, 0, -1):
+        total = total + sent(late, {k: (last, -1)}).astype(jnp.float32)
     return (total * (sites / clusters))[None]
 
 

time: 29.7 us -> 28 us (0.943)
  the two profiles are of different devices: /device:TPU:3 before, /device:TPU:31 now
where the time goes in v5:
time: 28 us; the launch traced here: 27.8 us
  starting transfers between devices  12.1 us (43%)
  Pallas kernels  6.63 us (24%)
  waiting for transfers between devices  5.73 us (20%)
  matrix products  2.33 us (8%)
  other arithmetic  0.72 us (3%)
  between operations  0.31 us (1%)
    ppermute x3, starting transfers between devices, per_device(): low = lax.ppermute(low, ('tm', 'col'), around)  7.84 us
    ppermute x5, waiting for transfers between devices, sent(): return lax.ppermute(term, ('tm', 'col'), route(targets))  5.03 us
    ppermute x5, starting transfers between devices, sent(): return lax.ppermute(term, ('tm', 'col'), route(targets))  4.24 us
    pallas_call x4, Pallas kernels, measured(): pl.pallas_call(functools.partial(measure_kernel, math.isqrt(forward.shape...  3.6 us
    pallas_call x1, Pallas kernels, turned(): pl.pallas_call(turned_kernel, out_shape=jax.ShapeDtypeStruct(dense.shape[...  1.89 us
    dot_general x3, matrix products, per_device(): jnp.dot(low[:ref_rows], forward_map, preferred_element_type=jnp.float32)  1.17 us
    dot_general x3, matrix products, per_device(): jnp.dot(low[ref_rows:], inverse_map, preferred_element_type=jnp.float32)  1.16 us
    pallas_call x1, Pallas kernels, packed(): pl.pallas_call(packed_kernel, out_shape=(low, low, full, full), in_specs=...  1.05 us
  transfers between devices with their start and end apart: 8, of which 4 were waited for; matrix products, arithmetic and copies ran while one was open for 3% of the time, Pallas kernels for 20%

profile of v5, /device:TPU:31, one launch (start us, length us, event | category | flops | bytes accessed | tf_op | source)
XLA Modules:
  0.0 27.8 jit_solution(17475061645683021379)
XLA Ops:
  0.0 0.0 copy-start
  0.0 1.1 %shard_map.64 = (bf16[16,1024]{1,0:T(8,128)(2,1)S(1)}, bf16[16,1024]{1,0:T(8,128)(2,1)S(1)}, f32[16,1024]{1,0:T(8,128)S(1)}, f32[16,1024]{1,0:T(8,128)S(1)}) custom-call(s32[1]{0:T(128)} %bitcast.1.base_ref, f32[16,1024]{1,0:T(8,128)} %bitcast.42, f32[16,1024]{1,0:T(8,128)} %bitcast.43), custom_call_target="tpu_custom_call" | custom-call | flops 65536 | bytes 196608 | tf_op jit(solution)/shard_map/pallas_call | solution.py:139
  1.1 0.6 %collective-permute-start = (bf16[32,1024]{1,0:T(8,128)(2,1)S(1)}, bf16[32,1024]{1,0:T(8,128)(2,1)S(1)}, u32[]{:S(2)}, u32[]{:S(2)}) collective-permute-start(bf16[32,1024]{1,0:T(8,128)(2,1)S(1)} %pad_maximum_fusion.1), channel_id=1, source_target_pairs={{0,4},{1,5},{4,8},{5,9},{8,12},{9,13},{12,1},{13,0},{2,6},{3,7},{6... | collective-permute-start | bytes 196616 | tf_op jit(solution)/shard_map/ppermute | solution.py:211
  1.6 1.9 %shard_map.65.rest_0_ = bf16[1024,1024]{1,0:T(8,128)(2,1)S(1)} custom-call(bf16[1024,1024]{1,0:T(8,128)(2,1)} %bitcast.41), custom_call_target="tpu_custom_call" | custom-call | flops 1048576 | bytes 4194304 | tf_op jit(solution)/shard_map/pallas_call | solution.py:170
  3.5 0.0 copy-start.1
  3.5 0.0 copy-start.3
  3.6 0.0 copy-start.4
  3.6 0.7 %collective-permute-done = bf16[32,1024]{1,0:T(8,128)(2,1)S(1)} collective-permute-done((bf16[32,1024]{1,0:T(8,128)(2,1)S(1)}, bf16[32,1024]{1,0:T(8,128)(2,1)S(1)}, u32[]{:S(2)}, u32[]{:S(2)}) %collective-permute-start) | collective-permute-done | bytes 65568 | tf_op jit(solution)/shard_map/ppermute | solution.py:211
  4.2 0.0 copy-done
  4.3 0.4 %fusion.15 = (bf16[16,1024]{1,0:T(8,128)(2,1)S(1)}, f32[16,1024]{1,0:T(8,128)S(1)}) fusion(bf16[1,1024,1024]{2,1,0:T(8,128)(2,1)S(1)} %copy-done, bf16[32,1024]{1,0:T(8,128)(2,1)S(1)} %collective-permute-done), kind=kOutput, calls=%fused_computation.24 | convolution fusion | flops 33570816 | bytes 2228224 | tf_op jit(solution)/shard_map/dot_general | solution.py:213
  4.6 0.4 %fusion.16 = (bf16[16,1024]{1,0:T(8,128)(2,1)S(1)}, f32[16,1024]{1,0:T(8,128)S(1)}) fusion(bf16[1024,1024]{1,0:T(8,128)(2,1)S(1)} %shard_map.65.rest_0_, bf16[32,1024]{1,0:T(8,128)(2,1)S(1)} %collective-permute-done), kind=kOutput, calls=%fused_computation.25 | convolution fusion | flops 33570816 | bytes 2228224 | tf_op jit(solution)/shard_map/dot_general | solution.py:212
  5.0 0.0 copy-done.1
  5.0 3.4 %collective-permute-start.1 = (bf16[32,1024]{1,0:T(8,128)(2,1)S(1)}, bf16[32,1024]{1,0:T(8,128)(2,1)S(1)}, u32[]{:S(2)}, u32[]{:S(2)}) collective-permute-start(bf16[32,1024]{1,0:T(8,128)(2,1)S(1)} %pad_maximum_fusion.2), channel_id=1, source_target_pairs={{0,4},{1,5},{4,8},{5,9},{8,12},{9,13},{12,1},{13,0},{2,6},{3,7},{6... | collective-permute-start | bytes 196616 | tf_op jit(solution)/shard_map/ppermute | solution.py:211
  8.4 0.0 copy-done.3
  8.4 0.0 copy-done.4
  8.4 0.1 shard_map.66.factors_ref
  8.6 0.0 copy-start.2
  8.6 0.9 %shard_map.67 = bf16[16,1024]{1,0:T(8,128)(2,1)S(1)} custom-call(s32[1]{0:T(128)} %bitcast.1.base_ref, f32[16,1024]{1,0:T(8,128)S(1)} %get-tuple-element.19.forward_ref, f32[16,1024]{1,0:T(8,128)S(1)} %get-tuple-element.20.partner_ref, f32[8,1024]{1,0:T(8,128)S(1)} %shard_map.66.factors_ref), custom_call_target="tpu_custom_call" | custom-call | flops 3276800 | bytes 196608 | tf_op jit(solution)/shard_map/pallas_call | solution.py:109
  9.5 0.9 %shard_map.68 = bf16[16,1024]{1,0:T(8,128)(2,1)S(1)} custom-call(s32[1]{0:T(128)} %bitcast.7.base_ref, f32[16,1024]{1,0:T(8,128)S(1)} %get-tuple-element.30.forward_ref, f32[16,1024]{1,0:T(8,128)S(1)} %get-tuple-element.28.partner_ref, f32[8,1024]{1,0:T(8,128)S(1)} %shard_map.66.factors_ref), custom_call_target="tpu_custom_call" | custom-call | flops 3276800 | bytes 196608 | tf_op jit(solution)/shard_map/pallas_call | solution.py:109
  10.5 0.0 collective-permute-done.1
  10.5 0.4 %fusion.17 = (bf16[16,1024]{1,0:T(8,128)(2,1)S(1)}, f32[16,1024]{1,0:T(8,128)S(1)}) fusion(bf16[1,1024,1024]{2,1,0:T(8,128)(2,1)S(1)} %copy-done, bf16[32,1024]{1,0:T(8,128)(2,1)S(1)} %collective-permute-done.1), kind=kOutput, calls=%fused_computation.26 | convolution fusion | flops 33570816 | bytes 2228224 | tf_op jit(solution)/shard_map/dot_general | solution.py:213
  10.9 0.0 copy-done.2
  10.9 0.4 %fusion.18 = (bf16[16,1024]{1,0:T(8,128)(2,1)S(1)}, f32[16,1024]{1,0:T(8,128)S(1)}) fusion(bf16[1024,1024]{1,0:T(8,128)(2,1)S(1)} %copy-done.2, bf16[32,1024]{1,0:T(8,128)(2,1)S(1)} %collective-permute-done.1), kind=kOutput, calls=%fused_computation.27 | convolution fusion | flops 33570816 | bytes 2228224 | tf_op jit(solution)/shard_map/dot_general | solution.py:212
  11.3 3.9 %collective-permute-start.2 = (bf16[32,1024]{1,0:T(8,128)(2,1)S(1)}, bf16[32,1024]{1,0:T(8,128)(2,1)S(1)}, u32[]{:S(2)}, u32[]{:S(2)}) collective-permute-start(bf16[32,1024]{1,0:T(8,128)(2,1)S(1)} %pad_maximum_fusion.3), channel_id=1, source_target_pairs={{0,4},{1,5},{4,8},{5,9},{8,12},{9,13},{12,1},{13,0},{2,6},{3,7},{6... | collective-permute-start | bytes 196616 | tf_op jit(solution)/shard_map/ppermute | solution.py:211
  15.2 0.9 %shard_map.70 = bf16[16,1024]{1,0:T(8,128)(2,1)S(1)} custom-call(s32[1]{0:T(128)} %bitcast.10.base_ref, f32[16,1024]{1,0:T(8,128)S(1)} %get-tuple-element.34.forward_ref, f32[16,1024]{1,0:T(8,128)S(1)} %get-tuple-element.32.partner_ref, f32[8,1024]{1,0:T(8,128)S(1)} %shard_map.66.factors_ref), custom_call_target="tpu_custom_call" | custom-call | flops 3276800 | bytes 196608 | tf_op jit(solution)/shard_map/pallas_call | solution.py:109
  16.1 0.1 collective-permute-start.3
  16.2 0.6 %collective-permute-start.4 = (bf16[16,1024]{1,0:T(8,128)(2,1)S(1)}, bf16[16,1024]{1,0:T(8,128)(2,1)S(1)}, u32[]{:S(2)}, u32[]{:S(2)}) collective-permute-start(bf16[16,1024]{1,0:T(8,128)(2,1)S(1)} %get-tuple-element.26), channel_id=1, source_target_pairs={{0,5},{1,4},{4,9},{5,8},{8,13},{9,12},{12,0},{13,1},{2,7},{3,6},{6... | collective-permute-start | bytes 98312 | tf_op jit(solution)/shard_map/ppermute | solution.py:228
  16.8 0.0 collective-permute-done.2
  16.8 0.4 %fusion.partner_ref = f32[16,1024]{1,0:T(8,128)S(1)} fusion(bf16[1,1024,1024]{2,1,0:T(8,128)(2,1)S(1)} %copy-done, bf16[32,1024]{1,0:T(8,128)(2,1)S(1)} %collective-permute-done.2), kind=kOutput, calls=%fused_computation | convolution fusion | flops 33554432 | bytes 2195456 | tf_op jit(solution)/shard_map/dot_general | solution.py:213
  17.2 0.4 %fusion.7.forward_ref = f32[16,1024]{1,0:T(8,128)S(1)} fusion(bf16[1024,1024]{1,0:T(8,128)(2,1)S(1)} %copy-done.2, bf16[32,1024]{1,0:T(8,128)(2,1)S(1)} %collective-permute-done.2), kind=kOutput, calls=%fused_computation.12 | convolution fusion | flops 33554432 | bytes 2195456 | tf_op jit(solution)/shard_map/dot_general | solution.py:212
  17.6 0.9 %shard_map.69 = bf16[16,1024]{1,0:T(8,128)(2,1)S(1)} custom-call(s32[1]{0:T(128)} %bitcast.base_ref, f32[16,1024]{1,0:T(8,128)S(1)} %fusion.7.forward_ref, f32[16,1024]{1,0:T(8,128)S(1)} %fusion.partner_ref, f32[8,1024]{1,0:T(8,128)S(1)} %shard_map.66.factors_ref, bf16[1024,1024]{1,0:T(8,128)(2,1)S(1)} %copy-done.2), custom_call_target="tpu_custom_call" | custom-call | flops 3276800 | bytes 196608 | tf_op jit(solution)/shard_map/pallas_call | solution.py:109
  18.5 1.0 %collective-permute-start.5 = (bf16[16,1024]{1,0:T(8,128)(2,1)S(1)}, bf16[16,1024]{1,0:T(8,128)(2,1)S(1)}, u32[]{:S(2)}, u32[]{:S(2)}) collective-permute-start(bf16[16,1024]{1,0:T(8,128)(2,1)S(1)} %bitcast_select_fusion), channel_id=1, source_target_pairs={{0,13},{1,12},{4,0},{5,1},{8,4},{9,5},{12,8},{13,9},{2,15},{3,14},... | collective-permute-start | bytes 98312 | tf_op jit(solution)/shard_map/ppermute | solution.py:228
  19.5 1.3 %collective-permute-start.7 = (bf16[16,1024]{1,0:T(8,128)(2,1)S(1)}, bf16[16,1024]{1,0:T(8,128)(2,1)S(1)}, u32[]{:S(2)}, u32[]{:S(2)}) collective-permute-start(bf16[16,1024]{1,0:T(8,128)(2,1)S(1)} %shard_map.69), channel_id=1, source_target_pairs={{4,13},{5,12},{6,15},{7,14},{20,29},{21,28},{22,31},{23,30}} | collective-permute-start | bytes 98312 | tf_op jit(solution)/shard_map/ppermute | solution.py:228
  20.8 1.3 %collective-permute-start.6 = (bf16[16,1024]{1,0:T(8,128)(2,1)S(1)}, bf16[16,1024]{1,0:T(8,128)(2,1)S(1)}, u32[]{:S(2)}, u32[]{:S(2)}) collective-permute-start(bf16[16,1024]{1,0:T(8,128)(2,1)S(1)} %shard_map.69), channel_id=1, source_target_pairs={{8,13},{9,12},{10,15},{11,14},{24,29},{25,28},{26,31},{27,30}} | collective-permute-start | bytes 98312 | tf_op jit(solution)/shard_map/ppermute | solution.py:228
  22.1 0.0 collective-permute-done.3
  22.1 0.0 collective-permute-done.4
  22.1 2.5 %collective-permute-done.5 = bf16[16,1024]{1,0:T(8,128)(2,1)S(1)} collective-permute-done((bf16[16,1024]{1,0:T(8,128)(2,1)S(1)}, bf16[16,1024]{1,0:T(8,128)(2,1)S(1)}, u32[]{:S(2)}, u32[]{:S(2)}) %collective-permute-start.5) | collective-permute-done | bytes 32800 | tf_op jit(solution)/shard_map/ppermute | solution.py:228
  24.6 1.8 %collective-permute-done.7 = bf16[16,1024]{1,0:T(8,128)(2,1)S(1)} collective-permute-done((bf16[16,1024]{1,0:T(8,128)(2,1)S(1)}, bf16[16,1024]{1,0:T(8,128)(2,1)S(1)}, u32[]{:S(2)}, u32[]{:S(2)}) %collective-permute-start.7) | collective-permute-done | bytes 32800 | tf_op jit(solution)/shard_map/ppermute | solution.py:228
  26.4 0.8 %collective-permute-done.6 = bf16[16,1024]{1,0:T(8,128)(2,1)S(1)} collective-permute-done((bf16[16,1024]{1,0:T(8,128)(2,1)S(1)}, bf16[16,1024]{1,0:T(8,128)(2,1)S(1)}, u32[]{:S(2)}, u32[]{:S(2)}) %collective-permute-start.6) | collective-permute-done | bytes 32800 | tf_op jit(solution)/shard_map/ppermute | solution.py:228
  27.2 0.7 %multiply_bitcast_fusion = f32[1,16,1024]{2,1,0:T(8,128)} fusion(bf16[16,1024]{1,0:T(8,128)(2,1)S(1)} %collective-permute-done.7, bf16[16,1024]{1,0:T(8,128)(2,1)S(1)} %collective-permute-done.6, bf16[16,1024]{1,0:T(8,128)(2,1)S(1)} %collective-permute-done.5, bf16[16,1024]{1,0:T(8,128)(2,1)S(1)} %collective-permute-done.4, ...), kind=kLoop, calls=%fused_computation.10 | loop fusion | flops 229376 | bytes 294917 | tf_op jit(solution)/shard_map/broadcast_in_dim | solution.py:241
  (6 shorter events, 0.1 us)
Async XLA Ops:
  0.0 4.3 %copy-start = (bf16[1,1024,1024]{2,1,0:T(8,128)(2,1)S(1)}, bf16[1,1024,1024]{2,1,0:T(8,128)(2,1)}, u32[]{:S(2)}) copy-start(bf16[1,1024,1024]{2,1,0:T(8,128)(2,1)} %param.7) | copy-start | bytes 6291460
  1.1 3.2 %collective-permute-start = (bf16[32,1024]{1,0:T(8,128)(2,1)S(1)}, bf16[32,1024]{1,0:T(8,128)(2,1)S(1)}, u32[]{:S(2)}, u32[]{:S(2)}) collective-permute-start(bf16[32,1024]{1,0:T(8,128)(2,1)S(1)} %pad_maximum_fusion.1), channel_id=1, source_target_pairs={{0,4},{1,5},{4,8},{5,9},{8,12},{9,13},{12,1},{13,0},{2,6},{3,7},{6... | collective-permute-start | bytes 196616 | tf_op jit(solution)/shard_map/ppermute | solution.py:211
  3.5 1.5 %copy-start.1 = (bf16[1024,1024]{1,0:T(8,128)(2,1)}, bf16[1024,1024]{1,0:T(8,128)(2,1)S(1)}, u32[]{:S(2)}) copy-start(bf16[1024,1024]{1,0:T(8,128)(2,1)S(1)} %shard_map.65.rest_0_) | copy-start | bytes 6291460
  3.5 4.9 %copy-start.3 = (s32[1,2,1024]{2,1,0:T(2,128)S(1)}, s32[1,2,1024]{2,1,0:T(2,128)}, u32[]{:S(2)}) copy-start(s32[1,2,1024]{2,1,0:T(2,128)} %param.10) | copy-start | bytes 24580
  3.6 4.9 %copy-start.4 = (s32[2,1024]{1,0:T(2,128)S(1)}, s32[2,1024]{1,0:T(2,128)}, u32[]{:S(2)}) copy-start(s32[2,1024]{1,0:T(2,128)} %bonds_ref.1) | copy-start | bytes 24580
  5.0 5.4 %collective-permute-start.1 = (bf16[32,1024]{1,0:T(8,128)(2,1)S(1)}, bf16[32,1024]{1,0:T(8,128)(2,1)S(1)}, u32[]{:S(2)}, u32[]{:S(2)}) collective-permute-start(bf16[32,1024]{1,0:T(8,128)(2,1)S(1)} %pad_maximum_fusion.2), channel_id=1, source_target_pairs={{0,4},{1,5},{4,8},{5,9},{8,12},{9,13},{12,1},{13,0},{2,6},{3,7},{6... | collective-permute-start | bytes 196616 | tf_op jit(solution)/shard_map/ppermute | solution.py:211
  8.6 2.2 %copy-start.2 = (bf16[1024,1024]{1,0:T(8,128)(2,1)S(1)}, bf16[1024,1024]{1,0:T(8,128)(2,1)}, u32[]{:S(2)}) copy-start(bf16[1024,1024]{1,0:T(8,128)(2,1)} %copy-done.1) | copy-start | bytes 6291460
  11.3 5.5 %collective-permute-start.2 = (bf16[32,1024]{1,0:T(8,128)(2,1)S(1)}, bf16[32,1024]{1,0:T(8,128)(2,1)S(1)}, u32[]{:S(2)}, u32[]{:S(2)}) collective-permute-start(bf16[32,1024]{1,0:T(8,128)(2,1)S(1)} %pad_maximum_fusion.3), channel_id=1, source_target_pairs={{0,4},{1,5},{4,8},{5,9},{8,12},{9,13},{12,1},{13,0},{2,6},{3,7},{6... | collective-permute-start | bytes 196616 | tf_op jit(solution)/shard_map/ppermute | solution.py:211
  16.1 6.0 %collective-permute-start.3 = (bf16[16,1024]{1,0:T(8,128)(2,1)S(1)}, bf16[16,1024]{1,0:T(8,128)(2,1)S(1)}, u32[]{:S(2)}, u32[]{:S(2)}) collective-permute-start(bf16[16,1024]{1,0:T(8,128)(2,1)S(1)} %get-tuple-element.25), channel_id=1, source_target_pairs={{0,9},{1,8},{4,13},{5,12},{8,0},{9,1},{12,4},{13,5},{2,11},{3,10},... | collective-permute-start | bytes 98312 | tf_op jit(solution)/shard_map/ppermute | solution.py:228
  16.2 5.9 %collective-permute-start.4 = (bf16[16,1024]{1,0:T(8,128)(2,1)S(1)}, bf16[16,1024]{1,0:T(8,128)(2,1)S(1)}, u32[]{:S(2)}, u32[]{:S(2)}) collective-permute-start(bf16[16,1024]{1,0:T(8,128)(2,1)S(1)} %get-tuple-element.26), channel_id=1, source_target_pairs={{0,5},{1,4},{4,9},{5,8},{8,13},{9,12},{12,0},{13,1},{2,7},{3,6},{6... | collective-permute-start | bytes 98312 | tf_op jit(solution)/shard_map/ppermute | solution.py:228
  18.5 6.1 %collective-permute-start.5 = (bf16[16,1024]{1,0:T(8,128)(2,1)S(1)}, bf16[16,1024]{1,0:T(8,128)(2,1)S(1)}, u32[]{:S(2)}, u32[]{:S(2)}) collective-permute-start(bf16[16,1024]{1,0:T(8,128)(2,1)S(1)} %bitcast_select_fusion), channel_id=1, source_target_pairs={{0,13},{1,12},{4,0},{5,1},{8,4},{9,5},{12,8},{13,9},{2,15},{3,14},... | collective-permute-start | bytes 98312 | tf_op jit(solution)/shard_map/ppermute | solution.py:228
  19.5 6.9 %collective-permute-start.7 = (bf16[16,1024]{1,0:T(8,128)(2,1)S(1)}, bf16[16,1024]{1,0:T(8,128)(2,1)S(1)}, u32[]{:S(2)}, u32[]{:S(2)}) collective-permute-start(bf16[16,1024]{1,0:T(8,128)(2,1)S(1)} %shard_map.69), channel_id=1, source_target_pairs={{4,13},{5,12},{6,15},{7,14},{20,29},{21,28},{22,31},{23,30}} | collective-permute-start | bytes 98312 | tf_op jit(solution)/shard_map/ppermute | solution.py:228
  20.8 6.4 %collective-permute-start.6 = (bf16[16,1024]{1,0:T(8,128)(2,1)S(1)}, bf16[16,1024]{1,0:T(8,128)(2,1)S(1)}, u32[]{:S(2)}, u32[]{:S(2)}) collective-permute-start(bf16[16,1024]{1,0:T(8,128)(2,1)S(1)} %shard_map.69), channel_id=1, source_target_pairs={{8,13},{9,12},{10,15},{11,14},{24,29},{25,28},{26,31},{27,30}} | collective-permute-start | bytes 98312 | tf_op jit(solution)/shard_map/ppermute | solution.py:228

commit v6 on v5

--- a/solution.py
+++ b/solution.py
@@ -12,6 +12,7 @@
 field_coupling = math.log(math.exp(0.5) + math.sqrt(math.exp(1.0) - 1.0))
 
 LANES = 128
+SUBLANES = 8
 VMEM = pl.BlockSpec(memory_space=pltpu.VMEM)
 SMEM = pl.BlockSpec(memory_space=pltpu.SMEM)
 ANY = pl.BlockSpec(memory_space=pl.ANY)
@@ -33,22 +34,28 @@
     return [values[:, j : j + LANES] for j in range(0, values.shape[1], LANES)]
 
 
-def hops(blocks, side, coefs):
-    count = len(blocks)
-    lane = lax.broadcasted_iota(jnp.int32, blocks[0].shape, 1)
-    column = lane % side
-    ahead = rolled(blocks, -side)
-    behind = rolled(blocks, side)
-    right, right_wrap = rolled(blocks, -1), rolled(blocks, side - 1)
-    left, left_wrap = rolled(blocks, 1), rolled(blocks, 1 - side)
+def leads(blocks, side):
+    return rolled(blocks, -side), rolled(blocks, side)
+
+
+def beside(blocks, rows, side):
+    column = lax.broadcasted_iota(jnp.int32, blocks[0].shape, 1) % side
+    ahead, behind = rows
+    right = [jnp.where(column == 0, q, u) for q, u in zip(behind, blocks)]
+    left = [jnp.where(column == side - 1, q, u) for q, u in zip(ahead, blocks)]
+    return rolled(right, -1), rolled(left, 1)
+
+
+def hops(rows, columns, side, coefs):
+    (ahead, behind), (right, left) = rows, columns
+    count = len(ahead)
+    lane = lax.broadcasted_iota(jnp.int32, ahead[0].shape, 1)
     out = []
     for j in range(count):
         row_ahead = jnp.where(lane < LANES - side, ahead[j], ahead[(j + 1) % count])
         row_behind = jnp.where(lane >= side, behind[j], behind[j - 1])
-        column_ahead = jnp.where(column == side - 1, right_wrap[j], right[j])
-        column_behind = jnp.where(column == 0, left_wrap[j], left[j])
         up, down, forth, back = [c[j] for c in coefs]
-        out.append((up * row_ahead + down * row_behind) + (forth * column_ahead + back * column_behind))
+        out.append((up * row_ahead + down * row_behind) + (forth * right[j] + back * left[j]))
     return out
 
 
@@ -82,38 +89,44 @@
     )(field, bonds)
 
 
-def measure_kernel(side, base_ref, forward_ref, partner_ref, factors_ref, *rest):
-    out_ref = rest[-1]
+def measure_kernel(side, base_ref, forward_ref, partner_ref, factors_ref, out_ref):
+    total = forward_ref.shape[0]
+    count = SUBLANES if total % SUBLANES == 0 else total
+    wraps = (factors_ref.shape[0] - 4) // 2
     coefs = [split(factors_ref[k : k + 1, :]) for k in range(4)]
-    wraps = (factors_ref.shape[0] - 4) // 2
-    forward, partner = split(forward_ref[...]), split(partner_ref[...])
+    halves = [[0.5 * c for c in blocks] for blocks in coefs]
+    groups = range(0, total, count)
+    chains = [(ref, row, sign, place) for row in groups for ref, sign, place in ((forward_ref, 1.0, 4), (partner_ref, -1.0, 4 + wraps))]
+    values = [split(ref[row : row + count, :]) for ref, row, _, _ in chains]
     for wrap in range(wraps):
-        scale_up = split(factors_ref[4 + wrap : 5 + wrap, :])
-        scale_down = split(factors_ref[4 + wraps + wrap : 5 + wraps + wrap, :])
-        forward = [u * s for u, s in zip(forward, scale_up)]
-        partner = [u * s for u, s in zip(partner, scale_down)]
-        hop_forward, hop_partner = hops(forward, side, coefs), hops(partner, side, coefs)
-        half_forward = [u + 0.5 * h for u, h in zip(forward, hop_forward)]
-        half_partner = [u - 0.5 * h for u, h in zip(partner, hop_partner)]
-        hop_forward, hop_partner = hops(half_forward, side, coefs), hops(half_partner, side, coefs)
-        forward = [u + h for u, h in zip(forward, hop_forward)]
-        partner = [u - h for u, h in zip(partner, hop_partner)]
-    row = lax.broadcasted_iota(jnp.int32, forward[0].shape, 0) + base_ref[0]
-    lane = lax.broadcasted_iota(jnp.int32, forward[0].shape, 1)
-    for j, (f, p) in enumerate(zip(forward, partner)):
-        term = jnp.where(lane + j * LANES == row, 0.0, f * p)
-        out_ref[:, j * LANES : (j + 1) * LANES] = term.astype(out_ref.dtype)
-
-
-def measured(base, forward, partner, rates, *kept):
+        scales = {place: split(factors_ref[place + wrap : place + wrap + 1, :]) for place in (4, 4 + wraps)}
+        values = [[u * s for u, s in zip(v, scales[place])] for v, (_, _, _, place) in zip(values, chains)]
+        inner = values
+        for weights in (halves, coefs):
+            rows = [leads(v, side) for v in inner]
+            columns = [beside(v, r, side) for v, r in zip(inner, rows)]
+            inner = [
+                [u + h if sign > 0 else u - h for u, h in zip(v, hops(r, c, side, weights))]
+                for v, r, c, (_, _, sign, _) in zip(values, rows, columns, chains)
+            ]
+        values = inner
+    lane = lax.broadcasted_iota(jnp.int32, (count, LANES), 1)
+    for row, forward, partner in zip(groups, values[0::2], values[1::2]):
+        site = lax.broadcasted_iota(jnp.int32, (count, LANES), 0) + base_ref[0] + row
+        for j, (f, p) in enumerate(zip(forward, partner)):
+            term = jnp.where(lane + j * LANES == site, 0.0, f * p)
+            out_ref[row : row + count, j * LANES : (j + 1) * LANES] = term.astype(out_ref.dtype)
+
+
+def measured(base, forward, partner, rates):
     return pl.pallas_call(
         functools.partial(measure_kernel, math.isqrt(forward.shape[1])),
         out_shape=jax.ShapeDtypeStruct(forward.shape, jnp.bfloat16),
-        in_specs=[SMEM, VMEM, VMEM, VMEM] + [ANY] * len(kept),
+        in_specs=[SMEM, VMEM, VMEM, VMEM],
         out_specs=VMEM,
         compiler_params=params(),
-        cost_estimate=cost(200 * forward.size, 12 * forward.size),
-    )(base, forward, partner, rates, *kept)
+        cost_estimate=cost(45000 * forward.size, 12 * forward.size),
+    )(base, forward, partner, rates)
 
 
 def packed_kernel(base_ref, columns_ref, rows_ref, forward_low, partner_low, forward_ref, partner_ref, rows, arrived):
@@ -215,8 +228,7 @@
         if displacement == 1:
             rates, *start = lax.optimization_barrier((rates, *start, forward_low))[:3]
             terms.append(measured(first, *start, rates))
-        kept = (forward_map,) if displacement == clusters - 1 else ()
-        terms.append(measured(first_ref(displacement)[None], forward, partner, rates, *kept))
+        terms.append(measured(first_ref(displacement)[None], forward, partner, rates))
     last = clusters - 1
     *early, late = terms
     early = jnp.stack(early)
@@ -235,9 +247,12 @@
 
     total = jnp.where(anchor == last, late, early_term(anchor)).astype(jnp.float32)
     total = total + jnp.where(anchor == last, 0.0, soon)
-    total = total + sent(jnp.where(anchor == 0, late, early_term(anchor - 1)), shifted(-1)).astype(jnp.float32)
-    for k in range(last - 1, 0, -1):
-        total = total + sent(late, {k: (last, -1)}).astype(jnp.float32)
+    others = [sent(late, {k: (last, -1)}) for k in range(1, last - 1)]
+    beside = sent(late, {k: (k ^ 1, -(k < k ^ 1)) for k in range(clusters)})
+    behind = sent(jnp.where(anchor == 0, late, early_term(anchor - 1)), shifted(-1))
+    total = total + sum(term.astype(jnp.float32) for term in others)
+    total = total + jnp.where(anchor == last, beside, 0.0).astype(jnp.float32)
+    total = total + behind.astype(jnp.float32)
     return (total * (sites / clusters))[None]
 
 

time: 28 us -> 27.8 us (level)
  the two profiles are of different devices: /device:TPU:31 before, /device:TPU:0 now
where the time goes in v6:
time: 27.8 us; the launch traced here: 27.6 us
  starting transfers between devices  12.1 us (44%)
  Pallas kernels  5.8 us (21%)
  waiting for transfers between devices  4.96 us (18%)
  matrix products  2.33 us (8%)
  local copies, waits for them, and re-layouts  1.41 us (5%)
  other arithmetic  0.72 us (3%)
    ppermute x5, starting transfers between devices, sent(): return lax.ppermute(term, ('tm', 'col'), route(targets))  6.95 us
    ppermute x3, starting transfers between devices, per_device(): low = lax.ppermute(low, ('tm', 'col'), around)  5.13 us
    ppermute x3, waiting for transfers between devices, per_device(): low = lax.ppermute(low, ('tm', 'col'), around)  2.99 us
    pallas_call x4, Pallas kernels, measured(): pl.pallas_call(functools.partial(measure_kernel, math.isqrt(forward.shape...  2.76 us
    ppermute x5, waiting for transfers between devices, sent(): return lax.ppermute(term, ('tm', 'col'), route(targets))  1.97 us
    pallas_call x1, Pallas kernels, turned(): pl.pallas_call(turned_kernel, out_shape=jax.ShapeDtypeStruct(dense.shape[...  1.89 us
    unnamed x6, local copies, waits for them, and re-layouts  1.4 us
    dot_general x3, matrix products, per_device(): jnp.dot(low[ref_rows:], inverse_map, preferred_element_type=jnp.float32)  1.17 us
  transfers between devices with their start and end apart: 8, of which 4 were waited for; matrix products, arithmetic and copies ran while one was open for 3% of the time, Pallas kernels for 17%

profile of v6, /device:TPU:0, one launch (start us, length us, event | category | flops | bytes accessed | tf_op | source)
XLA Modules:
  0.0 27.6 jit_solution(11343429386973667749)
XLA Ops:
  0.0 0.0 copy-start
  0.0 1.1 %shard_map.64 = (bf16[16,1024]{1,0:T(8,128)(2,1)S(1)}, bf16[16,1024]{1,0:T(8,128)(2,1)S(1)}, f32[16,1024]{1,0:T(8,128)S(1)}, f32[16,1024]{1,0:T(8,128)S(1)}) custom-call(s32[1]{0:T(128)} %bitcast.1.base_ref, f32[16,1024]{1,0:T(8,128)} %bitcast.42, f32[16,1024]{1,0:T(8,128)} %bitcast.43), custom_call_target="tpu_custom_call" | custom-call | flops 65536 | bytes 196608 | tf_op jit(solution)/shard_map/pallas_call | solution.py:152
  1.1 3.1 %collective-permute-start = (bf16[32,1024]{1,0:T(8,128)(2,1)S(1)}, bf16[32,1024]{1,0:T(8,128)(2,1)S(1)}, u32[]{:S(2)}, u32[]{:S(2)}) collective-permute-start(bf16[32,1024]{1,0:T(8,128)(2,1)S(1)} %pad_maximum_fusion.1), channel_id=1, source_target_pairs={{0,4},{1,5},{4,8},{5,9},{8,12},{9,13},{12,1},{13,0},{2,6},{3,7},{6... | collective-permute-start | bytes 196616 | tf_op jit(solution)/shard_map/ppermute | solution.py:224
  4.2 0.0 copy-start.1
  4.2 0.7 %copy-done.1 = s32[1,2,1024]{2,1,0:T(2,128)S(1)} copy-done((s32[1,2,1024]{2,1,0:T(2,128)S(1)}, s32[1,2,1024]{2,1,0:T(2,128)}, u32[]{:S(2)}) %copy-start.1) | copy-done | bytes 8216
  4.9 0.0 copy-start.2
  4.9 0.7 %copy-done.2 = s32[2,1024]{1,0:T(2,128)S(1)} copy-done((s32[2,1024]{1,0:T(2,128)S(1)}, s32[2,1024]{1,0:T(2,128)}, u32[]{:S(2)}) %copy-start.2) | copy-done | bytes 8216
  5.6 0.1 shard_map.66.factors_ref
  5.8 1.9 %shard_map.65 = bf16[1024,1024]{1,0:T(8,128)(2,1)S(1)} custom-call(bf16[1024,1024]{1,0:T(8,128)(2,1)} %bitcast.41), custom_call_target="tpu_custom_call" | custom-call | flops 1048576 | bytes 4194304 | tf_op jit(solution)/shard_map/pallas_call | solution.py:183
  7.7 0.0 collective-permute-done
  7.7 0.4 %fusion.16 = (bf16[16,1024]{1,0:T(8,128)(2,1)S(1)}, f32[16,1024]{1,0:T(8,128)S(1)}) fusion(bf16[1024,1024]{1,0:T(8,128)(2,1)S(1)} %shard_map.65, bf16[32,1024]{1,0:T(8,128)(2,1)S(1)} %collective-permute-done), kind=kOutput, calls=%fused_computation.25 | convolution fusion | flops 33570816 | bytes 2228224 | tf_op jit(solution)/shard_map/dot_general | solution.py:225
  8.1 0.0 copy-done
  8.1 0.4 %fusion.15 = (bf16[16,1024]{1,0:T(8,128)(2,1)S(1)}, f32[16,1024]{1,0:T(8,128)S(1)}) fusion(bf16[1,1024,1024]{2,1,0:T(8,128)(2,1)S(1)} %copy-done, bf16[32,1024]{1,0:T(8,128)(2,1)S(1)} %collective-permute-done), kind=kOutput, calls=%fused_computation.24 | convolution fusion | flops 33570816 | bytes 2228224 | tf_op jit(solution)/shard_map/dot_general | solution.py:226
  8.5 1.6 %collective-permute-start.1 = (bf16[32,1024]{1,0:T(8,128)(2,1)S(1)}, bf16[32,1024]{1,0:T(8,128)(2,1)S(1)}, u32[]{:S(2)}, u32[]{:S(2)}) collective-permute-start(bf16[32,1024]{1,0:T(8,128)(2,1)S(1)} %pad_maximum_fusion.2), channel_id=1, source_target_pairs={{0,4},{1,5},{4,8},{5,9},{8,12},{9,13},{12,1},{13,0},{2,6},{3,7},{6... | collective-permute-start | bytes 196616 | tf_op jit(solution)/shard_map/ppermute | solution.py:224
  10.1 0.7 %shard_map.67 = bf16[16,1024]{1,0:T(8,128)(2,1)S(1)} custom-call(s32[1]{0:T(128)} %bitcast.1.base_ref, f32[16,1024]{1,0:T(8,128)S(1)} %get-tuple-element.19.forward_ref, f32[16,1024]{1,0:T(8,128)S(1)} %get-tuple-element.20.partner_ref, f32[8,1024]{1,0:T(8,128)S(1)} %shard_map.66.factors_ref), custom_call_target="tpu_custom_call" | custom-call | flops 737280000 | bytes 196608 | tf_op jit(solution)/shard_map/pallas_call | solution.py:122
  10.8 0.7 %shard_map.68 = bf16[16,1024]{1,0:T(8,128)(2,1)S(1)} custom-call(s32[1]{0:T(128)} %bitcast.7.base_ref, f32[16,1024]{1,0:T(8,128)S(1)} %get-tuple-element.30.forward_ref, f32[16,1024]{1,0:T(8,128)S(1)} %get-tuple-element.28.partner_ref, f32[8,1024]{1,0:T(8,128)S(1)} %shard_map.66.factors_ref), custom_call_target="tpu_custom_call" | custom-call | flops 737280000 | bytes 196608 | tf_op jit(solution)/shard_map/pallas_call | solution.py:122
  11.5 2.5 %collective-permute-done.1 = bf16[32,1024]{1,0:T(8,128)(2,1)S(1)} collective-permute-done((bf16[32,1024]{1,0:T(8,128)(2,1)S(1)}, bf16[32,1024]{1,0:T(8,128)(2,1)S(1)}, u32[]{:S(2)}, u32[]{:S(2)}) %collective-permute-start.1) | collective-permute-done | bytes 65568 | tf_op jit(solution)/shard_map/ppermute | solution.py:224
  14.0 0.4 %fusion.17 = (bf16[16,1024]{1,0:T(8,128)(2,1)S(1)}, f32[16,1024]{1,0:T(8,128)S(1)}) fusion(bf16[1,1024,1024]{2,1,0:T(8,128)(2,1)S(1)} %copy-done, bf16[32,1024]{1,0:T(8,128)(2,1)S(1)} %collective-permute-done.1), kind=kOutput, calls=%fused_computation.26 | convolution fusion | flops 33570816 | bytes 2228224 | tf_op jit(solution)/shard_map/dot_general | solution.py:226
  14.4 0.4 %fusion.18 = (bf16[16,1024]{1,0:T(8,128)(2,1)S(1)}, f32[16,1024]{1,0:T(8,128)S(1)}) fusion(bf16[1024,1024]{1,0:T(8,128)(2,1)S(1)} %shard_map.65, bf16[32,1024]{1,0:T(8,128)(2,1)S(1)} %collective-permute-done.1), kind=kOutput, calls=%fused_computation.27 | convolution fusion | flops 33570816 | bytes 2228224 | tf_op jit(solution)/shard_map/dot_general | solution.py:225
  14.8 0.4 %collective-permute-start.2 = (bf16[32,1024]{1,0:T(8,128)(2,1)S(1)}, bf16[32,1024]{1,0:T(8,128)(2,1)S(1)}, u32[]{:S(2)}, u32[]{:S(2)}) collective-permute-start(bf16[32,1024]{1,0:T(8,128)(2,1)S(1)} %pad_maximum_fusion.3), channel_id=1, source_target_pairs={{0,4},{1,5},{4,8},{5,9},{8,12},{9,13},{12,1},{13,0},{2,6},{3,7},{6... | collective-permute-start | bytes 196616 | tf_op jit(solution)/shard_map/ppermute | solution.py:224
  15.2 0.7 %shard_map.70 = bf16[16,1024]{1,0:T(8,128)(2,1)S(1)} custom-call(s32[1]{0:T(128)} %bitcast.10.base_ref, f32[16,1024]{1,0:T(8,128)S(1)} %get-tuple-element.34.forward_ref, f32[16,1024]{1,0:T(8,128)S(1)} %get-tuple-element.32.partner_ref, f32[8,1024]{1,0:T(8,128)S(1)} %shard_map.66.factors_ref), custom_call_target="tpu_custom_call" | custom-call | flops 737280000 | bytes 196608 | tf_op jit(solution)/shard_map/pallas_call | solution.py:122
  16.0 0.1 collective-permute-start.3
  16.0 3.9 %collective-permute-start.4 = (bf16[16,1024]{1,0:T(8,128)(2,1)S(1)}, bf16[16,1024]{1,0:T(8,128)(2,1)S(1)}, u32[]{:S(2)}, u32[]{:S(2)}) collective-permute-start(bf16[16,1024]{1,0:T(8,128)(2,1)S(1)} %get-tuple-element.26), channel_id=1, source_target_pairs={{0,5},{1,4},{4,9},{5,8},{8,13},{9,12},{12,0},{13,1},{2,7},{3,6},{6... | collective-permute-start | bytes 98312 | tf_op jit(solution)/shard_map/ppermute | solution.py:240
  19.9 0.5 %collective-permute-done.2 = bf16[32,1024]{1,0:T(8,128)(2,1)S(1)} collective-permute-done((bf16[32,1024]{1,0:T(8,128)(2,1)S(1)}, bf16[32,1024]{1,0:T(8,128)(2,1)S(1)}, u32[]{:S(2)}, u32[]{:S(2)}) %collective-permute-start.2) | collective-permute-done | bytes 65568 | tf_op jit(solution)/shard_map/ppermute | solution.py:224
  20.4 0.4 %fusion.7.forward_ref = f32[16,1024]{1,0:T(8,128)S(1)} fusion(bf16[1024,1024]{1,0:T(8,128)(2,1)S(1)} %shard_map.65, bf16[32,1024]{1,0:T(8,128)(2,1)S(1)} %collective-permute-done.2), kind=kOutput, calls=%fused_computation.12 | convolution fusion | flops 33554432 | bytes 2195456 | tf_op jit(solution)/shard_map/dot_general | solution.py:225
  20.8 0.4 %fusion.partner_ref = f32[16,1024]{1,0:T(8,128)S(1)} fusion(bf16[1,1024,1024]{2,1,0:T(8,128)(2,1)S(1)} %copy-done, bf16[32,1024]{1,0:T(8,128)(2,1)S(1)} %collective-permute-done.2), kind=kOutput, calls=%fused_computation | convolution fusion | flops 33554432 | bytes 2195456 | tf_op jit(solution)/shard_map/dot_general | solution.py:226
  21.2 0.7 %shard_map.69 = bf16[16,1024]{1,0:T(8,128)(2,1)S(1)} custom-call(s32[1]{0:T(128)} %bitcast.base_ref, f32[16,1024]{1,0:T(8,128)S(1)} %fusion.7.forward_ref, f32[16,1024]{1,0:T(8,128)S(1)} %fusion.partner_ref, f32[8,1024]{1,0:T(8,128)S(1)} %shard_map.66.factors_ref), custom_call_target="tpu_custom_call" | custom-call | flops 737280000 | bytes 196608 | tf_op jit(solution)/shard_map/pallas_call | solution.py:122
  21.9 0.7 %collective-permute-start.7 = (bf16[16,1024]{1,0:T(8,128)(2,1)S(1)}, bf16[16,1024]{1,0:T(8,128)(2,1)S(1)}, u32[]{:S(2)}, u32[]{:S(2)}) collective-permute-start(bf16[16,1024]{1,0:T(8,128)(2,1)S(1)} %bitcast_select_fusion), channel_id=1, source_target_pairs={{0,13},{1,12},{4,0},{5,1},{8,4},{9,5},{12,8},{13,9},{2,15},{3,14},... | collective-permute-start | bytes 98312 | tf_op jit(solution)/shard_map/ppermute | solution.py:240
  22.6 1.6 %collective-permute-start.6 = (bf16[16,1024]{1,0:T(8,128)(2,1)S(1)}, bf16[16,1024]{1,0:T(8,128)(2,1)S(1)}, u32[]{:S(2)}, u32[]{:S(2)}) collective-permute-start(bf16[16,1024]{1,0:T(8,128)(2,1)S(1)} %shard_map.69), channel_id=1, source_target_pairs={{0,5},{1,4},{4,0},{5,1},{8,13},{9,12},{12,8},{13,9},{2,7},{3,6},{6... | collective-permute-start | bytes 98312 | tf_op jit(solution)/shard_map/ppermute | solution.py:240
  24.2 0.7 %collective-permute-start.5 = (bf16[16,1024]{1,0:T(8,128)(2,1)S(1)}, bf16[16,1024]{1,0:T(8,128)(2,1)S(1)}, u32[]{:S(2)}, u32[]{:S(2)}) collective-permute-start(bf16[16,1024]{1,0:T(8,128)(2,1)S(1)} %shard_map.69), channel_id=1, source_target_pairs={{4,13},{5,12},{6,15},{7,14},{20,29},{21,28},{22,31},{23,30}} | collective-permute-start | bytes 98312 | tf_op jit(solution)/shard_map/ppermute | solution.py:240
  24.9 0.0 collective-permute-done.3
  24.9 0.0 collective-permute-done.4
  24.9 1.3 %collective-permute-done.7 = bf16[16,1024]{1,0:T(8,128)(2,1)S(1)} collective-permute-done((bf16[16,1024]{1,0:T(8,128)(2,1)S(1)}, bf16[16,1024]{1,0:T(8,128)(2,1)S(1)}, u32[]{:S(2)}, u32[]{:S(2)}) %collective-permute-start.7) | collective-permute-done | bytes 32800 | tf_op jit(solution)/shard_map/ppermute | solution.py:240
  26.2 0.6 %collective-permute-done.6 = bf16[16,1024]{1,0:T(8,128)(2,1)S(1)} collective-permute-done((bf16[16,1024]{1,0:T(8,128)(2,1)S(1)}, bf16[16,1024]{1,0:T(8,128)(2,1)S(1)}, u32[]{:S(2)}, u32[]{:S(2)}) %collective-permute-start.6) | collective-permute-done | bytes 32800 | tf_op jit(solution)/shard_map/ppermute | solution.py:240
  26.9 0.0 collective-permute-done.5
  26.9 0.7 %multiply_bitcast_fusion = f32[1,16,1024]{2,1,0:T(8,128)} fusion(bf16[16,1024]{1,0:T(8,128)(2,1)S(1)} %collective-permute-done.7, bf16[16,1024]{1,0:T(8,128)(2,1)S(1)} %collective-permute-done.5, bf16[16,1024]{1,0:T(8,128)(2,1)S(1)} %collective-permute-done.4, bf16[16,1024]{1,0:T(8,128)(2,1)S(1)} %collective-permute-done.3, ...), kind=kLoop, calls=%fused_computation.10 | loop fusion | flops 245760 | bytes 294917 | tf_op jit(solution)/shard_map/broadcast_in_dim | solution.py:256
  (6 shorter events, 0.1 us)
Async XLA Ops:
  0.0 8.1 %copy-start = (bf16[1,1024,1024]{2,1,0:T(8,128)(2,1)S(1)}, bf16[1,1024,1024]{2,1,0:T(8,128)(2,1)}, u32[]{:S(2)}) copy-start(bf16[1,1024,1024]{2,1,0:T(8,128)(2,1)} %param.7) | copy-start | bytes 6291460
  1.1 6.6 %collective-permute-start = (bf16[32,1024]{1,0:T(8,128)(2,1)S(1)}, bf16[32,1024]{1,0:T(8,128)(2,1)S(1)}, u32[]{:S(2)}, u32[]{:S(2)}) collective-permute-start(bf16[32,1024]{1,0:T(8,128)(2,1)S(1)} %pad_maximum_fusion.1), channel_id=1, source_target_pairs={{0,4},{1,5},{4,8},{5,9},{8,12},{9,13},{12,1},{13,0},{2,6},{3,7},{6... | collective-permute-start | bytes 196616 | tf_op jit(solution)/shard_map/ppermute | solution.py:224
  4.2 0.7 %copy-start.1 = (s32[1,2,1024]{2,1,0:T(2,128)S(1)}, s32[1,2,1024]{2,1,0:T(2,128)}, u32[]{:S(2)}) copy-start(s32[1,2,1024]{2,1,0:T(2,128)} %param.10) | copy-start | bytes 24580
  4.9 0.7 %copy-start.2 = (s32[2,1024]{1,0:T(2,128)S(1)}, s32[2,1024]{1,0:T(2,128)}, u32[]{:S(2)}) copy-start(s32[2,1024]{1,0:T(2,128)} %bonds_ref.1) | copy-start | bytes 24580
  8.5 5.5 %collective-permute-start.1 = (bf16[32,1024]{1,0:T(8,128)(2,1)S(1)}, bf16[32,1024]{1,0:T(8,128)(2,1)S(1)}, u32[]{:S(2)}, u32[]{:S(2)}) collective-permute-start(bf16[32,1024]{1,0:T(8,128)(2,1)S(1)} %pad_maximum_fusion.2), channel_id=1, source_target_pairs={{0,4},{1,5},{4,8},{5,9},{8,12},{9,13},{12,1},{13,0},{2,6},{3,7},{6... | collective-permute-start | bytes 196616 | tf_op jit(solution)/shard_map/ppermute | solution.py:224
  14.8 5.6 %collective-permute-start.2 = (bf16[32,1024]{1,0:T(8,128)(2,1)S(1)}, bf16[32,1024]{1,0:T(8,128)(2,1)S(1)}, u32[]{:S(2)}, u32[]{:S(2)}) collective-permute-start(bf16[32,1024]{1,0:T(8,128)(2,1)S(1)} %pad_maximum_fusion.3), channel_id=1, source_target_pairs={{0,4},{1,5},{4,8},{5,9},{8,12},{9,13},{12,1},{13,0},{2,6},{3,7},{6... | collective-permute-start | bytes 196616 | tf_op jit(solution)/shard_map/ppermute | solution.py:224
  16.0 8.9 %collective-permute-start.3 = (bf16[16,1024]{1,0:T(8,128)(2,1)S(1)}, bf16[16,1024]{1,0:T(8,128)(2,1)S(1)}, u32[]{:S(2)}, u32[]{:S(2)}) collective-permute-start(bf16[16,1024]{1,0:T(8,128)(2,1)S(1)} %get-tuple-element.25), channel_id=1, source_target_pairs={{0,9},{1,8},{4,13},{5,12},{8,0},{9,1},{12,4},{13,5},{2,11},{3,10},... | collective-permute-start | bytes 98312 | tf_op jit(solution)/shard_map/ppermute | solution.py:240
  16.0 8.9 %collective-permute-start.4 = (bf16[16,1024]{1,0:T(8,128)(2,1)S(1)}, bf16[16,1024]{1,0:T(8,128)(2,1)S(1)}, u32[]{:S(2)}, u32[]{:S(2)}) collective-permute-start(bf16[16,1024]{1,0:T(8,128)(2,1)S(1)} %get-tuple-element.26), channel_id=1, source_target_pairs={{0,5},{1,4},{4,9},{5,8},{8,13},{9,12},{12,0},{13,1},{2,7},{3,6},{6... | collective-permute-start | bytes 98312 | tf_op jit(solution)/shard_map/ppermute | solution.py:240
  21.9 4.3 %collective-permute-start.7 = (bf16[16,1024]{1,0:T(8,128)(2,1)S(1)}, bf16[16,1024]{1,0:T(8,128)(2,1)S(1)}, u32[]{:S(2)}, u32[]{:S(2)}) collective-permute-start(bf16[16,1024]{1,0:T(8,128)(2,1)S(1)} %bitcast_select_fusion), channel_id=1, source_target_pairs={{0,13},{1,12},{4,0},{5,1},{8,4},{9,5},{12,8},{13,9},{2,15},{3,14},... | collective-permute-start | bytes 98312 | tf_op jit(solution)/shard_map/ppermute | solution.py:240
  22.6 4.3 %collective-permute-start.6 = (bf16[16,1024]{1,0:T(8,128)(2,1)S(1)}, bf16[16,1024]{1,0:T(8,128)(2,1)S(1)}, u32[]{:S(2)}, u32[]{:S(2)}) collective-permute-start(bf16[16,1024]{1,0:T(8,128)(2,1)S(1)} %shard_map.69), channel_id=1, source_target_pairs={{0,5},{1,4},{4,0},{5,1},{8,13},{9,12},{12,8},{13,9},{2,7},{3,6},{6... | collective-permute-start | bytes 98312 | tf_op jit(solution)/shard_map/ppermute | solution.py:240
  24.2 2.6 %collective-permute-start.5 = (bf16[16,1024]{1,0:T(8,128)(2,1)S(1)}, bf16[16,1024]{1,0:T(8,128)(2,1)S(1)}, u32[]{:S(2)}, u32[]{:S(2)}) collective-permute-start(bf16[16,1024]{1,0:T(8,128)(2,1)S(1)} %shard_map.69), channel_id=1, source_target_pairs={{4,13},{5,12},{6,15},{7,14},{20,29},{21,28},{22,31},{23,30}} | collective-permute-start | bytes 98312 | tf_op jit(solution)/shard_map/ppermute | solution.py:240

commit v7 on v6

--- a/solution.py
+++ b/solution.py
@@ -211,7 +211,6 @@
 
     around = route({k: ((k + 1) % clusters, (k + 1) // clusters) for k in range(clusters)})
     forward_map, inverse_map = turned(cluster_maps[0]), inverse_maps[0]
-    rates = factors(ising_field[0], hop_bonds)
     first = first_ref(0)[None]
     forward_low, partner_low, forward, partner = packed(first, seed_columns[0], seed_rows[0])
     start = (forward, partner)
@@ -226,7 +225,8 @@
         partner = jnp.dot(low[ref_rows:], inverse_map, preferred_element_type=jnp.float32)
         forward_low, partner_low = forward.astype(jnp.bfloat16), partner.astype(jnp.bfloat16)
         if displacement == 1:
-            rates, *start = lax.optimization_barrier((rates, *start, forward_low))[:3]
+            field, bonds, *start = lax.optimization_barrier((ising_field[0], hop_bonds, *start, forward_low))[:4]
+            rates = factors(field, bonds)
             terms.append(measured(first, *start, rates))
         terms.append(measured(first_ref(displacement)[None], forward, partner, rates))
     last = clusters - 1
@@ -247,12 +247,19 @@
 
     total = jnp.where(anchor == last, late, early_term(anchor)).astype(jnp.float32)
     total = total + jnp.where(anchor == last, 0.0, soon)
-    others = [sent(late, {k: (last, -1)}) for k in range(1, last - 1)]
-    beside = sent(late, {k: (k ^ 1, -(k < k ^ 1)) for k in range(clusters)})
-    behind = sent(jnp.where(anchor == 0, late, early_term(anchor - 1)), shifted(-1))
-    total = total + sum(term.astype(jnp.float32) for term in others)
-    total = total + jnp.where(anchor == last, beside, 0.0).astype(jnp.float32)
-    total = total + behind.astype(jnp.float32)
+    behind = jnp.where(anchor == 0, late, early_term(anchor - 1))
+    soonest = jnp.where(anchor == 1, late, early_term(anchor))
+    soonest, behind, late = lax.optimization_barrier((soonest, behind, late))
+
+    def sent_last(term, k):
+        swap = {m: (m, 1) for m in range(clusters)}
+        term = sent(term, {**swap, k: (last, -1), last: (k, 1)})
+        return jnp.where(anchor == last, term, 0.0).astype(jnp.float32)
+
+    total = total + sent_last(soonest, 1)
+    for k in range(last - 1, 1, -1):
+        total = total + sent_last(late, k)
+    total = total + sent(behind, shifted(-1)).astype(jnp.float32)
     return (total * (sites / clusters))[None]
 
 

time: 27.8 us -> 27.6 us (level)
  waiting for transfers between devices: 4.96 us -> 8.4 us
  starting transfers between devices: 12.1 us -> 10 us
  local copies, waits for them, and re-layouts: 1.41 us -> 0.03 us
    ppermute x3, waiting for transfers between devices: 2.99 us -> 4.99 us  [per_device(): low = lax.ppermute(low, ('tm', 'col'), around)]
    ppermute x5, waiting for transfers between devices: 1.97 us -> 3.41 us  [sent(): return lax.ppermute(term, ('tm', 'col'), route(targets))]
    unnamed x6, local copies, waits for them, and re-layouts: 1.4 us -> 0.02 us
    ppermute x3, starting transfers between devices: 5.13 us -> 4.06 us  [per_device(): low = lax.ppermute(low, ('tm', 'col'), around)]
    ppermute x5, starting transfers between devices: 6.95 us -> 5.98 us  [sent(): return lax.ppermute(term, ('tm', 'col'), route(targets))]
  transfers between devices with their start and end apart: 8 -> 8, of which waited for: 4 -> 6; matrix products, arithmetic and copies ran while one was open for 3% -> 3% of each run, Pallas kernels for 17% -> 17%
where the time goes in v7:
time: 27.6 us; the launch traced here: 27.5 us
  starting transfers between devices  10 us (36%)
  waiting for transfers between devices  8.4 us (30%)
  Pallas kernels  5.8 us (21%)
  matrix products  2.32 us (8%)
  other arithmetic  0.72 us (3%)
    ppermute x5, starting transfers between devices, sent(): return lax.ppermute(term, ('tm', 'col'), route(targets))  5.98 us
    ppermute x3, waiting for transfers between devices, per_device(): low = lax.ppermute(low, ('tm', 'col'), around)  4.99 us
    ppermute x3, starting transfers between devices, per_device(): low = lax.ppermute(low, ('tm', 'col'), around)  4.06 us
    ppermute x5, waiting for transfers between devices, sent(): return lax.ppermute(term, ('tm', 'col'), route(targets))  3.41 us
    pallas_call x4, Pallas kernels, measured(): pl.pallas_call(functools.partial(measure_kernel, math.isqrt(forward.shape...  2.77 us
    pallas_call x1, Pallas kernels, turned(): pl.pallas_call(turned_kernel, out_shape=jax.ShapeDtypeStruct(dense.shape[...  1.89 us
    dot_general x3, matrix products, per_device(): jnp.dot(low[ref_rows:], inverse_map, preferred_element_type=jnp.float32)  1.17 us
    dot_general x3, matrix products, per_device(): jnp.dot(low[:ref_rows], forward_map, preferred_element_type=jnp.float32)  1.16 us
  transfers between devices with their start and end apart: 8, of which 6 were waited for; matrix products, arithmetic and copies ran while one was open for 3% of the time, Pallas kernels for 17%

profile of v7, /device:TPU:0, one launch (start us, length us, event | category | flops | bytes accessed | tf_op | source)
XLA Modules:
  0.0 27.5 jit_solution(8604427771167072095)
XLA Ops:
  0.0 0.0 copy-start
  0.0 1.1 %shard_map.64 = (bf16[16,1024]{1,0:T(8,128)(2,1)S(1)}, bf16[16,1024]{1,0:T(8,128)(2,1)S(1)}, f32[16,1024]{1,0:T(8,128)S(1)}, f32[16,1024]{1,0:T(8,128)S(1)}) custom-call(s32[1]{0:T(128)} %bitcast.1.base_ref, f32[16,1024]{1,0:T(8,128)} %bitcast.43, f32[16,1024]{1,0:T(8,128)} %bitcast.44), custom_call_target="tpu_custom_call" | custom-call | flops 65536 | bytes 196608 | tf_op jit(solution)/shard_map/pallas_call | solution.py:152
  1.1 3.1 %collective-permute-start = (bf16[32,1024]{1,0:T(8,128)(2,1)S(1)}, bf16[32,1024]{1,0:T(8,128)(2,1)S(1)}, u32[]{:S(2)}, u32[]{:S(2)}) collective-permute-start(bf16[32,1024]{1,0:T(8,128)(2,1)S(1)} %pad_maximum_fusion.1), channel_id=1, source_target_pairs={{0,4},{1,5},{4,8},{5,9},{8,12},{9,13},{12,1},{13,0},{2,6},{3,7},{6... | collective-permute-start | bytes 196616 | tf_op jit(solution)/shard_map/ppermute | solution.py:223
  4.2 1.9 %shard_map.65 = bf16[1024,1024]{1,0:T(8,128)(2,1)S(1)} custom-call(bf16[1024,1024]{1,0:T(8,128)(2,1)} %bitcast.42), custom_call_target="tpu_custom_call" | custom-call | flops 1048576 | bytes 4194304 | tf_op jit(solution)/shard_map/pallas_call | solution.py:183
  6.1 0.0 copy-start.1
  6.1 0.0 copy-start.2
  6.1 1.5 %collective-permute-done = bf16[32,1024]{1,0:T(8,128)(2,1)S(1)} collective-permute-done((bf16[32,1024]{1,0:T(8,128)(2,1)S(1)}, bf16[32,1024]{1,0:T(8,128)(2,1)S(1)}, u32[]{:S(2)}, u32[]{:S(2)}) %collective-permute-start) | collective-permute-done | bytes 65568 | tf_op jit(solution)/shard_map/ppermute | solution.py:223
  7.6 0.4 %fusion.16 = (bf16[16,1024]{1,0:T(8,128)(2,1)S(1)}, f32[16,1024]{1,0:T(8,128)S(1)}) fusion(bf16[1024,1024]{1,0:T(8,128)(2,1)S(1)} %shard_map.65, bf16[32,1024]{1,0:T(8,128)(2,1)S(1)} %collective-permute-done), kind=kOutput, calls=%fused_computation.26 | convolution fusion | flops 33570816 | bytes 2228224 | tf_op jit(solution)/shard_map/dot_general | solution.py:224
  8.0 0.0 copy-done
  8.0 0.4 %fusion.15 = (bf16[16,1024]{1,0:T(8,128)(2,1)S(1)}, f32[16,1024]{1,0:T(8,128)S(1)}) fusion(bf16[1,1024,1024]{2,1,0:T(8,128)(2,1)S(1)} %copy-done, bf16[32,1024]{1,0:T(8,128)(2,1)S(1)} %collective-permute-done), kind=kOutput, calls=%fused_computation.25 | convolution fusion | flops 33570816 | bytes 2228224 | tf_op jit(solution)/shard_map/dot_general | solution.py:225
  8.4 0.9 %collective-permute-start.1 = (bf16[32,1024]{1,0:T(8,128)(2,1)S(1)}, bf16[32,1024]{1,0:T(8,128)(2,1)S(1)}, u32[]{:S(2)}, u32[]{:S(2)}) collective-permute-start(bf16[32,1024]{1,0:T(8,128)(2,1)S(1)} %pad_maximum_fusion.2), channel_id=1, source_target_pairs={{0,4},{1,5},{4,8},{5,9},{8,12},{9,13},{12,1},{13,0},{2,6},{3,7},{6... | collective-permute-start | bytes 196616 | tf_op jit(solution)/shard_map/ppermute | solution.py:223
  9.3 0.0 copy-done.1
  9.3 0.0 copy-done.2
  9.3 0.1 shard_map.66.factors_ref
  9.4 0.7 %shard_map.67 = bf16[16,1024]{1,0:T(8,128)(2,1)S(1)} custom-call(s32[1]{0:T(128)} %bitcast.1.base_ref, f32[16,1024]{1,0:T(8,128)S(1)} %get-tuple-element.23.forward_ref, f32[16,1024]{1,0:T(8,128)S(1)} %get-tuple-element.24.partner_ref, f32[8,1024]{1,0:T(8,128)S(1)} %shard_map.66.factors_ref), custom_call_target="tpu_custom_call" | custom-call | flops 737280000 | bytes 196608 | tf_op jit(solution)/shard_map/pallas_call | solution.py:122
  10.1 0.7 %shard_map.68 = bf16[16,1024]{1,0:T(8,128)(2,1)S(1)} custom-call(s32[1]{0:T(128)} %bitcast.7.base_ref, f32[16,1024]{1,0:T(8,128)S(1)} %get-tuple-element.40.forward_ref, f32[16,1024]{1,0:T(8,128)S(1)} %get-tuple-element.38.partner_ref, f32[8,1024]{1,0:T(8,128)S(1)} %shard_map.66.factors_ref), custom_call_target="tpu_custom_call" | custom-call | flops 737280000 | bytes 196608 | tf_op jit(solution)/shard_map/pallas_call | solution.py:122
  10.8 3.1 %collective-permute-done.1 = bf16[32,1024]{1,0:T(8,128)(2,1)S(1)} collective-permute-done((bf16[32,1024]{1,0:T(8,128)(2,1)S(1)}, bf16[32,1024]{1,0:T(8,128)(2,1)S(1)}, u32[]{:S(2)}, u32[]{:S(2)}) %collective-permute-start.1) | collective-permute-done | bytes 65568 | tf_op jit(solution)/shard_map/ppermute | solution.py:223
  13.9 0.4 %fusion.17 = (bf16[16,1024]{1,0:T(8,128)(2,1)S(1)}, f32[16,1024]{1,0:T(8,128)S(1)}) fusion(bf16[1,1024,1024]{2,1,0:T(8,128)(2,1)S(1)} %copy-done, bf16[32,1024]{1,0:T(8,128)(2,1)S(1)} %collective-permute-done.1), kind=kOutput, calls=%fused_computation.27 | convolution fusion | flops 33570816 | bytes 2228224 | tf_op jit(solution)/shard_map/dot_general | solution.py:225
  14.3 0.4 %fusion.18 = (bf16[16,1024]{1,0:T(8,128)(2,1)S(1)}, f32[16,1024]{1,0:T(8,128)S(1)}) fusion(bf16[1024,1024]{1,0:T(8,128)(2,1)S(1)} %shard_map.65, bf16[32,1024]{1,0:T(8,128)(2,1)S(1)} %collective-permute-done.1), kind=kOutput, calls=%fused_computation.28 | convolution fusion | flops 33570816 | bytes 2228224 | tf_op jit(solution)/shard_map/dot_general | solution.py:224
  14.7 0.1 collective-permute-start.2
  14.8 0.7 %shard_map.70 = bf16[16,1024]{1,0:T(8,128)(2,1)S(1)} custom-call(s32[1]{0:T(128)} %bitcast.10.base_ref, f32[16,1024]{1,0:T(8,128)S(1)} %get-tuple-element.44.forward_ref, f32[16,1024]{1,0:T(8,128)S(1)} %get-tuple-element.42.partner_ref, f32[8,1024]{1,0:T(8,128)S(1)} %shard_map.66.factors_ref), custom_call_target="tpu_custom_call" | custom-call | flops 737280000 | bytes 196608 | tf_op jit(solution)/shard_map/pallas_call | solution.py:122
  15.5 0.1 collective-permute-start.3
  15.6 4.4 %collective-permute-start.4 = (bf16[16,1024]{1,0:T(8,128)(2,1)S(1)}, bf16[16,1024]{1,0:T(8,128)(2,1)S(1)}, u32[]{:S(2)}, u32[]{:S(2)}) collective-permute-start(bf16[16,1024]{1,0:T(8,128)(2,1)S(1)} %get-tuple-element.36), channel_id=1, source_target_pairs={{0,5},{1,4},{4,9},{5,8},{8,13},{9,12},{12,0},{13,1},{2,7},{3,6},{6... | collective-permute-start | bytes 98312 | tf_op jit(solution)/shard_map/ppermute | solution.py:240
  19.9 0.4 %collective-permute-done.2 = bf16[32,1024]{1,0:T(8,128)(2,1)S(1)} collective-permute-done((bf16[32,1024]{1,0:T(8,128)(2,1)S(1)}, bf16[32,1024]{1,0:T(8,128)(2,1)S(1)}, u32[]{:S(2)}, u32[]{:S(2)}) %collective-permute-start.2) | collective-permute-done | bytes 65568 | tf_op jit(solution)/shard_map/ppermute | solution.py:223
  20.3 0.4 %fusion.7.forward_ref = f32[16,1024]{1,0:T(8,128)S(1)} fusion(bf16[1024,1024]{1,0:T(8,128)(2,1)S(1)} %shard_map.65, bf16[32,1024]{1,0:T(8,128)(2,1)S(1)} %collective-permute-done.2), kind=kOutput, calls=%fused_computation.12 | convolution fusion | flops 33554432 | bytes 2195456 | tf_op jit(solution)/shard_map/dot_general | solution.py:224
  20.7 0.4 %fusion.partner_ref = f32[16,1024]{1,0:T(8,128)S(1)} fusion(bf16[1,1024,1024]{2,1,0:T(8,128)(2,1)S(1)} %copy-done, bf16[32,1024]{1,0:T(8,128)(2,1)S(1)} %collective-permute-done.2), kind=kOutput, calls=%fused_computation | convolution fusion | flops 33554432 | bytes 2195456 | tf_op jit(solution)/shard_map/dot_general | solution.py:225
  21.1 0.7 %shard_map.69 = bf16[16,1024]{1,0:T(8,128)(2,1)S(1)} custom-call(s32[1]{0:T(128)} %bitcast.base_ref, f32[16,1024]{1,0:T(8,128)S(1)} %fusion.7.forward_ref, f32[16,1024]{1,0:T(8,128)S(1)} %fusion.partner_ref, f32[8,1024]{1,0:T(8,128)S(1)} %shard_map.66.factors_ref), custom_call_target="tpu_custom_call" | custom-call | flops 737280000 | bytes 196608 | tf_op jit(solution)/shard_map/pallas_call | solution.py:122
  21.8 1.0 %collective-permute-start.5 = (bf16[16,1024]{1,0:T(8,128)(2,1)S(1)}, bf16[16,1024]{1,0:T(8,128)(2,1)S(1)}, u32[]{:S(2)}, u32[]{:S(2)}) collective-permute-start(bf16[16,1024]{1,0:T(8,128)(2,1)S(1)} %get-tuple-element.30), channel_id=1, source_target_pairs={{0,1},{1,0},{4,13},{5,12},{8,9},{9,8},{12,5},{13,4},{2,3},{3,2},{6... | collective-permute-start | bytes 98312 | tf_op jit(solution)/shard_map/ppermute | solution.py:240
  22.8 0.1 collective-permute-start.6
  22.9 0.5 %collective-permute-start.7 = (bf16[16,1024]{1,0:T(8,128)(2,1)S(1)}, bf16[16,1024]{1,0:T(8,128)(2,1)S(1)}, u32[]{:S(2)}, u32[]{:S(2)}) collective-permute-start(bf16[16,1024]{1,0:T(8,128)(2,1)S(1)} %get-tuple-element.32), channel_id=1, source_target_pairs={{0,13},{1,12},{4,0},{5,1},{8,4},{9,5},{12,8},{13,9},{2,15},{3,14},... | collective-permute-start | bytes 98312 | tf_op jit(solution)/shard_map/ppermute | solution.py:240
  23.4 0.0 collective-permute-done.3
  23.4 0.0 collective-permute-done.4
  23.4 0.3 collective-permute-done.5
  23.7 0.3 %collective-permute-done.6 = bf16[16,1024]{1,0:T(8,128)(2,1)S(1)} collective-permute-done((bf16[16,1024]{1,0:T(8,128)(2,1)S(1)}, bf16[16,1024]{1,0:T(8,128)(2,1)S(1)}, u32[]{:S(2)}, u32[]{:S(2)}) %collective-permute-start.6) | collective-permute-done | bytes 32800 | tf_op jit(solution)/shard_map/ppermute | solution.py:240
  24.0 2.8 %collective-permute-done.7 = bf16[16,1024]{1,0:T(8,128)(2,1)S(1)} collective-permute-done((bf16[16,1024]{1,0:T(8,128)(2,1)S(1)}, bf16[16,1024]{1,0:T(8,128)(2,1)S(1)}, u32[]{:S(2)}, u32[]{:S(2)}) %collective-permute-start.7) | collective-permute-done | bytes 32800 | tf_op jit(solution)/shard_map/ppermute | solution.py:240
  26.8 0.7 %multiply_bitcast_fusion = f32[1,16,1024]{2,1,0:T(8,128)} fusion(bf16[16,1024]{1,0:T(8,128)(2,1)S(1)} %collective-permute-done.7, bf16[16,1024]{1,0:T(8,128)(2,1)S(1)} %collective-permute-done.4, bf16[16,1024]{1,0:T(8,128)(2,1)S(1)} %collective-permute-done.3, bf16[16,1024]{1,0:T(8,128)(2,1)S(1)} %shard_map.69, ...), kind=kLoop, calls=%fused_computation.10 | loop fusion | flops 262144 | bytes 294917 | tf_op jit(solution)/shard_map/broadcast_in_dim | solution.py:263
  (6 shorter events, 0.1 us)
Async XLA Ops:
  0.0 8.0 %copy-start = (bf16[1,1024,1024]{2,1,0:T(8,128)(2,1)S(1)}, bf16[1,1024,1024]{2,1,0:T(8,128)(2,1)}, u32[]{:S(2)}) copy-start(bf16[1,1024,1024]{2,1,0:T(8,128)(2,1)} %param.7) | copy-start | bytes 6291460
  1.1 6.5 %collective-permute-start = (bf16[32,1024]{1,0:T(8,128)(2,1)S(1)}, bf16[32,1024]{1,0:T(8,128)(2,1)S(1)}, u32[]{:S(2)}, u32[]{:S(2)}) collective-permute-start(bf16[32,1024]{1,0:T(8,128)(2,1)S(1)} %pad_maximum_fusion.1), channel_id=1, source_target_pairs={{0,4},{1,5},{4,8},{5,9},{8,12},{9,13},{12,1},{13,0},{2,6},{3,7},{6... | collective-permute-start | bytes 196616 | tf_op jit(solution)/shard_map/ppermute | solution.py:223
  6.1 3.2 %copy-start.1 = (s32[1,2,1024]{2,1,0:T(2,128)S(1)}, s32[1,2,1024]{2,1,0:T(2,128)}, u32[]{:S(2)}) copy-start(s32[1,2,1024]{2,1,0:T(2,128)} %param.10) | copy-start | bytes 24580
  6.1 3.2 %copy-start.2 = (s32[2,1024]{1,0:T(2,128)S(1)}, s32[2,1024]{1,0:T(2,128)}, u32[]{:S(2)}) copy-start(s32[2,1024]{1,0:T(2,128)} %bonds_ref) | copy-start | bytes 24580
  8.4 5.5 %collective-permute-start.1 = (bf16[32,1024]{1,0:T(8,128)(2,1)S(1)}, bf16[32,1024]{1,0:T(8,128)(2,1)S(1)}, u32[]{:S(2)}, u32[]{:S(2)}) collective-permute-start(bf16[32,1024]{1,0:T(8,128)(2,1)S(1)} %pad_maximum_fusion.2), channel_id=1, source_target_pairs={{0,4},{1,5},{4,8},{5,9},{8,12},{9,13},{12,1},{13,0},{2,6},{3,7},{6... | collective-permute-start | bytes 196616 | tf_op jit(solution)/shard_map/ppermute | solution.py:223
  14.7 5.6 %collective-permute-start.2 = (bf16[32,1024]{1,0:T(8,128)(2,1)S(1)}, bf16[32,1024]{1,0:T(8,128)(2,1)S(1)}, u32[]{:S(2)}, u32[]{:S(2)}) collective-permute-start(bf16[32,1024]{1,0:T(8,128)(2,1)S(1)} %pad_maximum_fusion.3), channel_id=1, source_target_pairs={{0,4},{1,5},{4,8},{5,9},{8,12},{9,13},{12,1},{13,0},{2,6},{3,7},{6... | collective-permute-start | bytes 196616 | tf_op jit(solution)/shard_map/ppermute | solution.py:223
  15.5 7.9 %collective-permute-start.3 = (bf16[16,1024]{1,0:T(8,128)(2,1)S(1)}, bf16[16,1024]{1,0:T(8,128)(2,1)S(1)}, u32[]{:S(2)}, u32[]{:S(2)}) collective-permute-start(bf16[16,1024]{1,0:T(8,128)(2,1)S(1)} %get-tuple-element.35), channel_id=1, source_target_pairs={{0,9},{1,8},{4,13},{5,12},{8,0},{9,1},{12,4},{13,5},{2,11},{3,10},... | collective-permute-start | bytes 98312 | tf_op jit(solution)/shard_map/ppermute | solution.py:240
  15.6 7.8 %collective-permute-start.4 = (bf16[16,1024]{1,0:T(8,128)(2,1)S(1)}, bf16[16,1024]{1,0:T(8,128)(2,1)S(1)}, u32[]{:S(2)}, u32[]{:S(2)}) collective-permute-start(bf16[16,1024]{1,0:T(8,128)(2,1)S(1)} %get-tuple-element.36), channel_id=1, source_target_pairs={{0,5},{1,4},{4,9},{5,8},{8,13},{9,12},{12,0},{13,1},{2,7},{3,6},{6... | collective-permute-start | bytes 98312 | tf_op jit(solution)/shard_map/ppermute | solution.py:240
  21.8 1.8 %collective-permute-start.5 = (bf16[16,1024]{1,0:T(8,128)(2,1)S(1)}, bf16[16,1024]{1,0:T(8,128)(2,1)S(1)}, u32[]{:S(2)}, u32[]{:S(2)}) collective-permute-start(bf16[16,1024]{1,0:T(8,128)(2,1)S(1)} %get-tuple-element.30), channel_id=1, source_target_pairs={{0,1},{1,0},{4,13},{5,12},{8,9},{9,8},{12,5},{13,4},{2,3},{3,2},{6... | collective-permute-start | bytes 98312 | tf_op jit(solution)/shard_map/ppermute | solution.py:240
  22.8 1.2 %collective-permute-start.6 = (bf16[16,1024]{1,0:T(8,128)(2,1)S(1)}, bf16[16,1024]{1,0:T(8,128)(2,1)S(1)}, u32[]{:S(2)}, u32[]{:S(2)}) collective-permute-start(bf16[16,1024]{1,0:T(8,128)(2,1)S(1)} %shard_map.69), channel_id=1, source_target_pairs={{0,1},{1,0},{4,5},{5,4},{8,13},{9,12},{12,9},{13,8},{2,3},{3,2},{6... | collective-permute-start | bytes 98312 | tf_op jit(solution)/shard_map/ppermute | solution.py:240
  22.9 3.9 %collective-permute-start.7 = (bf16[16,1024]{1,0:T(8,128)(2,1)S(1)}, bf16[16,1024]{1,0:T(8,128)(2,1)S(1)}, u32[]{:S(2)}, u32[]{:S(2)}) collective-permute-start(bf16[16,1024]{1,0:T(8,128)(2,1)S(1)} %get-tuple-element.32), channel_id=1, source_target_pairs={{0,13},{1,12},{4,0},{5,1},{8,4},{9,5},{12,8},{13,9},{2,15},{3,14},... | collective-permute-start | bytes 98312 | tf_op jit(solution)/shard_map/ppermute | solution.py:240

commit v8 on v7

--- a/solution.py
+++ b/solution.py
@@ -110,12 +110,12 @@
                 for v, r, c, (_, _, sign, _) in zip(values, rows, columns, chains)
             ]
         values = inner
-    lane = lax.broadcasted_iota(jnp.int32, (count, LANES), 1)
-    for row, forward, partner in zip(groups, values[0::2], values[1::2]):
-        site = lax.broadcasted_iota(jnp.int32, (count, LANES), 0) + base_ref[0] + row
-        for j, (f, p) in enumerate(zip(forward, partner)):
-            term = jnp.where(lane + j * LANES == site, 0.0, f * p)
-            out_ref[row : row + count, j * LANES : (j + 1) * LANES] = term.astype(out_ref.dtype)
+    row = lax.broadcasted_iota(jnp.int32, (total, LANES), 0) + base_ref[0]
+    lane = lax.broadcasted_iota(jnp.int32, (total, LANES), 1)
+    for j in range(len(coefs[0])):
+        products = [f[j] * p[j] for f, p in zip(values[0::2], values[1::2])]
+        term = jnp.where(lane + j * LANES == row, 0.0, jnp.concatenate(products))
+        out_ref[:, j * LANES : (j + 1) * LANES] = term.astype(out_ref.dtype)
 
 
 def measured(base, forward, partner, rates):

time: 27.6 us -> 27.6 us (level)
  no operation moved by 1% of the time
where the time goes in v8:
time: 27.6 us; the launch traced here: 27.5 us
  starting transfers between devices  10 us (36%)
  waiting for transfers between devices  8.4 us (30%)
  Pallas kernels  5.8 us (21%)
  matrix products  2.32 us (8%)
  other arithmetic  0.72 us (3%)
    ppermute x5, starting transfers between devices, sent(): return lax.ppermute(term, ('tm', 'col'), route(targets))  5.98 us
    ppermute x3, waiting for transfers between devices, per_device(): low = lax.ppermute(low, ('tm', 'col'), around)  4.99 us
    ppermute x3, starting transfers between devices, per_device(): low = lax.ppermute(low, ('tm', 'col'), around)  4.06 us
    ppermute x5, waiting for transfers between devices, sent(): return lax.ppermute(term, ('tm', 'col'), route(targets))  3.41 us
    pallas_call x4, Pallas kernels, measured(): pl.pallas_call(functools.partial(measure_kernel, math.isqrt(forward.shape...  2.77 us
    pallas_call x1, Pallas kernels, turned(): pl.pallas_call(turned_kernel, out_shape=jax.ShapeDtypeStruct(dense.shape[...  1.89 us
    dot_general x3, matrix products, per_device(): jnp.dot(low[ref_rows:], inverse_map, preferred_element_type=jnp.float32)  1.17 us
    dot_general x3, matrix products, per_device(): jnp.dot(low[:ref_rows], forward_map, preferred_element_type=jnp.float32)  1.16 us
  transfers between devices with their start and end apart: 8, of which 6 were waited for; matrix products, arithmetic and copies ran while one was open for 3% of the time, Pallas kernels for 17%

profile of v8, /device:TPU:0, one launch (start us, length us, event | category | flops | bytes accessed | tf_op | source)
XLA Modules:
  0.0 27.5 jit_solution(6983386556471589857)
XLA Ops:
  0.0 0.0 copy-start
  0.0 1.1 %shard_map.64 = (bf16[16,1024]{1,0:T(8,128)(2,1)S(1)}, bf16[16,1024]{1,0:T(8,128)(2,1)S(1)}, f32[16,1024]{1,0:T(8,128)S(1)}, f32[16,1024]{1,0:T(8,128)S(1)}) custom-call(s32[1]{0:T(128)} %bitcast.1.base_ref, f32[16,1024]{1,0:T(8,128)} %bitcast.43, f32[16,1024]{1,0:T(8,128)} %bitcast.44), custom_call_target="tpu_custom_call" | custom-call | flops 65536 | bytes 196608 | tf_op jit(solution)/shard_map/pallas_call | solution.py:152
  1.1 3.1 %collective-permute-start = (bf16[32,1024]{1,0:T(8,128)(2,1)S(1)}, bf16[32,1024]{1,0:T(8,128)(2,1)S(1)}, u32[]{:S(2)}, u32[]{:S(2)}) collective-permute-start(bf16[32,1024]{1,0:T(8,128)(2,1)S(1)} %pad_maximum_fusion.1), channel_id=1, source_target_pairs={{0,4},{1,5},{4,8},{5,9},{8,12},{9,13},{12,1},{13,0},{2,6},{3,7},{6... | collective-permute-start | bytes 196616 | tf_op jit(solution)/shard_map/ppermute | solution.py:223
  4.2 1.9 %shard_map.65 = bf16[1024,1024]{1,0:T(8,128)(2,1)S(1)} custom-call(bf16[1024,1024]{1,0:T(8,128)(2,1)} %bitcast.42), custom_call_target="tpu_custom_call" | custom-call | flops 1048576 | bytes 4194304 | tf_op jit(solution)/shard_map/pallas_call | solution.py:183
  6.1 0.0 copy-start.1
  6.1 0.0 copy-start.2
  6.1 1.5 %collective-permute-done = bf16[32,1024]{1,0:T(8,128)(2,1)S(1)} collective-permute-done((bf16[32,1024]{1,0:T(8,128)(2,1)S(1)}, bf16[32,1024]{1,0:T(8,128)(2,1)S(1)}, u32[]{:S(2)}, u32[]{:S(2)}) %collective-permute-start) | collective-permute-done | bytes 65568 | tf_op jit(solution)/shard_map/ppermute | solution.py:223
  7.6 0.4 %fusion.16 = (bf16[16,1024]{1,0:T(8,128)(2,1)S(1)}, f32[16,1024]{1,0:T(8,128)S(1)}) fusion(bf16[1024,1024]{1,0:T(8,128)(2,1)S(1)} %shard_map.65, bf16[32,1024]{1,0:T(8,128)(2,1)S(1)} %collective-permute-done), kind=kOutput, calls=%fused_computation.26 | convolution fusion | flops 33570816 | bytes 2228224 | tf_op jit(solution)/shard_map/dot_general | solution.py:224
  8.0 0.0 copy-done
  8.0 0.4 %fusion.15 = (bf16[16,1024]{1,0:T(8,128)(2,1)S(1)}, f32[16,1024]{1,0:T(8,128)S(1)}) fusion(bf16[1,1024,1024]{2,1,0:T(8,128)(2,1)S(1)} %copy-done, bf16[32,1024]{1,0:T(8,128)(2,1)S(1)} %collective-permute-done), kind=kOutput, calls=%fused_computation.25 | convolution fusion | flops 33570816 | bytes 2228224 | tf_op jit(solution)/shard_map/dot_general | solution.py:225
  8.4 0.9 %collective-permute-start.1 = (bf16[32,1024]{1,0:T(8,128)(2,1)S(1)}, bf16[32,1024]{1,0:T(8,128)(2,1)S(1)}, u32[]{:S(2)}, u32[]{:S(2)}) collective-permute-start(bf16[32,1024]{1,0:T(8,128)(2,1)S(1)} %pad_maximum_fusion.2), channel_id=1, source_target_pairs={{0,4},{1,5},{4,8},{5,9},{8,12},{9,13},{12,1},{13,0},{2,6},{3,7},{6... | collective-permute-start | bytes 196616 | tf_op jit(solution)/shard_map/ppermute | solution.py:223
  9.3 0.0 copy-done.1
  9.3 0.0 copy-done.2
  9.3 0.1 shard_map.66.factors_ref
  9.4 0.7 %shard_map.67 = bf16[16,1024]{1,0:T(8,128)(2,1)S(1)} custom-call(s32[1]{0:T(128)} %bitcast.1.base_ref, f32[16,1024]{1,0:T(8,128)S(1)} %get-tuple-element.23.forward_ref, f32[16,1024]{1,0:T(8,128)S(1)} %get-tuple-element.24.partner_ref, f32[8,1024]{1,0:T(8,128)S(1)} %shard_map.66.factors_ref), custom_call_target="tpu_custom_call" | custom-call | flops 737280000 | bytes 196608 | tf_op jit(solution)/shard_map/pallas_call | solution.py:122
  10.1 0.7 %shard_map.68 = bf16[16,1024]{1,0:T(8,128)(2,1)S(1)} custom-call(s32[1]{0:T(128)} %bitcast.7.base_ref, f32[16,1024]{1,0:T(8,128)S(1)} %get-tuple-element.40.forward_ref, f32[16,1024]{1,0:T(8,128)S(1)} %get-tuple-element.38.partner_ref, f32[8,1024]{1,0:T(8,128)S(1)} %shard_map.66.factors_ref), custom_call_target="tpu_custom_call" | custom-call | flops 737280000 | bytes 196608 | tf_op jit(solution)/shard_map/pallas_call | solution.py:122
  10.8 3.1 %collective-permute-done.1 = bf16[32,1024]{1,0:T(8,128)(2,1)S(1)} collective-permute-done((bf16[32,1024]{1,0:T(8,128)(2,1)S(1)}, bf16[32,1024]{1,0:T(8,128)(2,1)S(1)}, u32[]{:S(2)}, u32[]{:S(2)}) %collective-permute-start.1) | collective-permute-done | bytes 65568 | tf_op jit(solution)/shard_map/ppermute | solution.py:223
  13.9 0.4 %fusion.17 = (bf16[16,1024]{1,0:T(8,128)(2,1)S(1)}, f32[16,1024]{1,0:T(8,128)S(1)}) fusion(bf16[1,1024,1024]{2,1,0:T(8,128)(2,1)S(1)} %copy-done, bf16[32,1024]{1,0:T(8,128)(2,1)S(1)} %collective-permute-done.1), kind=kOutput, calls=%fused_computation.27 | convolution fusion | flops 33570816 | bytes 2228224 | tf_op jit(solution)/shard_map/dot_general | solution.py:225
  14.3 0.4 %fusion.18 = (bf16[16,1024]{1,0:T(8,128)(2,1)S(1)}, f32[16,1024]{1,0:T(8,128)S(1)}) fusion(bf16[1024,1024]{1,0:T(8,128)(2,1)S(1)} %shard_map.65, bf16[32,1024]{1,0:T(8,128)(2,1)S(1)} %collective-permute-done.1), kind=kOutput, calls=%fused_computation.28 | convolution fusion | flops 33570816 | bytes 2228224 | tf_op jit(solution)/shard_map/dot_general | solution.py:224
  14.7 0.1 collective-permute-start.2
  14.8 0.7 %shard_map.70 = bf16[16,1024]{1,0:T(8,128)(2,1)S(1)} custom-call(s32[1]{0:T(128)} %bitcast.10.base_ref, f32[16,1024]{1,0:T(8,128)S(1)} %get-tuple-element.44.forward_ref, f32[16,1024]{1,0:T(8,128)S(1)} %get-tuple-element.42.partner_ref, f32[8,1024]{1,0:T(8,128)S(1)} %shard_map.66.factors_ref), custom_call_target="tpu_custom_call" | custom-call | flops 737280000 | bytes 196608 | tf_op jit(solution)/shard_map/pallas_call | solution.py:122
  15.5 0.1 collective-permute-start.3
  15.6 4.4 %collective-permute-start.4 = (bf16[16,1024]{1,0:T(8,128)(2,1)S(1)}, bf16[16,1024]{1,0:T(8,128)(2,1)S(1)}, u32[]{:S(2)}, u32[]{:S(2)}) collective-permute-start(bf16[16,1024]{1,0:T(8,128)(2,1)S(1)} %get-tuple-element.36), channel_id=1, source_target_pairs={{0,5},{1,4},{4,9},{5,8},{8,13},{9,12},{12,0},{13,1},{2,7},{3,6},{6... | collective-permute-start | bytes 98312 | tf_op jit(solution)/shard_map/ppermute | solution.py:240
  19.9 0.4 %collective-permute-done.2 = bf16[32,1024]{1,0:T(8,128)(2,1)S(1)} collective-permute-done((bf16[32,1024]{1,0:T(8,128)(2,1)S(1)}, bf16[32,1024]{1,0:T(8,128)(2,1)S(1)}, u32[]{:S(2)}, u32[]{:S(2)}) %collective-permute-start.2) | collective-permute-done | bytes 65568 | tf_op jit(solution)/shard_map/ppermute | solution.py:223
  20.3 0.4 %fusion.7.forward_ref = f32[16,1024]{1,0:T(8,128)S(1)} fusion(bf16[1024,1024]{1,0:T(8,128)(2,1)S(1)} %shard_map.65, bf16[32,1024]{1,0:T(8,128)(2,1)S(1)} %collective-permute-done.2), kind=kOutput, calls=%fused_computation.12 | convolution fusion | flops 33554432 | bytes 2195456 | tf_op jit(solution)/shard_map/dot_general | solution.py:224
  20.7 0.4 %fusion.partner_ref = f32[16,1024]{1,0:T(8,128)S(1)} fusion(bf16[1,1024,1024]{2,1,0:T(8,128)(2,1)S(1)} %copy-done, bf16[32,1024]{1,0:T(8,128)(2,1)S(1)} %collective-permute-done.2), kind=kOutput, calls=%fused_computation | convolution fusion | flops 33554432 | bytes 2195456 | tf_op jit(solution)/shard_map/dot_general | solution.py:225
  21.1 0.7 %shard_map.69 = bf16[16,1024]{1,0:T(8,128)(2,1)S(1)} custom-call(s32[1]{0:T(128)} %bitcast.base_ref, f32[16,1024]{1,0:T(8,128)S(1)} %fusion.7.forward_ref, f32[16,1024]{1,0:T(8,128)S(1)} %fusion.partner_ref, f32[8,1024]{1,0:T(8,128)S(1)} %shard_map.66.factors_ref), custom_call_target="tpu_custom_call" | custom-call | flops 737280000 | bytes 196608 | tf_op jit(solution)/shard_map/pallas_call | solution.py:122
  21.8 1.0 %collective-permute-start.5 = (bf16[16,1024]{1,0:T(8,128)(2,1)S(1)}, bf16[16,1024]{1,0:T(8,128)(2,1)S(1)}, u32[]{:S(2)}, u32[]{:S(2)}) collective-permute-start(bf16[16,1024]{1,0:T(8,128)(2,1)S(1)} %get-tuple-element.30), channel_id=1, source_target_pairs={{0,1},{1,0},{4,13},{5,12},{8,9},{9,8},{12,5},{13,4},{2,3},{3,2},{6... | collective-permute-start | bytes 98312 | tf_op jit(solution)/shard_map/ppermute | solution.py:240
  22.8 0.1 collective-permute-start.6
  22.9 0.5 %collective-permute-start.7 = (bf16[16,1024]{1,0:T(8,128)(2,1)S(1)}, bf16[16,1024]{1,0:T(8,128)(2,1)S(1)}, u32[]{:S(2)}, u32[]{:S(2)}) collective-permute-start(bf16[16,1024]{1,0:T(8,128)(2,1)S(1)} %get-tuple-element.32), channel_id=1, source_target_pairs={{0,13},{1,12},{4,0},{5,1},{8,4},{9,5},{12,8},{13,9},{2,15},{3,14},... | collective-permute-start | bytes 98312 | tf_op jit(solution)/shard_map/ppermute | solution.py:240
  23.4 0.0 collective-permute-done.3
  23.4 0.0 collective-permute-done.4
  23.4 0.3 collective-permute-done.5
  23.7 0.3 %collective-permute-done.6 = bf16[16,1024]{1,0:T(8,128)(2,1)S(1)} collective-permute-done((bf16[16,1024]{1,0:T(8,128)(2,1)S(1)}, bf16[16,1024]{1,0:T(8,128)(2,1)S(1)}, u32[]{:S(2)}, u32[]{:S(2)}) %collective-permute-start.6) | collective-permute-done | bytes 32800 | tf_op jit(solution)/shard_map/ppermute | solution.py:240
  24.0 2.8 %collective-permute-done.7 = bf16[16,1024]{1,0:T(8,128)(2,1)S(1)} collective-permute-done((bf16[16,1024]{1,0:T(8,128)(2,1)S(1)}, bf16[16,1024]{1,0:T(8,128)(2,1)S(1)}, u32[]{:S(2)}, u32[]{:S(2)}) %collective-permute-start.7) | collective-permute-done | bytes 32800 | tf_op jit(solution)/shard_map/ppermute | solution.py:240
  26.8 0.7 %multiply_bitcast_fusion = f32[1,16,1024]{2,1,0:T(8,128)} fusion(bf16[16,1024]{1,0:T(8,128)(2,1)S(1)} %collective-permute-done.7, bf16[16,1024]{1,0:T(8,128)(2,1)S(1)} %collective-permute-done.4, bf16[16,1024]{1,0:T(8,128)(2,1)S(1)} %collective-permute-done.3, bf16[16,1024]{1,0:T(8,128)(2,1)S(1)} %shard_map.69, ...), kind=kLoop, calls=%fused_computation.10 | loop fusion | flops 262144 | bytes 294917 | tf_op jit(solution)/shard_map/broadcast_in_dim | solution.py:263
  (6 shorter events, 0.1 us)
Async XLA Ops:
  0.0 8.0 %copy-start = (bf16[1,1024,1024]{2,1,0:T(8,128)(2,1)S(1)}, bf16[1,1024,1024]{2,1,0:T(8,128)(2,1)}, u32[]{:S(2)}) copy-start(bf16[1,1024,1024]{2,1,0:T(8,128)(2,1)} %param.7) | copy-start | bytes 6291460
  1.1 6.5 %collective-permute-start = (bf16[32,1024]{1,0:T(8,128)(2,1)S(1)}, bf16[32,1024]{1,0:T(8,128)(2,1)S(1)}, u32[]{:S(2)}, u32[]{:S(2)}) collective-permute-start(bf16[32,1024]{1,0:T(8,128)(2,1)S(1)} %pad_maximum_fusion.1), channel_id=1, source_target_pairs={{0,4},{1,5},{4,8},{5,9},{8,12},{9,13},{12,1},{13,0},{2,6},{3,7},{6... | collective-permute-start | bytes 196616 | tf_op jit(solution)/shard_map/ppermute | solution.py:223
  6.1 3.2 %copy-start.1 = (s32[1,2,1024]{2,1,0:T(2,128)S(1)}, s32[1,2,1024]{2,1,0:T(2,128)}, u32[]{:S(2)}) copy-start(s32[1,2,1024]{2,1,0:T(2,128)} %param.10) | copy-start | bytes 24580
  6.1 3.2 %copy-start.2 = (s32[2,1024]{1,0:T(2,128)S(1)}, s32[2,1024]{1,0:T(2,128)}, u32[]{:S(2)}) copy-start(s32[2,1024]{1,0:T(2,128)} %bonds_ref) | copy-start | bytes 24580
  8.4 5.5 %collective-permute-start.1 = (bf16[32,1024]{1,0:T(8,128)(2,1)S(1)}, bf16[32,1024]{1,0:T(8,128)(2,1)S(1)}, u32[]{:S(2)}, u32[]{:S(2)}) collective-permute-start(bf16[32,1024]{1,0:T(8,128)(2,1)S(1)} %pad_maximum_fusion.2), channel_id=1, source_target_pairs={{0,4},{1,5},{4,8},{5,9},{8,12},{9,13},{12,1},{13,0},{2,6},{3,7},{6... | collective-permute-start | bytes 196616 | tf_op jit(solution)/shard_map/ppermute | solution.py:223
  14.7 5.6 %collective-permute-start.2 = (bf16[32,1024]{1,0:T(8,128)(2,1)S(1)}, bf16[32,1024]{1,0:T(8,128)(2,1)S(1)}, u32[]{:S(2)}, u32[]{:S(2)}) collective-permute-start(bf16[32,1024]{1,0:T(8,128)(2,1)S(1)} %pad_maximum_fusion.3), channel_id=1, source_target_pairs={{0,4},{1,5},{4,8},{5,9},{8,12},{9,13},{12,1},{13,0},{2,6},{3,7},{6... | collective-permute-start | bytes 196616 | tf_op jit(solution)/shard_map/ppermute | solution.py:223
  15.5 7.9 %collective-permute-start.3 = (bf16[16,1024]{1,0:T(8,128)(2,1)S(1)}, bf16[16,1024]{1,0:T(8,128)(2,1)S(1)}, u32[]{:S(2)}, u32[]{:S(2)}) collective-permute-start(bf16[16,1024]{1,0:T(8,128)(2,1)S(1)} %get-tuple-element.35), channel_id=1, source_target_pairs={{0,9},{1,8},{4,13},{5,12},{8,0},{9,1},{12,4},{13,5},{2,11},{3,10},... | collective-permute-start | bytes 98312 | tf_op jit(solution)/shard_map/ppermute | solution.py:240
  15.6 7.8 %collective-permute-start.4 = (bf16[16,1024]{1,0:T(8,128)(2,1)S(1)}, bf16[16,1024]{1,0:T(8,128)(2,1)S(1)}, u32[]{:S(2)}, u32[]{:S(2)}) collective-permute-start(bf16[16,1024]{1,0:T(8,128)(2,1)S(1)} %get-tuple-element.36), channel_id=1, source_target_pairs={{0,5},{1,4},{4,9},{5,8},{8,13},{9,12},{12,0},{13,1},{2,7},{3,6},{6... | collective-permute-start | bytes 98312 | tf_op jit(solution)/shard_map/ppermute | solution.py:240
  21.8 1.8 %collective-permute-start.5 = (bf16[16,1024]{1,0:T(8,128)(2,1)S(1)}, bf16[16,1024]{1,0:T(8,128)(2,1)S(1)}, u32[]{:S(2)}, u32[]{:S(2)}) collective-permute-start(bf16[16,1024]{1,0:T(8,128)(2,1)S(1)} %get-tuple-element.30), channel_id=1, source_target_pairs={{0,1},{1,0},{4,13},{5,12},{8,9},{9,8},{12,5},{13,4},{2,3},{3,2},{6... | collective-permute-start | bytes 98312 | tf_op jit(solution)/shard_map/ppermute | solution.py:240
  22.8 1.2 %collective-permute-start.6 = (bf16[16,1024]{1,0:T(8,128)(2,1)S(1)}, bf16[16,1024]{1,0:T(8,128)(2,1)S(1)}, u32[]{:S(2)}, u32[]{:S(2)}) collective-permute-start(bf16[16,1024]{1,0:T(8,128)(2,1)S(1)} %shard_map.69), channel_id=1, source_target_pairs={{0,1},{1,0},{4,5},{5,4},{8,13},{9,12},{12,9},{13,8},{2,3},{3,2},{6... | collective-permute-start | bytes 98312 | tf_op jit(solution)/shard_map/ppermute | solution.py:240
  22.9 3.9 %collective-permute-start.7 = (bf16[16,1024]{1,0:T(8,128)(2,1)S(1)}, bf16[16,1024]{1,0:T(8,128)(2,1)S(1)}, u32[]{:S(2)}, u32[]{:S(2)}) collective-permute-start(bf16[16,1024]{1,0:T(8,128)(2,1)S(1)} %get-tuple-element.32), channel_id=1, source_target_pairs={{0,13},{1,12},{4,0},{5,1},{8,4},{9,5},{12,8},{13,9},{2,15},{3,14},... | collective-permute-start | bytes 98312 | tf_op jit(solution)/shard_map/ppermute | solution.py:240

commit v9 on v8

--- a/solution.py
+++ b/solution.py
@@ -136,14 +136,14 @@
     ]
     for copy in copies:
         copy.start()
-    for copy in copies:
-        copy.wait()
+    copies[0].wait()
+    forward_low[...] = forward_ref[...].astype(forward_low.dtype)
+    copies[1].wait()
     row = lax.broadcasted_iota(jnp.int32, rows.shape, 0) + base_ref[0]
     lane = lax.broadcasted_iota(jnp.int32, rows.shape, 1)
     partner = jnp.where(lane == row, rows[...] - 1.0, rows[...])
     partner_ref[...] = partner
     partner_low[...] = partner.astype(partner_low.dtype)
-    forward_low[...] = forward_ref[...].astype(forward_low.dtype)
 
 
 def packed(base, columns, rows):
@@ -189,6 +189,25 @@
         compiler_params=params(8),
         cost_estimate=cost(dense.size, 4 * dense.size),
     )(pltpu.with_memory_space_constraint(dense, pltpu.HBM))
+
+
+def finished_kernel(scale, known_ref, arrived_ref, out_ref, held, sent):
+    held[...] = (known_ref[...] + arrived_ref[...].astype(jnp.float32)) * scale
+    copy = pltpu.make_async_copy(held, out_ref, sent.at[0])
+    copy.start()
+    copy.wait()
+
+
+def finished(known, arrived, scale):
+    return pl.pallas_call(
+        functools.partial(finished_kernel, scale),
+        out_shape=jax.ShapeDtypeStruct(known.shape, known.dtype),
+        in_specs=[VMEM, VMEM],
+        out_specs=ANY,
+        scratch_shapes=[pltpu.VMEM(known.shape, known.dtype), pltpu.SemaphoreType.DMA((1,))],
+        compiler_params=params(),
+        cost_estimate=cost(3 * known.size, 10 * known.size),
+    )(known, arrived)
 
 
 def per_device(cluster_maps, inverse_maps, seed_columns, seed_rows, ising_field, hop_bonds):
@@ -256,11 +275,11 @@
         term = sent(term, {**swap, k: (last, -1), last: (k, 1)})
         return jnp.where(anchor == last, term, 0.0).astype(jnp.float32)
 
-    total = total + sent_last(soonest, 1)
     for k in range(last - 1, 1, -1):
         total = total + sent_last(late, k)
-    total = total + sent(behind, shifted(-1)).astype(jnp.float32)
-    return (total * (sites / clusters))[None]
+    total = total + sent_last(soonest, 1)
+    arrived = sent(behind, shifted(-1))
+    return finished(total, arrived, sites / clusters)[None]
 
 
 def solution(mesh):

time: 27.6 us -> 27.6 us (level)
  starting transfers between devices: 10 us -> 10.7 us
  waiting for transfers between devices: 8.4 us -> 7.71 us
  Pallas kernels: 5.8 us -> 6.44 us
  other arithmetic: 0.72 us -> 0.09 us
    ppermute x5, waiting for transfers between devices: 3.41 us -> 2.72 us  [sent(): return lax.ppermute(term, ('tm', 'col'), route(targets))]
    broadcast_in_dim x1 -> x0, other arithmetic: 0.67 us -> none  [per_device(): return (total * (sites / clusters))[None]]
    pallas_call x0 -> x1, Pallas kernels: none -> 0.65 us  [finished(): pl.pallas_call(functools.partial(finished_kernel, scale), out_shape=jax.S...]
    ppermute x5, starting transfers between devices: 5.98 us -> 6.62 us  [sent(): return lax.ppermute(term, ('tm', 'col'), route(targets))]
  transfers between devices with their start and end apart: 8 -> 8, of which waited for: 6 -> 4; matrix products, arithmetic and copies ran while one was open for 3% -> 3% of each run, Pallas kernels for 17% -> 17%
where the time goes in v9:
time: 27.6 us; the launch traced here: 27.4 us
  starting transfers between devices  10.7 us (39%)
  waiting for transfers between devices  7.71 us (28%)
  Pallas kernels  6.44 us (23%)
  matrix products  2.32 us (8%)
    ppermute x5, starting transfers between devices, sent(): return lax.ppermute(term, ('tm', 'col'), route(targets))  6.62 us
    ppermute x3, waiting for transfers between devices, per_device(): low = lax.ppermute(low, ('tm', 'col'), around)  4.99 us
    ppermute x3, starting transfers between devices, per_device(): low = lax.ppermute(low, ('tm', 'col'), around)  4.06 us
    pallas_call x4, Pallas kernels, measured(): pl.pallas_call(functools.partial(measure_kernel, math.isqrt(forward.shape...  2.77 us
    ppermute x5, waiting for transfers between devices, sent(): return lax.ppermute(term, ('tm', 'col'), route(targets))  2.72 us
    pallas_call x1, Pallas kernels, turned(): pl.pallas_call(turned_kernel, out_shape=jax.ShapeDtypeStruct(dense.shape[...  1.89 us
    dot_general x3, matrix products, per_device(): jnp.dot(low[ref_rows:], inverse_map, preferred_element_type=jnp.float32)  1.17 us
    dot_general x3, matrix products, per_device(): jnp.dot(low[:ref_rows], forward_map, preferred_element_type=jnp.float32)  1.16 us
  transfers between devices with their start and end apart: 8, of which 4 were waited for; matrix products, arithmetic and copies ran while one was open for 3% of the time, Pallas kernels for 17%

profile of v9, /device:TPU:0, one launch (start us, length us, event | category | flops | bytes accessed | tf_op | source)
XLA Modules:
  0.0 27.4 jit_solution(15088004224437923802)
XLA Ops:
  0.0 0.0 copy-start
  0.0 1.0 %shard_map.64 = (bf16[16,1024]{1,0:T(8,128)(2,1)S(1)}, bf16[16,1024]{1,0:T(8,128)(2,1)S(1)}, f32[16,1024]{1,0:T(8,128)S(1)}, f32[16,1024]{1,0:T(8,128)S(1)}) custom-call(s32[1]{0:T(128)} %bitcast.1.base_ref, f32[16,1024]{1,0:T(8,128)} %bitcast.42, f32[16,1024]{1,0:T(8,128)} %bitcast.43), custom_call_target="tpu_custom_call" | custom-call | flops 65536 | bytes 196608 | tf_op jit(solution)/shard_map/pallas_call | solution.py:152
  1.1 3.1 %collective-permute-start = (bf16[32,1024]{1,0:T(8,128)(2,1)S(1)}, bf16[32,1024]{1,0:T(8,128)(2,1)S(1)}, u32[]{:S(2)}, u32[]{:S(2)}) collective-permute-start(bf16[32,1024]{1,0:T(8,128)(2,1)S(1)} %pad_maximum_fusion.1), channel_id=1, source_target_pairs={{0,4},{1,5},{4,8},{5,9},{8,12},{9,13},{12,1},{13,0},{2,6},{3,7},{6... | collective-permute-start | bytes 196616 | tf_op jit(solution)/shard_map/ppermute | solution.py:242
  4.2 1.9 %shard_map.65 = bf16[1024,1024]{1,0:T(8,128)(2,1)S(1)} custom-call(bf16[1024,1024]{1,0:T(8,128)(2,1)} %bitcast.41), custom_call_target="tpu_custom_call" | custom-call | flops 1048576 | bytes 4194304 | tf_op jit(solution)/shard_map/pallas_call | solution.py:183
  6.1 0.0 copy-start.1
  6.1 0.0 copy-start.2
  6.1 1.5 %collective-permute-done = bf16[32,1024]{1,0:T(8,128)(2,1)S(1)} collective-permute-done((bf16[32,1024]{1,0:T(8,128)(2,1)S(1)}, bf16[32,1024]{1,0:T(8,128)(2,1)S(1)}, u32[]{:S(2)}, u32[]{:S(2)}) %collective-permute-start) | collective-permute-done | bytes 65568 | tf_op jit(solution)/shard_map/ppermute | solution.py:242
  7.6 0.4 %fusion.16 = (bf16[16,1024]{1,0:T(8,128)(2,1)S(1)}, f32[16,1024]{1,0:T(8,128)S(1)}) fusion(bf16[1024,1024]{1,0:T(8,128)(2,1)S(1)} %shard_map.65, bf16[32,1024]{1,0:T(8,128)(2,1)S(1)} %collective-permute-done), kind=kOutput, calls=%fused_computation.26 | convolution fusion | flops 33570816 | bytes 2228224 | tf_op jit(solution)/shard_map/dot_general | solution.py:243
  8.0 0.0 copy-done
  8.0 0.4 %fusion.15 = (bf16[16,1024]{1,0:T(8,128)(2,1)S(1)}, f32[16,1024]{1,0:T(8,128)S(1)}) fusion(bf16[1,1024,1024]{2,1,0:T(8,128)(2,1)S(1)} %copy-done, bf16[32,1024]{1,0:T(8,128)(2,1)S(1)} %collective-permute-done), kind=kOutput, calls=%fused_computation.25 | convolution fusion | flops 33570816 | bytes 2228224 | tf_op jit(solution)/shard_map/dot_general | solution.py:244
  8.4 0.9 %collective-permute-start.1 = (bf16[32,1024]{1,0:T(8,128)(2,1)S(1)}, bf16[32,1024]{1,0:T(8,128)(2,1)S(1)}, u32[]{:S(2)}, u32[]{:S(2)}) collective-permute-start(bf16[32,1024]{1,0:T(8,128)(2,1)S(1)} %pad_maximum_fusion.2), channel_id=1, source_target_pairs={{0,4},{1,5},{4,8},{5,9},{8,12},{9,13},{12,1},{13,0},{2,6},{3,7},{6... | collective-permute-start | bytes 196616 | tf_op jit(solution)/shard_map/ppermute | solution.py:242
  9.3 0.0 copy-done.1
  9.3 0.0 copy-done.2
  9.3 0.1 shard_map.66.factors_ref
  9.4 0.7 %shard_map.67 = bf16[16,1024]{1,0:T(8,128)(2,1)S(1)} custom-call(s32[1]{0:T(128)} %bitcast.1.base_ref, f32[16,1024]{1,0:T(8,128)S(1)} %get-tuple-element.23.forward_ref, f32[16,1024]{1,0:T(8,128)S(1)} %get-tuple-element.24.partner_ref, f32[8,1024]{1,0:T(8,128)S(1)} %shard_map.66.factors_ref), custom_call_target="tpu_custom_call" | custom-call | flops 737280000 | bytes 196608 | tf_op jit(solution)/shard_map/pallas_call | solution.py:122
  10.1 0.7 %shard_map.68 = bf16[16,1024]{1,0:T(8,128)(2,1)S(1)} custom-call(s32[1]{0:T(128)} %bitcast.7.base_ref, f32[16,1024]{1,0:T(8,128)S(1)} %get-tuple-element.40.forward_ref, f32[16,1024]{1,0:T(8,128)S(1)} %get-tuple-element.38.partner_ref, f32[8,1024]{1,0:T(8,128)S(1)} %shard_map.66.factors_ref), custom_call_target="tpu_custom_call" | custom-call | flops 737280000 | bytes 196608 | tf_op jit(solution)/shard_map/pallas_call | solution.py:122
  10.8 3.1 %collective-permute-done.1 = bf16[32,1024]{1,0:T(8,128)(2,1)S(1)} collective-permute-done((bf16[32,1024]{1,0:T(8,128)(2,1)S(1)}, bf16[32,1024]{1,0:T(8,128)(2,1)S(1)}, u32[]{:S(2)}, u32[]{:S(2)}) %collective-permute-start.1) | collective-permute-done | bytes 65568 | tf_op jit(solution)/shard_map/ppermute | solution.py:242
  13.9 0.4 %fusion.17 = (bf16[16,1024]{1,0:T(8,128)(2,1)S(1)}, f32[16,1024]{1,0:T(8,128)S(1)}) fusion(bf16[1,1024,1024]{2,1,0:T(8,128)(2,1)S(1)} %copy-done, bf16[32,1024]{1,0:T(8,128)(2,1)S(1)} %collective-permute-done.1), kind=kOutput, calls=%fused_computation.27 | convolution fusion | flops 33570816 | bytes 2228224 | tf_op jit(solution)/shard_map/dot_general | solution.py:244
  14.3 0.4 %fusion.18 = (bf16[16,1024]{1,0:T(8,128)(2,1)S(1)}, f32[16,1024]{1,0:T(8,128)S(1)}) fusion(bf16[1024,1024]{1,0:T(8,128)(2,1)S(1)} %shard_map.65, bf16[32,1024]{1,0:T(8,128)(2,1)S(1)} %collective-permute-done.1), kind=kOutput, calls=%fused_computation.28 | convolution fusion | flops 33570816 | bytes 2228224 | tf_op jit(solution)/shard_map/dot_general | solution.py:243
  14.7 0.1 collective-permute-start.2
  14.8 0.7 %shard_map.70 = bf16[16,1024]{1,0:T(8,128)(2,1)S(1)} custom-call(s32[1]{0:T(128)} %bitcast.10.base_ref, f32[16,1024]{1,0:T(8,128)S(1)} %get-tuple-element.44.forward_ref, f32[16,1024]{1,0:T(8,128)S(1)} %get-tuple-element.42.partner_ref, f32[8,1024]{1,0:T(8,128)S(1)} %shard_map.66.factors_ref), custom_call_target="tpu_custom_call" | custom-call | flops 737280000 | bytes 196608 | tf_op jit(solution)/shard_map/pallas_call | solution.py:122
  15.5 0.1 collective-permute-start.3
  15.6 4.4 %collective-permute-start.4 = (bf16[16,1024]{1,0:T(8,128)(2,1)S(1)}, bf16[16,1024]{1,0:T(8,128)(2,1)S(1)}, u32[]{:S(2)}, u32[]{:S(2)}) collective-permute-start(bf16[16,1024]{1,0:T(8,128)(2,1)S(1)} %get-tuple-element.36), channel_id=1, source_target_pairs={{0,5},{1,4},{4,9},{5,8},{8,13},{9,12},{12,0},{13,1},{2,7},{3,6},{6... | collective-permute-start | bytes 98312 | tf_op jit(solution)/shard_map/ppermute | solution.py:259
  19.9 0.4 %collective-permute-done.2 = bf16[32,1024]{1,0:T(8,128)(2,1)S(1)} collective-permute-done((bf16[32,1024]{1,0:T(8,128)(2,1)S(1)}, bf16[32,1024]{1,0:T(8,128)(2,1)S(1)}, u32[]{:S(2)}, u32[]{:S(2)}) %collective-permute-start.2) | collective-permute-done | bytes 65568 | tf_op jit(solution)/shard_map/ppermute | solution.py:242
  20.3 0.4 %fusion.7.forward_ref = f32[16,1024]{1,0:T(8,128)S(1)} fusion(bf16[1024,1024]{1,0:T(8,128)(2,1)S(1)} %shard_map.65, bf16[32,1024]{1,0:T(8,128)(2,1)S(1)} %collective-permute-done.2), kind=kOutput, calls=%fused_computation.12 | convolution fusion | flops 33554432 | bytes 2195456 | tf_op jit(solution)/shard_map/dot_general | solution.py:243
  20.7 0.4 %fusion.partner_ref = f32[16,1024]{1,0:T(8,128)S(1)} fusion(bf16[1,1024,1024]{2,1,0:T(8,128)(2,1)S(1)} %copy-done, bf16[32,1024]{1,0:T(8,128)(2,1)S(1)} %collective-permute-done.2), kind=kOutput, calls=%fused_computation | convolution fusion | flops 33554432 | bytes 2195456 | tf_op jit(solution)/shard_map/dot_general | solution.py:244
  21.1 0.7 %shard_map.69 = bf16[16,1024]{1,0:T(8,128)(2,1)S(1)} custom-call(s32[1]{0:T(128)} %bitcast.base_ref, f32[16,1024]{1,0:T(8,128)S(1)} %fusion.7.forward_ref, f32[16,1024]{1,0:T(8,128)S(1)} %fusion.partner_ref, f32[8,1024]{1,0:T(8,128)S(1)} %shard_map.66.factors_ref), custom_call_target="tpu_custom_call" | custom-call | flops 737280000 | bytes 196608 | tf_op jit(solution)/shard_map/pallas_call | solution.py:122
  21.8 1.0 %collective-permute-start.5 = (bf16[16,1024]{1,0:T(8,128)(2,1)S(1)}, bf16[16,1024]{1,0:T(8,128)(2,1)S(1)}, u32[]{:S(2)}, u32[]{:S(2)}) collective-permute-start(bf16[16,1024]{1,0:T(8,128)(2,1)S(1)} %shard_map.69), channel_id=1, source_target_pairs={{0,1},{1,0},{4,5},{5,4},{8,13},{9,12},{12,9},{13,8},{2,3},{3,2},{6... | collective-permute-start | bytes 98312 | tf_op jit(solution)/shard_map/ppermute | solution.py:259
  22.8 0.1 collective-permute-start.6
  22.9 1.1 %collective-permute-start.7 = (bf16[16,1024]{1,0:T(8,128)(2,1)S(1)}, bf16[16,1024]{1,0:T(8,128)(2,1)S(1)}, u32[]{:S(2)}, u32[]{:S(2)}) collective-permute-start(bf16[16,1024]{1,0:T(8,128)(2,1)S(1)} %get-tuple-element.32), channel_id=1, source_target_pairs={{0,13},{1,12},{4,0},{5,1},{8,4},{9,5},{12,8},{13,9},{2,15},{3,14},... | collective-permute-start | bytes 98312 | tf_op jit(solution)/shard_map/ppermute | solution.py:259
  24.0 0.0 collective-permute-done.3
  24.0 0.0 collective-permute-done.4
  24.0 0.0 collective-permute-done.5
  24.0 0.0 collective-permute-done.6
  24.1 2.7 %collective-permute-done.7.arrived_ref = bf16[16,1024]{1,0:T(8,128)(2,1)S(1)} collective-permute-done((bf16[16,1024]{1,0:T(8,128)(2,1)S(1)}, bf16[16,1024]{1,0:T(8,128)(2,1)S(1)}, u32[]{:S(2)}, u32[]{:S(2)}) %collective-permute-start.7) | collective-permute-done | bytes 32800 | tf_op jit(solution)/shard_map/ppermute | solution.py:259
  26.8 0.6 %shard_map.71 = f32[16,1024]{1,0:T(8,128)} custom-call(f32[16,1024]{1,0:T(8,128)S(1)} %convert_add_fusion.known_ref, bf16[16,1024]{1,0:T(8,128)(2,1)S(1)} %collective-permute-done.7.arrived_ref), custom_call_target="tpu_custom_call" | custom-call | flops 49152 | bytes 163840 | tf_op jit(solution)/shard_map/pallas_call | solution.py:202
  (7 shorter events, 0.1 us)
Async XLA Ops:
  0.0 8.0 %copy-start = (bf16[1,1024,1024]{2,1,0:T(8,128)(2,1)S(1)}, bf16[1,1024,1024]{2,1,0:T(8,128)(2,1)}, u32[]{:S(2)}) copy-start(bf16[1,1024,1024]{2,1,0:T(8,128)(2,1)} %param.7) | copy-start | bytes 6291460
  1.1 6.5 %collective-permute-start = (bf16[32,1024]{1,0:T(8,128)(2,1)S(1)}, bf16[32,1024]{1,0:T(8,128)(2,1)S(1)}, u32[]{:S(2)}, u32[]{:S(2)}) collective-permute-start(bf16[32,1024]{1,0:T(8,128)(2,1)S(1)} %pad_maximum_fusion.1), channel_id=1, source_target_pairs={{0,4},{1,5},{4,8},{5,9},{8,12},{9,13},{12,1},{13,0},{2,6},{3,7},{6... | collective-permute-start | bytes 196616 | tf_op jit(solution)/shard_map/ppermute | solution.py:242
  6.1 3.2 %copy-start.1 = (s32[1,2,1024]{2,1,0:T(2,128)S(1)}, s32[1,2,1024]{2,1,0:T(2,128)}, u32[]{:S(2)}) copy-start(s32[1,2,1024]{2,1,0:T(2,128)} %param.10) | copy-start | bytes 24580
  6.1 3.2 %copy-start.2 = (s32[2,1024]{1,0:T(2,128)S(1)}, s32[2,1024]{1,0:T(2,128)}, u32[]{:S(2)}) copy-start(s32[2,1024]{1,0:T(2,128)} %bonds_ref) | copy-start | bytes 24580
  8.4 5.5 %collective-permute-start.1 = (bf16[32,1024]{1,0:T(8,128)(2,1)S(1)}, bf16[32,1024]{1,0:T(8,128)(2,1)S(1)}, u32[]{:S(2)}, u32[]{:S(2)}) collective-permute-start(bf16[32,1024]{1,0:T(8,128)(2,1)S(1)} %pad_maximum_fusion.2), channel_id=1, source_target_pairs={{0,4},{1,5},{4,8},{5,9},{8,12},{9,13},{12,1},{13,0},{2,6},{3,7},{6... | collective-permute-start | bytes 196616 | tf_op jit(solution)/shard_map/ppermute | solution.py:242
  14.7 5.6 %collective-permute-start.2 = (bf16[32,1024]{1,0:T(8,128)(2,1)S(1)}, bf16[32,1024]{1,0:T(8,128)(2,1)S(1)}, u32[]{:S(2)}, u32[]{:S(2)}) collective-permute-start(bf16[32,1024]{1,0:T(8,128)(2,1)S(1)} %pad_maximum_fusion.3), channel_id=1, source_target_pairs={{0,4},{1,5},{4,8},{5,9},{8,12},{9,13},{12,1},{13,0},{2,6},{3,7},{6... | collective-permute-start | bytes 196616 | tf_op jit(solution)/shard_map/ppermute | solution.py:242
  15.5 8.5 %collective-permute-start.3 = (bf16[16,1024]{1,0:T(8,128)(2,1)S(1)}, bf16[16,1024]{1,0:T(8,128)(2,1)S(1)}, u32[]{:S(2)}, u32[]{:S(2)}) collective-permute-start(bf16[16,1024]{1,0:T(8,128)(2,1)S(1)} %get-tuple-element.35), channel_id=1, source_target_pairs={{0,9},{1,8},{4,13},{5,12},{8,0},{9,1},{12,4},{13,5},{2,11},{3,10},... | collective-permute-start | bytes 98312 | tf_op jit(solution)/shard_map/ppermute | solution.py:259
  15.6 8.4 %collective-permute-start.4 = (bf16[16,1024]{1,0:T(8,128)(2,1)S(1)}, bf16[16,1024]{1,0:T(8,128)(2,1)S(1)}, u32[]{:S(2)}, u32[]{:S(2)}) collective-permute-start(bf16[16,1024]{1,0:T(8,128)(2,1)S(1)} %get-tuple-element.36), channel_id=1, source_target_pairs={{0,5},{1,4},{4,9},{5,8},{8,13},{9,12},{12,0},{13,1},{2,7},{3,6},{6... | collective-permute-start | bytes 98312 | tf_op jit(solution)/shard_map/ppermute | solution.py:259
  21.8 2.2 %collective-permute-start.5 = (bf16[16,1024]{1,0:T(8,128)(2,1)S(1)}, bf16[16,1024]{1,0:T(8,128)(2,1)S(1)}, u32[]{:S(2)}, u32[]{:S(2)}) collective-permute-start(bf16[16,1024]{1,0:T(8,128)(2,1)S(1)} %shard_map.69), channel_id=1, source_target_pairs={{0,1},{1,0},{4,5},{5,4},{8,13},{9,12},{12,9},{13,8},{2,3},{3,2},{6... | collective-permute-start | bytes 98312 | tf_op jit(solution)/shard_map/ppermute | solution.py:259
  22.8 1.2 %collective-permute-start.6 = (bf16[16,1024]{1,0:T(8,128)(2,1)S(1)}, bf16[16,1024]{1,0:T(8,128)(2,1)S(1)}, u32[]{:S(2)}, u32[]{:S(2)}) collective-permute-start(bf16[16,1024]{1,0:T(8,128)(2,1)S(1)} %get-tuple-element.31), channel_id=1, source_target_pairs={{0,1},{1,0},{4,13},{5,12},{8,9},{9,8},{12,5},{13,4},{2,3},{3,2},{6... | collective-permute-start | bytes 98312 | tf_op jit(solution)/shard_map/ppermute | solution.py:259
  22.9 3.9 %collective-permute-start.7 = (bf16[16,1024]{1,0:T(8,128)(2,1)S(1)}, bf16[16,1024]{1,0:T(8,128)(2,1)S(1)}, u32[]{:S(2)}, u32[]{:S(2)}) collective-permute-start(bf16[16,1024]{1,0:T(8,128)(2,1)S(1)} %get-tuple-element.32), channel_id=1, source_target_pairs={{0,13},{1,12},{4,0},{5,1},{8,4},{9,5},{12,8},{13,9},{2,15},{3,14},... | collective-permute-start | bytes 98312 | tf_op jit(solution)/shard_map/ppermute | solution.py:259

commit v10 on v8

--- a/solution.py
+++ b/solution.py
@@ -242,7 +242,7 @@
     def shifted(step):
         return {k: ((k + step) % clusters, -(k < (k + step) % clusters)) for k in range(clusters)}
 
-    arrived = [sent(early_term((anchor + step) % clusters), shifted(step)) for step in range(clusters - 2, 0, -1)]
+    arrived = [sent(early_term((anchor + step) % clusters), shifted(step)) for step in range(1, last)]
     soon = sum(term.astype(jnp.float32) for term in arrived)
 
     total = jnp.where(anchor == last, late, early_term(anchor)).astype(jnp.float32)

time: 27.6 us -> 27.8 us (level)
  starting transfers between devices: 10 us -> 10.3 us
    ppermute x5, starting transfers between devices: 5.98 us -> 6.29 us  [sent(): return lax.ppermute(term, ('tm', 'col'), route(targets))]
where the time goes in v10:
time: 27.8 us; the launch traced here: 27.6 us
  starting transfers between devices  10.3 us (37%)
  waiting for transfers between devices  8.25 us (30%)
  Pallas kernels  5.8 us (21%)
  matrix products  2.32 us (8%)
  other arithmetic  0.72 us (3%)
    ppermute x5, starting transfers between devices, sent(): return lax.ppermute(term, ('tm', 'col'), route(targets))  6.29 us
    ppermute x3, waiting for transfers between devices, per_device(): low = lax.ppermute(low, ('tm', 'col'), around)  4.93 us
    ppermute x3, starting transfers between devices, per_device(): low = lax.ppermute(low, ('tm', 'col'), around)  4.06 us
    ppermute x5, waiting for transfers between devices, sent(): return lax.ppermute(term, ('tm', 'col'), route(targets))  3.32 us
    pallas_call x4, Pallas kernels, measured(): pl.pallas_call(functools.partial(measure_kernel, math.isqrt(forward.shape...  2.77 us
    pallas_call x1, Pallas kernels, turned(): pl.pallas_call(turned_kernel, out_shape=jax.ShapeDtypeStruct(dense.shape[...  1.89 us
    dot_general x3, matrix products, per_device(): jnp.dot(low[ref_rows:], inverse_map, preferred_element_type=jnp.float32)  1.17 us
    dot_general x3, matrix products, per_device(): jnp.dot(low[:ref_rows], forward_map, preferred_element_type=jnp.float32)  1.16 us
  transfers between devices with their start and end apart: 8, of which 6 were waited for; matrix products, arithmetic and copies ran while one was open for 3% of the time, Pallas kernels for 17%

profile of v10, /device:TPU:0, one launch (start us, length us, event | category | flops | bytes accessed | tf_op | source)
XLA Modules:
  0.0 27.6 jit_solution(12248000630381590405)
XLA Ops:
  0.0 0.0 copy-start
  0.0 1.1 %shard_map.64 = (bf16[16,1024]{1,0:T(8,128)(2,1)S(1)}, bf16[16,1024]{1,0:T(8,128)(2,1)S(1)}, f32[16,1024]{1,0:T(8,128)S(1)}, f32[16,1024]{1,0:T(8,128)S(1)}) custom-call(s32[1]{0:T(128)} %bitcast.1.base_ref, f32[16,1024]{1,0:T(8,128)} %bitcast.43, f32[16,1024]{1,0:T(8,128)} %bitcast.44), custom_call_target="tpu_custom_call" | custom-call | flops 65536 | bytes 196608 | tf_op jit(solution)/shard_map/pallas_call | solution.py:152
  1.1 3.1 %collective-permute-start = (bf16[32,1024]{1,0:T(8,128)(2,1)S(1)}, bf16[32,1024]{1,0:T(8,128)(2,1)S(1)}, u32[]{:S(2)}, u32[]{:S(2)}) collective-permute-start(bf16[32,1024]{1,0:T(8,128)(2,1)S(1)} %pad_maximum_fusion.1), channel_id=1, source_target_pairs={{0,4},{1,5},{4,8},{5,9},{8,12},{9,13},{12,1},{13,0},{2,6},{3,7},{6... | collective-permute-start | bytes 196616 | tf_op jit(solution)/shard_map/ppermute | solution.py:223
  4.2 1.9 %shard_map.65 = bf16[1024,1024]{1,0:T(8,128)(2,1)S(1)} custom-call(bf16[1024,1024]{1,0:T(8,128)(2,1)} %bitcast.42), custom_call_target="tpu_custom_call" | custom-call | flops 1048576 | bytes 4194304 | tf_op jit(solution)/shard_map/pallas_call | solution.py:183
  6.1 0.0 copy-start.1
  6.1 0.0 copy-start.2
  6.1 1.5 %collective-permute-done = bf16[32,1024]{1,0:T(8,128)(2,1)S(1)} collective-permute-done((bf16[32,1024]{1,0:T(8,128)(2,1)S(1)}, bf16[32,1024]{1,0:T(8,128)(2,1)S(1)}, u32[]{:S(2)}, u32[]{:S(2)}) %collective-permute-start) | collective-permute-done | bytes 65568 | tf_op jit(solution)/shard_map/ppermute | solution.py:223
  7.6 0.4 %fusion.16 = (bf16[16,1024]{1,0:T(8,128)(2,1)S(1)}, f32[16,1024]{1,0:T(8,128)S(1)}) fusion(bf16[1024,1024]{1,0:T(8,128)(2,1)S(1)} %shard_map.65, bf16[32,1024]{1,0:T(8,128)(2,1)S(1)} %collective-permute-done), kind=kOutput, calls=%fused_computation.26 | convolution fusion | flops 33570816 | bytes 2228224 | tf_op jit(solution)/shard_map/dot_general | solution.py:224
  8.0 0.0 copy-done
  8.0 0.4 %fusion.15 = (bf16[16,1024]{1,0:T(8,128)(2,1)S(1)}, f32[16,1024]{1,0:T(8,128)S(1)}) fusion(bf16[1,1024,1024]{2,1,0:T(8,128)(2,1)S(1)} %copy-done, bf16[32,1024]{1,0:T(8,128)(2,1)S(1)} %collective-permute-done), kind=kOutput, calls=%fused_computation.25 | convolution fusion | flops 33570816 | bytes 2228224 | tf_op jit(solution)/shard_map/dot_general | solution.py:225
  8.4 0.9 %collective-permute-start.1 = (bf16[32,1024]{1,0:T(8,128)(2,1)S(1)}, bf16[32,1024]{1,0:T(8,128)(2,1)S(1)}, u32[]{:S(2)}, u32[]{:S(2)}) collective-permute-start(bf16[32,1024]{1,0:T(8,128)(2,1)S(1)} %pad_maximum_fusion.2), channel_id=1, source_target_pairs={{0,4},{1,5},{4,8},{5,9},{8,12},{9,13},{12,1},{13,0},{2,6},{3,7},{6... | collective-permute-start | bytes 196616 | tf_op jit(solution)/shard_map/ppermute | solution.py:223
  9.3 0.0 copy-done.1
  9.3 0.0 copy-done.2
  9.3 0.1 shard_map.66.factors_ref
  9.4 0.7 %shard_map.67 = bf16[16,1024]{1,0:T(8,128)(2,1)S(1)} custom-call(s32[1]{0:T(128)} %bitcast.1.base_ref, f32[16,1024]{1,0:T(8,128)S(1)} %get-tuple-element.23.forward_ref, f32[16,1024]{1,0:T(8,128)S(1)} %get-tuple-element.24.partner_ref, f32[8,1024]{1,0:T(8,128)S(1)} %shard_map.66.factors_ref), custom_call_target="tpu_custom_call" | custom-call | flops 737280000 | bytes 196608 | tf_op jit(solution)/shard_map/pallas_call | solution.py:122
  10.1 0.7 %shard_map.68 = bf16[16,1024]{1,0:T(8,128)(2,1)S(1)} custom-call(s32[1]{0:T(128)} %bitcast.7.base_ref, f32[16,1024]{1,0:T(8,128)S(1)} %get-tuple-element.40.forward_ref, f32[16,1024]{1,0:T(8,128)S(1)} %get-tuple-element.38.partner_ref, f32[8,1024]{1,0:T(8,128)S(1)} %shard_map.66.factors_ref), custom_call_target="tpu_custom_call" | custom-call | flops 737280000 | bytes 196608 | tf_op jit(solution)/shard_map/pallas_call | solution.py:122
  10.8 3.1 %collective-permute-done.1 = bf16[32,1024]{1,0:T(8,128)(2,1)S(1)} collective-permute-done((bf16[32,1024]{1,0:T(8,128)(2,1)S(1)}, bf16[32,1024]{1,0:T(8,128)(2,1)S(1)}, u32[]{:S(2)}, u32[]{:S(2)}) %collective-permute-start.1) | collective-permute-done | bytes 65568 | tf_op jit(solution)/shard_map/ppermute | solution.py:223
  13.9 0.4 %fusion.17 = (bf16[16,1024]{1,0:T(8,128)(2,1)S(1)}, f32[16,1024]{1,0:T(8,128)S(1)}) fusion(bf16[1,1024,1024]{2,1,0:T(8,128)(2,1)S(1)} %copy-done, bf16[32,1024]{1,0:T(8,128)(2,1)S(1)} %collective-permute-done.1), kind=kOutput, calls=%fused_computation.27 | convolution fusion | flops 33570816 | bytes 2228224 | tf_op jit(solution)/shard_map/dot_general | solution.py:225
  14.3 0.4 %fusion.18 = (bf16[16,1024]{1,0:T(8,128)(2,1)S(1)}, f32[16,1024]{1,0:T(8,128)S(1)}) fusion(bf16[1024,1024]{1,0:T(8,128)(2,1)S(1)} %shard_map.65, bf16[32,1024]{1,0:T(8,128)(2,1)S(1)} %collective-permute-done.1), kind=kOutput, calls=%fused_computation.28 | convolution fusion | flops 33570816 | bytes 2228224 | tf_op jit(solution)/shard_map/dot_general | solution.py:224
  14.7 0.1 collective-permute-start.2
  14.8 0.7 %shard_map.70 = bf16[16,1024]{1,0:T(8,128)(2,1)S(1)} custom-call(s32[1]{0:T(128)} %bitcast.10.base_ref, f32[16,1024]{1,0:T(8,128)S(1)} %get-tuple-element.44.forward_ref, f32[16,1024]{1,0:T(8,128)S(1)} %get-tuple-element.42.partner_ref, f32[8,1024]{1,0:T(8,128)S(1)} %shard_map.66.factors_ref), custom_call_target="tpu_custom_call" | custom-call | flops 737280000 | bytes 196608 | tf_op jit(solution)/shard_map/pallas_call | solution.py:122
  15.5 0.1 collective-permute-start.3
  15.6 4.4 %collective-permute-start.4 = (bf16[16,1024]{1,0:T(8,128)(2,1)S(1)}, bf16[16,1024]{1,0:T(8,128)(2,1)S(1)}, u32[]{:S(2)}, u32[]{:S(2)}) collective-permute-start(bf16[16,1024]{1,0:T(8,128)(2,1)S(1)} %get-tuple-element.36), channel_id=1, source_target_pairs={{0,9},{1,8},{4,13},{5,12},{8,0},{9,1},{12,4},{13,5},{2,11},{3,10},... | collective-permute-start | bytes 98312 | tf_op jit(solution)/shard_map/ppermute | solution.py:240
  20.0 0.3 %collective-permute-done.2 = bf16[32,1024]{1,0:T(8,128)(2,1)S(1)} collective-permute-done((bf16[32,1024]{1,0:T(8,128)(2,1)S(1)}, bf16[32,1024]{1,0:T(8,128)(2,1)S(1)}, u32[]{:S(2)}, u32[]{:S(2)}) %collective-permute-start.2) | collective-permute-done | bytes 65568 | tf_op jit(solution)/shard_map/ppermute | solution.py:223
  20.3 0.4 %fusion.7.forward_ref = f32[16,1024]{1,0:T(8,128)S(1)} fusion(bf16[1024,1024]{1,0:T(8,128)(2,1)S(1)} %shard_map.65, bf16[32,1024]{1,0:T(8,128)(2,1)S(1)} %collective-permute-done.2), kind=kOutput, calls=%fused_computation.12 | convolution fusion | flops 33554432 | bytes 2195456 | tf_op jit(solution)/shard_map/dot_general | solution.py:224
  20.6 0.4 %fusion.partner_ref = f32[16,1024]{1,0:T(8,128)S(1)} fusion(bf16[1,1024,1024]{2,1,0:T(8,128)(2,1)S(1)} %copy-done, bf16[32,1024]{1,0:T(8,128)(2,1)S(1)} %collective-permute-done.2), kind=kOutput, calls=%fused_computation | convolution fusion | flops 33554432 | bytes 2195456 | tf_op jit(solution)/shard_map/dot_general | solution.py:225
  21.0 0.7 %shard_map.69 = bf16[16,1024]{1,0:T(8,128)(2,1)S(1)} custom-call(s32[1]{0:T(128)} %bitcast.base_ref, f32[16,1024]{1,0:T(8,128)S(1)} %fusion.7.forward_ref, f32[16,1024]{1,0:T(8,128)S(1)} %fusion.partner_ref, f32[8,1024]{1,0:T(8,128)S(1)} %shard_map.66.factors_ref), custom_call_target="tpu_custom_call" | custom-call | flops 737280000 | bytes 196608 | tf_op jit(solution)/shard_map/pallas_call | solution.py:122
  21.8 1.2 %collective-permute-start.5 = (bf16[16,1024]{1,0:T(8,128)(2,1)S(1)}, bf16[16,1024]{1,0:T(8,128)(2,1)S(1)}, u32[]{:S(2)}, u32[]{:S(2)}) collective-permute-start(bf16[16,1024]{1,0:T(8,128)(2,1)S(1)} %get-tuple-element.30), channel_id=1, source_target_pairs={{0,1},{1,0},{4,13},{5,12},{8,9},{9,8},{12,5},{13,4},{2,3},{3,2},{6... | collective-permute-start | bytes 98312 | tf_op jit(solution)/shard_map/ppermute | solution.py:240
  23.0 0.1 collective-permute-start.6
  23.0 0.6 %collective-permute-start.7 = (bf16[16,1024]{1,0:T(8,128)(2,1)S(1)}, bf16[16,1024]{1,0:T(8,128)(2,1)S(1)}, u32[]{:S(2)}, u32[]{:S(2)}) collective-permute-start(bf16[16,1024]{1,0:T(8,128)(2,1)S(1)} %get-tuple-element.32), channel_id=1, source_target_pairs={{0,13},{1,12},{4,0},{5,1},{8,4},{9,5},{12,8},{13,9},{2,15},{3,14},... | collective-permute-start | bytes 98312 | tf_op jit(solution)/shard_map/ppermute | solution.py:240
  23.6 0.0 collective-permute-done.3
  23.6 0.0 collective-permute-done.4
  23.6 0.2 collective-permute-done.5
  23.8 0.3 %collective-permute-done.6 = bf16[16,1024]{1,0:T(8,128)(2,1)S(1)} collective-permute-done((bf16[16,1024]{1,0:T(8,128)(2,1)S(1)}, bf16[16,1024]{1,0:T(8,128)(2,1)S(1)}, u32[]{:S(2)}, u32[]{:S(2)}) %collective-permute-start.6) | collective-permute-done | bytes 32800 | tf_op jit(solution)/shard_map/ppermute | solution.py:240
  24.2 2.8 %collective-permute-done.7 = bf16[16,1024]{1,0:T(8,128)(2,1)S(1)} collective-permute-done((bf16[16,1024]{1,0:T(8,128)(2,1)S(1)}, bf16[16,1024]{1,0:T(8,128)(2,1)S(1)}, u32[]{:S(2)}, u32[]{:S(2)}) %collective-permute-start.7) | collective-permute-done | bytes 32800 | tf_op jit(solution)/shard_map/ppermute | solution.py:240
  27.0 0.7 %multiply_bitcast_fusion = f32[1,16,1024]{2,1,0:T(8,128)} fusion(bf16[16,1024]{1,0:T(8,128)(2,1)S(1)} %collective-permute-done.7, bf16[16,1024]{1,0:T(8,128)(2,1)S(1)} %collective-permute-done.4, bf16[16,1024]{1,0:T(8,128)(2,1)S(1)} %collective-permute-done.3, bf16[16,1024]{1,0:T(8,128)(2,1)S(1)} %shard_map.69, ...), kind=kLoop, calls=%fused_computation.10 | loop fusion | flops 262144 | bytes 294917 | tf_op jit(solution)/shard_map/broadcast_in_dim | solution.py:263
  (6 shorter events, 0.1 us)
Async XLA Ops:
  0.0 8.0 %copy-start = (bf16[1,1024,1024]{2,1,0:T(8,128)(2,1)S(1)}, bf16[1,1024,1024]{2,1,0:T(8,128)(2,1)}, u32[]{:S(2)}) copy-start(bf16[1,1024,1024]{2,1,0:T(8,128)(2,1)} %param.7) | copy-start | bytes 6291460
  1.1 6.5 %collective-permute-start = (bf16[32,1024]{1,0:T(8,128)(2,1)S(1)}, bf16[32,1024]{1,0:T(8,128)(2,1)S(1)}, u32[]{:S(2)}, u32[]{:S(2)}) collective-permute-start(bf16[32,1024]{1,0:T(8,128)(2,1)S(1)} %pad_maximum_fusion.1), channel_id=1, source_target_pairs={{0,4},{1,5},{4,8},{5,9},{8,12},{9,13},{12,1},{13,0},{2,6},{3,7},{6... | collective-permute-start | bytes 196616 | tf_op jit(solution)/shard_map/ppermute | solution.py:223
  6.1 3.2 %copy-start.1 = (s32[1,2,1024]{2,1,0:T(2,128)S(1)}, s32[1,2,1024]{2,1,0:T(2,128)}, u32[]{:S(2)}) copy-start(s32[1,2,1024]{2,1,0:T(2,128)} %param.10) | copy-start | bytes 24580
  6.1 3.2 %copy-start.2 = (s32[2,1024]{1,0:T(2,128)S(1)}, s32[2,1024]{1,0:T(2,128)}, u32[]{:S(2)}) copy-start(s32[2,1024]{1,0:T(2,128)} %bonds_ref) | copy-start | bytes 24580
  8.4 5.5 %collective-permute-start.1 = (bf16[32,1024]{1,0:T(8,128)(2,1)S(1)}, bf16[32,1024]{1,0:T(8,128)(2,1)S(1)}, u32[]{:S(2)}, u32[]{:S(2)}) collective-permute-start(bf16[32,1024]{1,0:T(8,128)(2,1)S(1)} %pad_maximum_fusion.2), channel_id=1, source_target_pairs={{0,4},{1,5},{4,8},{5,9},{8,12},{9,13},{12,1},{13,0},{2,6},{3,7},{6... | collective-permute-start | bytes 196616 | tf_op jit(solution)/shard_map/ppermute | solution.py:223
  14.7 5.5 %collective-permute-start.2 = (bf16[32,1024]{1,0:T(8,128)(2,1)S(1)}, bf16[32,1024]{1,0:T(8,128)(2,1)S(1)}, u32[]{:S(2)}, u32[]{:S(2)}) collective-permute-start(bf16[32,1024]{1,0:T(8,128)(2,1)S(1)} %pad_maximum_fusion.3), channel_id=1, source_target_pairs={{0,4},{1,5},{4,8},{5,9},{8,12},{9,13},{12,1},{13,0},{2,6},{3,7},{6... | collective-permute-start | bytes 196616 | tf_op jit(solution)/shard_map/ppermute | solution.py:223
  15.5 8.1 %collective-permute-start.3 = (bf16[16,1024]{1,0:T(8,128)(2,1)S(1)}, bf16[16,1024]{1,0:T(8,128)(2,1)S(1)}, u32[]{:S(2)}, u32[]{:S(2)}) collective-permute-start(bf16[16,1024]{1,0:T(8,128)(2,1)S(1)} %get-tuple-element.35), channel_id=1, source_target_pairs={{0,5},{1,4},{4,9},{5,8},{8,13},{9,12},{12,0},{13,1},{2,7},{3,6},{6... | collective-permute-start | bytes 98312 | tf_op jit(solution)/shard_map/ppermute | solution.py:240
  15.6 8.0 %collective-permute-start.4 = (bf16[16,1024]{1,0:T(8,128)(2,1)S(1)}, bf16[16,1024]{1,0:T(8,128)(2,1)S(1)}, u32[]{:S(2)}, u32[]{:S(2)}) collective-permute-start(bf16[16,1024]{1,0:T(8,128)(2,1)S(1)} %get-tuple-element.36), channel_id=1, source_target_pairs={{0,9},{1,8},{4,13},{5,12},{8,0},{9,1},{12,4},{13,5},{2,11},{3,10},... | collective-permute-start | bytes 98312 | tf_op jit(solution)/shard_map/ppermute | solution.py:240
  21.8 2.1 %collective-permute-start.5 = (bf16[16,1024]{1,0:T(8,128)(2,1)S(1)}, bf16[16,1024]{1,0:T(8,128)(2,1)S(1)}, u32[]{:S(2)}, u32[]{:S(2)}) collective-permute-start(bf16[16,1024]{1,0:T(8,128)(2,1)S(1)} %get-tuple-element.30), channel_id=1, source_target_pairs={{0,1},{1,0},{4,13},{5,12},{8,9},{9,8},{12,5},{13,4},{2,3},{3,2},{6... | collective-permute-start | bytes 98312 | tf_op jit(solution)/shard_map/ppermute | solution.py:240
  23.0 1.2 %collective-permute-start.6 = (bf16[16,1024]{1,0:T(8,128)(2,1)S(1)}, bf16[16,1024]{1,0:T(8,128)(2,1)S(1)}, u32[]{:S(2)}, u32[]{:S(2)}) collective-permute-start(bf16[16,1024]{1,0:T(8,128)(2,1)S(1)} %shard_map.69), channel_id=1, source_target_pairs={{0,1},{1,0},{4,5},{5,4},{8,13},{9,12},{12,9},{13,8},{2,3},{3,2},{6... | collective-permute-start | bytes 98312 | tf_op jit(solution)/shard_map/ppermute | solution.py:240
  23.0 3.9 %collective-permute-start.7 = (bf16[16,1024]{1,0:T(8,128)(2,1)S(1)}, bf16[16,1024]{1,0:T(8,128)(2,1)S(1)}, u32[]{:S(2)}, u32[]{:S(2)}) collective-permute-start(bf16[16,1024]{1,0:T(8,128)(2,1)S(1)} %get-tuple-element.32), channel_id=1, source_target_pairs={{0,13},{1,12},{4,0},{5,1},{8,4},{9,5},{12,8},{13,9},{2,15},{3,14},... | collective-permute-start | bytes 98312 | tf_op jit(solution)/shard_map/ppermute | solution.py:240
